TPU v7x, 32 devices: a whole 2x2x4 slice. The times are simulated.
32 devices in a mesh: recv: 8 (over z, x), tm: 4 (over y, core).
Axes of the slice: x: 2, y: 2, z: 4, core: 2. Of those that a mesh axis runs over, the one named last changes fastest.
Arguments:
- record: float32 [128, 4096], P('recv', 'tm')
- source_channels: int32 [16], replicated, may hold values from 0 to 127, as said below
- valid_mask: int32 [128, 4], P('recv', 'tm'), may hold values 0 or 1
Outputs:
- lag_stack: float32 [16, 128, 256], P('tm', 'recv')
Inputs may be any that keep to these rules, and one draw needn't show every extreme that they name: `source_channels`: ascending and distinct; source s lies in channels s * 8 to (s + 1) * 8 - 1; the first is channel 0 and the last channel 128 - 1.
All inputs are finite; a program needn't handle non-finite values. No bound on the sum of `valid_mask` on one device may be relied on, other than what follows from the above.
Results may differ from a plain program's by a relative error of at most 0.0001.
Values sent between devices are 32-bit elements; how exact they have to be, the bound alone decides.
No kernel may reach another device: no remote copies, remote signals or barrier semaphores. Data moves between devices by JAX's collectives and lax.ppermute only.
A program may use at most 64 MiB of HBM per device.

v0:
```python
import jax
import jax.numpy as jnp
from jax import lax
from jax.sharding import PartitionSpec as P

SEGLEN = 2048
NF = 1024
LAGS = 256
SMOOTH = 64
NSRC = 16


def shifted(block, axis, distance):
    devices = range(lax.axis_size(axis))
    route = [(i - distance, i) for i in devices if i - distance in devices]
    return lax.ppermute(block, axis, route)


def angle_table(rows, cols, period):
    first = lax.broadcasted_iota(jnp.int32, (rows, cols), 0)
    second = lax.broadcasted_iota(jnp.int32, (rows, cols), 1)
    return (first * second % period).astype(jnp.float32) * (2.0 * jnp.pi / period)


def fourier(tapered):
    row_count = tapered.shape[0]
    low_len = 16
    high_len = SEGLEN // 16
    keep_len = NF // 16
    blocks = tapered.reshape(row_count, low_len, high_len)
    first_angle = angle_table(low_len, low_len, low_len)
    first_re = jnp.einsum(
        "rmn,mf->rfn", blocks, jnp.cos(first_angle), precision=lax.Precision.HIGHEST
    )
    first_im = jnp.einsum(
        "rmn,mf->rfn", blocks, -jnp.sin(first_angle), precision=lax.Precision.HIGHEST
    )
    twist_angle = angle_table(low_len, high_len, SEGLEN)
    twist_re = jnp.cos(twist_angle)
    twist_im = -jnp.sin(twist_angle)
    mid_re = first_re * twist_re - first_im * twist_im
    mid_im = first_re * twist_im + first_im * twist_re
    last_angle = angle_table(high_len, keep_len, high_len)
    last_re = jnp.cos(last_angle)
    last_im = -jnp.sin(last_angle)
    out_re = jnp.einsum(
        "rfn,ng->rgf", mid_re, last_re, precision=lax.Precision.HIGHEST
    ) - jnp.einsum("rfn,ng->rgf", mid_im, last_im, precision=lax.Precision.HIGHEST)
    out_im = jnp.einsum(
        "rfn,ng->rgf", mid_re, last_im, precision=lax.Precision.HIGHEST
    ) + jnp.einsum("rfn,ng->rgf", mid_im, last_re, precision=lax.Precision.HIGHEST)
    return (out_re.reshape(row_count, NF), out_im.reshape(row_count, NF))


def inverse_table():
    freq_idx = lax.broadcasted_iota(jnp.int32, (NF, LAGS), 0)
    lag_idx = (lax.broadcasted_iota(jnp.int32, (NF, LAGS), 1) - LAGS // 2) % SEGLEN
    angle = (freq_idx * lag_idx % SEGLEN).astype(jnp.float32) * (2.0 * jnp.pi / SEGLEN)
    factor = jnp.where(freq_idx == 0, 1.0, 2.0) / SEGLEN
    return jnp.concatenate([factor * jnp.cos(angle), -factor * jnp.sin(angle)], axis=0)


def whiten(segments):
    sample_idx = lax.broadcasted_iota(jnp.int32, (1, SEGLEN), 1).astype(jnp.float32)
    taper_weights = 0.5 - 0.5 * jnp.cos(2.0 * jnp.pi * sample_idx / SEGLEN)
    tapered = (segments - jnp.mean(segments, axis=1, keepdims=True)) * taper_weights
    spec_re, spec_im = fourier(tapered)
    power_spec = spec_re * spec_re + spec_im * spec_im
    zero_init = jnp.zeros((), jnp.float32)
    counts = lax.reduce_window(
        jnp.ones((1, NF), jnp.float32),
        zero_init,
        lax.add,
        (1, 2 * SMOOTH + 1),
        (1, 1),
        [(0, 0), (SMOOTH, SMOOTH)],
    )
    smoothed = (
        lax.reduce_window(
            power_spec, zero_init, lax.add, (1, 2 * SMOOTH + 1), (1, 1), [(0, 0), (SMOOTH, SMOOTH)]
        )
        / counts
    )
    inv_scale = 1.0 / jnp.sqrt(smoothed + 1e-06)
    return jnp.concatenate([spec_re * inv_scale, spec_im * inv_scale], axis=1)


def cut_segments(extended):
    return jnp.stack([extended], axis=0)


def correlate(src_spec, recv_spec, src_valid, recv_valid, inv_tab):
    src_re = src_spec[:, None, :NF]
    src_im = src_spec[:, None, NF:]
    rec_re = recv_spec[None, :, :NF]
    rec_im = recv_spec[None, :, NF:]
    cross_re = src_re * rec_re + src_im * rec_im
    cross_im = src_re * rec_im - src_im * rec_re
    src_count = src_spec.shape[0]
    row_count = recv_spec.shape[0]
    cross = jnp.concatenate([cross_re, cross_im], axis=2).reshape(src_count * row_count, 2 * NF)
    lag_corr = jnp.dot(
        cross, inv_tab, precision=lax.Precision.HIGHEST, preferred_element_type=jnp.float32
    )
    lag_corr = lag_corr.reshape(src_count, row_count, LAGS)
    normed = lag_corr / jnp.sqrt(jnp.mean(lag_corr * lag_corr, axis=2, keepdims=True) + 1e-06)
    return normed * (src_valid[:, None] * recv_valid[None, :])[:, :, None]


def local(record, source_channels, valid_mask):
    row_count = record.shape[0]
    seg_count = valid_mask.shape[1]
    inv_tab = inverse_table()
    following = shifted(record, "tm", -1)
    extended = jnp.concatenate([record, following], axis=1)
    local_segments = cut_segments(extended).reshape(seg_count * row_count, SEGLEN)
    local_spec = whiten(local_segments).reshape(seg_count, row_count, 2 * NF)
    recv_mask = valid_mask.astype(jnp.float32).T
    first_row = lax.axis_index("recv") * row_count
    row_ids = lax.broadcasted_iota(jnp.int32, (NSRC, row_count), 1) + first_row
    onehot = (source_channels[:, None] == row_ids).astype(jnp.float32)
    picked_mask = jnp.dot(
        recv_mask, onehot.T, precision=lax.Precision.HIGHEST, preferred_element_type=jnp.float32
    )
    picked = jnp.einsum("sr,krc->ksc", onehot, local_spec, precision=lax.Precision.HIGHEST)
    src_spec, src_mask = lax.psum((picked, picked_mask), "recv")
    partial_stack = correlate(src_spec[0], local_spec[0], src_mask[0], recv_mask[0], inv_tab)
    lag_stack = lax.psum_scatter(partial_stack, "tm", scatter_dimension=0, tiled=True)
    return lag_stack


def solution(mesh):
    placed = (P("recv", "tm"), P(), P("recv", "tm"))
    return jax.shard_map(
        local, mesh=mesh, in_specs=placed, out_specs=P("tm", "recv", None), check_vma=False
    )
```

profile of v0, /device:TPU:0, one launch (start us, length us, event | category | flops | bytes accessed | tf_op | source)
XLA Modules:
  0.0 157.9 jit_solution(15202526156247623894)
XLA Ops:
  6.5 1.3 collective-permute-start
  7.9 1.0 reduce_sum.29
  8.9 0.7 convert_bitcast_fusion
  9.6 0.9 convolution_bitcast_fusion.1
  10.4 0.9 copy.6
  11.3 23.1 %psum.15 = f32[16]{0:T(128)S(1)} all-reduce(f32[16]{0:T(128)S(1)} %convolution_bitcast_fusion.1), channel_id=1, replica_groups=mesh['recv'=8,'tm'=4] {'recv'}, use_global_device_ids=true, to_apply=%region_5.6 | all-reduce | flops 16 | bytes 128 | tf_op jit(solution)/shard_map/psum | solution.py:126
  34.4 4.2 %cosine_multiply_fusion = (f32[1024,256]{1,0:T(8,128)S(1)}, f32[1024,256]{1,0:T(8,128)S(1)}) fusion(s32[256]{0:T(256)S(1)} %get-tuple-element.17, s32[256]{0:T(256)S(1)} %get-tuple-element.18, f32[1024]{0:T(1024)S(1)} %get-tuple-element.15, pred[256]{0:T(512)(128)(4,1)S(1)} %compare_and_fusion, f32[1024]{0:T(1024)S(1)} %get-tuple-element.16), kind=kLoop, calls=%fused_computation.20 | loop fusion | flops 4456448 | bytes 2107648 | tf_op jit(solution)/shard_map/mul | solution.py:60
  38.8 0.3 fusion.21
  39.1 0.3 fusion.23
  39.4 0.4 fusion.19
  39.8 0.4 fusion.17
  40.2 0.4 fusion.7
  40.9 0.3 reshape.179
  41.1 0.4 fusion.6
  41.6 0.2 copy.5
  41.8 0.3 reshape.180
  42.1 16.6 %reduce_window.6 = f32[16,1024]{1,0:T(8,128)S(1)} reduce-window(f32[16,1024]{1,0:T(8,128)S(1)} %multiply_add_fusion.2, f32[]{:T(128)} %constant.92.clone.1), window={size=1x129 pad=0_0x64_64}, to_apply=%region_2.3 | reduce-window | flops 2097152 | bytes 131076 | tf_op jit(solution)/shard_map/reduce_window | solution.py:79
  58.7 1.1 convolution_bitcast_fusion
  59.9 67.6 %all-reduce.2.cloned.1.call-done = f32[16,2048]{1,0:T(8,128)} async-done(((f32[16,2048]{1,0:T(8,128)}), f32[16,2048]{1,0:T(8,128)}) %all-reduce.2.cloned.1.call-update) | async-done | bytes 131088 | tf_op jit(solution)/shard_map/psum | solution.py:126
  127.6 0.9 fusion.103
  128.4 0.3 multiply_add_fusion
  128.7 2.0 %multiply_reduce_fusion = (f32[16,16]{1,0:T(8,128)S(1)}, f32[16,16,256]{2,1,0:T(8,128)S(1)}) fusion(f32[1024,256]{1,0:T(8,128)S(1)} %get-tuple-element.12, f32[1024,256]{1,0:T(8,128)S(1)} %get-tuple-element.11, f32[16,16,1024]{2,1,0:T(8,128)S(1)} %get-tuple-element.6, f32[16,16,1024]{2,1,0:T(8,128)S(1)} %get-tuple-element.5), kind=kOutput, calls=%fused_computation.24 | convolution fusion | flops 1611792128 | bytes 4457472 | tf_op jit(solution)/shard_map/dot_general | solution.py:102
  130.7 0.8 divide_multiply_fusion
  131.6 19.4 %reduce-scatter.2.cloned.1.call-done = f32[4,16,256]{2,1,0:T(8,128)} async-done(((f32[16,16,256]{2,1,0:T(8,128)}), f32[4,16,256]{2,1,0:T(8,128)}) %reduce-scatter.2.cloned.1.call-update) | async-done | bytes 65552 | tf_op jit(solution)/shard_map/reduce_scatter | solution.py:128
  (23 shorter events, 0.7 us)
Async XLA Ops:
  6.5 121.0 %all-reduce.2.cloned.1.call-start = ((), (), s32[]{:S(2)}) async-start(), calls=%async_computation.1 | async-start | bytes 262144 | tf_op jit(solution)/shard_map/psum | solution.py:126
  6.5 32.1 %collective-permute-start = (f32[16,1024]{1,0:T(8,128)}, f32[16,1024]{1,0:T(8,128)S(1)}, u32[]{:S(2)}, u32[]{:S(2)}) collective-permute-start(f32[16,1024]{1,0:T(8,128)} %param.3), channel_id=1, source_target_pairs={{1,0},{2,1},{3,2},{5,4},{6,5},{7,6},{9,8},{10,9},{11,10},{13,12},{... | collective-permute-start | bytes 196616 | tf_op jit(solution)/shard_map/ppermute | solution.py:16
  41.1 17.5 %copy-start = (f32[1024]{0:T(1024)S(1)}, f32[1024]{0:T(1024)}, u32[]{:S(2)}) copy-start(f32[1024]{0:T(1024)} %constant.98.clone.1) | copy-start | bytes 12292
  41.6 17.1 %copy-start.1 = (s32[16]{0:T(128)S(1)}, s32[16]{0:T(128)}, u32[]{:S(2)}) copy-start(s32[16]{0:T(128)} %param.4) | copy-start | bytes 196
  59.8 91.2 %reduce-scatter.2.cloned.1.call-start = ((), (), s32[]{:S(2)}) async-start(), calls=%async_computation.2 | async-start | bytes 327680 | tf_op jit(solution)/shard_map/reduce_scatter | solution.py:128
Sparse Core Ops, SparseCore 0:
  59.9 67.6 all-reduce.1
  131.7 19.2 reduce-scatter.1
where the time goes:
time: 158 us
  waiting for transfers between devices  87.1 us (55%)
  other arithmetic  23.9 us (15%)
  blocking collectives  23.1 us (15%)
  between operations  13.6 us (9%)
  matrix products  6.17 us (4%)
  local copies, waits for them, and re-layouts  2.72 us (2%)
    psum x1, waiting for transfers between devices, local(): src_spec, src_mask = lax.psum((picked, picked_mask), 'recv')  67.6 us
    psum x1, blocking collectives, local(): src_spec, src_mask = lax.psum((picked, picked_mask), 'recv')  23.1 us
    reduce_scatter x1, waiting for transfers between devices, local(): lax.psum_scatter(partial_stack, 'tm', scatter_dimension=0, tiled=True)  19.4 us
    another operation x1, other arithmetic, whiten(): lax.reduce_window(power_spec, zero_init, lax.add, (1, 2 * SMOOTH + 1), (1...  16.6 us
    mul x1, other arithmetic, inverse_table(): factor * jnp.cos(angle)  4.15 us
  transfers between devices with their start and end apart: 3, of which 2 were waited for; matrix products, arithmetic and copies ran while one was open for 5% of the time, Pallas kernels for 0%

commit v1 on v0

v1 whole, which is shorter than its diff:
```python
import functools

import jax
import jax.numpy as jnp
import ml_dtypes
import numpy as np
from jax import lax
from jax.experimental import pallas as pl
from jax.experimental.pallas import tpu as pltpu
from jax.sharding import PartitionSpec as P

LANES = 128
LAGS = 256
SMOOTH = 64
RADIX = 16
PAIRS = RADIX // 2
BF = jnp.bfloat16
F32 = jnp.float32


def order():
    return [(0, 8)] + [(p, RADIX - p) for p in range(1, PAIRS)]


def halves(table):
    high = table.astype(ml_dtypes.bfloat16)
    low = (table - high.astype(np.float64)).astype(ml_dtypes.bfloat16)
    return high, low


@functools.cache
def tables(seglen):
    bins = seglen // 2
    keep = bins // RADIX
    samples = np.arange(seglen)
    taper = (0.5 - 0.5 * np.cos(2 * np.pi * samples / seglen)).reshape(RADIX, LANES)
    n2 = np.arange(LANES)[:, None]
    f2 = np.arange(keep)[None, :]
    forward = np.zeros((PAIRS, 2 * LANES, 2 * LANES))
    lag = np.zeros((PAIRS, 2, 2, keep, LAGS))
    counts = np.zeros((PAIRS, 2, 2, keep))
    lags = np.arange(LAGS)[None, :] - LAGS // 2
    for p, pair in enumerate(order()):
        for half, f1 in enumerate(pair):
            angle = 2 * np.pi * ((n2 * (f1 + RADIX * f2)) % seglen) / seglen
            cos, sin = np.cos(angle), np.sin(angle)
            cols = slice(half * LANES, (half + 1) * LANES)
            if p == 0:
                rows = slice(half * LANES, (half + 1) * LANES)
                forward[p, rows, cols] = np.concatenate([cos, -sin], 1)
            else:
                sign = -1.0 if half == 0 else 1.0
                forward[p, :LANES, cols] = np.concatenate([cos, -sin], 1)
                forward[p, LANES:, cols] = sign * np.concatenate([sin, cos], 1)
            f = f1 + RADIX * np.arange(keep)[:, None]
            angle = 2 * np.pi * ((f * lags) % seglen) / seglen
            factor = np.where(f == 0, 1.0, 2.0) / seglen
            lag[p, half, 0] = factor * np.cos(angle)
            lag[p, half, 1] = -factor * np.sin(angle)
            f = f[:, 0]
            counts[p, half] = np.minimum(f + SMOOTH, bins - 1) - np.maximum(f - SMOOTH, 0) + 1
    inverse_counts = (1.0 / counts).reshape(RADIX, LANES)
    lag = lag.reshape(PAIRS, 2 * LANES, LAGS)
    return (
        taper.astype(np.float32),
        inverse_counts.astype(np.float32),
        *halves(forward),
        *halves(lag),
    )


def radix_step(x):
    r = float(np.sqrt(0.5))
    c1 = float(np.cos(np.pi / 8))
    c3 = float(np.cos(3 * np.pi / 8))
    c = [None] + [x[n] + x[16 - n] for n in range(1, 8)]
    s = [None] + [x[n] - x[16 - n] for n in range(1, 8)]
    e = [x[0] + x[8]] + [c[n] + c[8 - n] for n in range(1, 4)] + [c[4]]
    o = [x[0] - x[8]] + [c[n] - c[8 - n] for n in range(1, 4)]
    g = [None] + [s[n] - s[8 - n] for n in range(1, 4)]
    h = [None] + [s[n] + s[8 - n] for n in range(1, 4)] + [s[4]]
    e04 = e[0] + e[4]
    e04m = e[0] - e[4]
    e13 = e[1] + e[3]
    e13m = r * (e[1] - e[3])
    e042 = e04 + e[2]
    g13 = r * (g[1] + g[3])
    o2 = r * o[2]
    h2 = r * h[2]
    re = {
        0: e042 + e13,
        8: e042 - e13,
        4: e04 - e[2],
        2: e04m + e13m,
        6: e04m - e13m,
        1: (o[0] + o2) + (c1 * o[1] + c3 * o[3]),
        7: (o[0] + o2) - (c1 * o[1] + c3 * o[3]),
        3: (o[0] - o2) + (c3 * o[1] - c1 * o[3]),
        5: (o[0] - o2) - (c3 * o[1] - c1 * o[3]),
    }
    im = {
        2: g13 + g[2],
        4: g[1] - g[3],
        6: g13 - g[2],
        1: (h2 + h[4]) + (c3 * h[1] + c1 * h[3]),
        7: (c3 * h[1] + c1 * h[3]) - (h2 + h[4]),
        3: (h2 - h[4]) + (c1 * h[1] - c3 * h[3]),
        5: (c1 * h[1] - c3 * h[3]) - (h2 - h[4]),
    }
    return [(re[0], re[8])] + [(re[p], im[p]) for p in range(1, PAIRS)]


def split(value):
    high = value.astype(BF)
    return high, (value - high.astype(F32)).astype(BF)


def dot(a, b):
    return jnp.dot(a, b, preferred_element_type=F32)


def spectra(xs, count, shift, taper, high_table, low_table, lhs, z):
    seglen = RADIX * LANES
    step = 16

    def group(first):
        x = [xs[first : first + step, n * LANES : (n + 1) * LANES] for n in range(PAIRS)]
        x += [xs[first + shift : first + shift + step, n * LANES : (n + 1) * LANES] for n in range(PAIRS)]
        total = x[0]
        for part in x[1:]:
            total = total + part
        mean = jnp.sum(total, axis=1, keepdims=True) * (1.0 / seglen)
        x = [(x[n] - mean) * taper[n : n + 1, :] for n in range(RADIX)]
        for p, parts in enumerate(radix_step(x)):
            for i, part in enumerate(parts):
                high, low = split(part)
                lhs[p, first : first + step, i * LANES : (i + 1) * LANES] = high
                lhs[p, count + first : count + first + step, i * LANES : (i + 1) * LANES] = low

    for first in range(0, count, step):
        group(first)
    for p in range(PAIRS):
        both = dot(lhs[p], high_table[p])
        z[p] = both[:count] + both[count:] + dot(lhs[p, :count, :], low_table[p])


def whiten(z, first, inverse_counts, put):
    keep = LANES // 2
    lane = lax.broadcasted_iota(jnp.int32, (8, LANES), 1) % keep
    blocks = [z[q // 2, pl.ds(first, 8), (q % 2) * LANES : (q % 2 + 1) * LANES] for q in range(RADIX)]
    place = [f1 for pair in order() for f1 in pair]
    power = [None] * RADIX
    for q, block in enumerate(blocks):
        square = block * block
        power[place[q]] = square + pltpu.roll(square, keep, 1)
    upto = [power[0]]
    for f1 in range(1, RADIX):
        upto.append(upto[-1] + power[f1])
    since = [power[RADIX - 1]]
    for f1 in range(RADIX - 2, -1, -1):
        since.append(since[-1] + power[f1])
    since = since[::-1]
    total = upto[-1]

    def later(value, by):
        return jnp.where(lane < keep - by, pltpu.roll(value, LANES - by, 1), 0.0)

    def earlier(value, by):
        return jnp.where(lane >= by, pltpu.roll(value, by, 1), 0.0)

    reach = SMOOTH // RADIX
    inner = total
    for by in range(1, reach):
        inner = inner + (later(total, by) + earlier(total, by))
    for q, block in enumerate(blocks):
        f1 = place[q]
        window = inner + (earlier(since[f1], reach) + later(upto[f1], reach))
        scale = lax.rsqrt(window * inverse_counts[q : q + 1, :] + 1e-6)
        put(q, block * scale)


def pick_kernel(per_group, src, *refs):
    blocks, out = refs[:-1], refs[-1]
    rows = blocks[0].shape[0]
    group = lax.axis_index("recv")
    me = lax.axis_index("tm")
    for i in range(per_group):
        row = src[group * per_group + i] - group * rows
        for k, block in enumerate(blocks):
            out[pl.ds((me ^ k) * per_group + i, 1), :] = block[pl.ds(row, 1), :]


def receiver_kernel(segs, *refs):
    blocks = refs[:segs]
    taper, inverse_counts, high_table, low_table, out, mask, xs, lhs, z = refs[segs:]
    rows, width = blocks[0].shape
    hop = width - LANES
    me = lax.axis_index("tm")
    for k, block in enumerate(blocks):
        start = pl.multiple_of((me ^ k) * rows, rows)
        xs[pl.ds(start, rows), :] = block[:, :hop]
        mask[pl.ds(start, rows), :] = block[:, hop:]
    xs[segs * rows :, :] = jnp.zeros((rows, hop), F32)
    count = segs * rows
    spectra(xs, count, rows, taper, high_table, low_table, lhs, z)
    for first in range(0, count, 8):

        def put(q, value):
            out[q // 2, pl.ds(first, 8), (q % 2) * LANES : (q % 2 + 1) * LANES] = value

        whiten(z, first, inverse_counts, put)


def stack_kernel(segs, parts, spectrum, mask, *refs):
    pay = refs[:parts]
    taper, inverse_counts, high_table, low_table, high_lag, low_lag, out = refs[parts : parts + 7]
    xs, lhs, z, straight, crossed, prod_high, prod_low = refs[parts + 7 :]
    hop = pay[0].shape[1] - LANES
    keep = LANES // 2
    per_part = pay[0].shape[0] // segs
    sources = per_part * parts
    rows = mask.shape[0] // segs
    group = lax.axis_index("recv")
    for j, part in enumerate(pay):
        slot = (group + j) % parts
        for k in range(segs):
            for i in range(per_part):
                row = k * per_part + i
                xs[pl.ds(k * sources + slot * per_part + i, 1), :] = part[row : row + 1, :]
    xs[segs * sources :, :] = jnp.zeros((sources, hop + LANES), F32)
    count = segs * sources
    spectra(xs, count, sources, taper, high_table, low_table, lhs, z)
    low_half = lax.broadcasted_iota(jnp.int32, (8, LANES), 1) < keep
    for first in range(0, count, 8):

        def put(q, value):
            turned = pltpu.roll(value, keep, 1)
            cols = slice((q % 2) * LANES, (q % 2 + 1) * LANES)
            straight[q // 2, first : first + 8, cols] = jnp.where(low_half, value, turned)
            crossed[q // 2, first : first + 8, cols] = jnp.where(low_half, turned, -value)

        whiten(z, first, inverse_counts, put)
    total = None
    for p in range(PAIRS):
        for half in range(2):
            cols = slice(half * LANES, (half + 1) * LANES)
            for k in range(segs):
                recv = spectrum[p, k * rows : (k + 1) * rows, cols]
                turned = pltpu.roll(recv, keep, 1)
                for s in range(sources):
                    i = k * sources + s
                    cross = straight[p, i : i + 1, cols] * recv + crossed[p, i : i + 1, cols] * turned
                    prod_high[p, i * rows : (i + 1) * rows, cols], prod_low[p, i * rows : (i + 1) * rows, cols] = split(cross)
        part = dot(prod_high[p], high_lag[p]) + dot(prod_low[p], high_lag[p]) + dot(prod_high[p], low_lag[p])
        total = part if total is None else total + part
    scale = lax.rsqrt(jnp.mean(total * total, axis=1, keepdims=True) + 1e-6)
    normed = total * scale
    for s in range(sources):
        stack = None
        for k in range(segs):
            i = k * sources + s
            weight = mask[k * rows : (k + 1) * rows, :] * xs[i : i + 1, hop:]
            weight = jnp.concatenate([weight] * (LAGS // LANES), axis=1)
            term = weight * normed[i * rows : (i + 1) * rows, :]
            stack = term if stack is None else stack + term
        out[s] = stack


def vmem(count):
    return [pl.BlockSpec(memory_space=pltpu.VMEM)] * count


PARAMS = dict(compiler_params=pltpu.CompilerParams(vmem_limit_bytes=32 * 1024 * 1024))


def local(record, source_channels, valid_mask):
    rows, hop = record.shape
    segs = lax.axis_size("tm")
    groups = lax.axis_size("recv")
    sources = source_channels.shape[0]
    mine = sources // segs
    taper, inverse_counts, high_table, low_table, high_lag, low_lag = tables(2 * hop)
    mask = jnp.broadcast_to(valid_mask.astype(F32), (rows, LANES))
    payload = jnp.concatenate([record, mask], axis=1)
    width = hop + LANES
    blocks = [payload] + [lax.ppermute(payload, "tm", [(i, i ^ k) for i in range(segs)]) for k in range(1, segs)]

    if groups <= sources and groups % segs == 0:
        per_group = sources // groups
        parts = groups // segs
        picked = pl.pallas_call(
            functools.partial(pick_kernel, per_group),
            out_shape=jax.ShapeDtypeStruct((segs * per_group, width), F32),
            in_specs=[pl.BlockSpec(memory_space=pltpu.SMEM)] + vmem(segs),
            out_specs=pl.BlockSpec(memory_space=pltpu.VMEM),
            name="pick",
            **PARAMS,
        )(source_channels, *blocks)
        pay = []
        for j in range(parts):
            route = [
                ((t * parts + (r + j) % parts) * segs + (r // parts + segs // 2) % segs, r * segs + t)
                for r in range(groups)
                for t in range(segs)
            ]
            pay.append(lax.ppermute(picked, ("recv", "tm"), route))
    else:
        parts = 1
        row = source_channels - lax.axis_index("recv") * rows
        here = (row >= 0) & (row < rows)
        places = lax.axis_index("tm") ^ jnp.arange(segs)
        held = jnp.stack(blocks)[places]
        picked = jnp.where(here[None, :, None], held[:, jnp.clip(row, 0, rows - 1), :], 0.0)
        whole = lax.psum(picked, "recv")
        whole = lax.dynamic_slice_in_dim(whole, lax.axis_index("tm") * mine, mine, 1)
        pay = [whole.reshape(segs * mine, width)]

    count = segs * rows
    spectrum, weights = pl.pallas_call(
        functools.partial(receiver_kernel, segs),
        out_shape=(
            jax.ShapeDtypeStruct((PAIRS, count, 2 * LANES), F32),
            jax.ShapeDtypeStruct((count, LANES), F32),
        ),
        in_specs=vmem(segs + 4),
        out_specs=tuple(vmem(2)),
        scratch_shapes=[
            pltpu.VMEM((count + rows, hop), F32),
            pltpu.VMEM((PAIRS, 2 * count, 2 * LANES), BF),
            pltpu.VMEM((PAIRS, count, 2 * LANES), F32),
        ],
        name="receivers",
        **PARAMS,
    )(*blocks, taper, inverse_counts, high_table, low_table)

    src_count = segs * mine
    return pl.pallas_call(
        functools.partial(stack_kernel, segs, parts),
        out_shape=jax.ShapeDtypeStruct((mine, rows, LAGS), F32),
        in_specs=vmem(2 + parts + 6),
        out_specs=pl.BlockSpec(memory_space=pltpu.VMEM),
        scratch_shapes=[
            pltpu.VMEM((src_count + mine, width), F32),
            pltpu.VMEM((PAIRS, 2 * src_count, 2 * LANES), BF),
            pltpu.VMEM((PAIRS, src_count, 2 * LANES), F32),
            pltpu.VMEM((PAIRS, src_count, 2 * LANES), F32),
            pltpu.VMEM((PAIRS, src_count, 2 * LANES), F32),
            pltpu.VMEM((PAIRS, src_count * rows, 2 * LANES), BF),
            pltpu.VMEM((PAIRS, src_count * rows, 2 * LANES), BF),
        ],
        name="stacks",
        **PARAMS,
    )(spectrum, weights, *pay, taper, inverse_counts, high_table, low_table, high_lag, low_lag)


def solution(mesh):
    placed = (P("recv", "tm"), P(), P("recv", "tm"))
    return jax.shard_map(
        local, mesh=mesh, in_specs=placed, out_specs=P("tm", "recv", None), check_vma=False
    )
```

time: 158 us -> 24.7 us (0.16)
  the two profiles are of different devices: /device:TPU:0 before, /device:TPU:1 now
where the time goes in v1:
time: 24.7 us; the launch traced here: 24.4 us
  starting transfers between devices  8.68 us (35%)
  local copies, waits for them, and re-layouts  5.43 us (22%)
  Pallas kernels  4.49 us (18%)
  waiting for transfers between devices  4.18 us (17%)
  other arithmetic  1.52 us (6%)
    ppermute x2, starting transfers between devices, local(): pay.append(lax.ppermute(picked, ('recv', 'tm'), route))  5.82 us
    unnamed x18, local copies, waits for them, and re-layouts  5.35 us
    ppermute x3, waiting for transfers between devices, local(): lax.ppermute(payload, 'tm', [(i, i ^ k) for i in range(segs)])  4.18 us
    ppermute x3, starting transfers between devices, local(): lax.ppermute(payload, 'tm', [(i, i ^ k) for i in range(segs)])  2.87 us
    pallas_call x1, Pallas kernels, local(): pl.pallas_call(functools.partial(stack_kernel, segs, parts), out_shape=ja...  2.85 us
    pallas_call x1, Pallas kernels, local(): pl.pallas_call(functools.partial(receiver_kernel, segs), out_shape=(jax.S...  1.07 us
    concatenate x1, other arithmetic, local(): payload = jnp.concatenate([record, mask], axis=1)  0.86 us
    broadcast_in_dim x1, other arithmetic, local(): mask = jnp.broadcast_to(valid_mask.astype(F32), (rows, LANES))  0.66 us
  transfers between devices with their start and end apart: 5, of which 2 were waited for; matrix products, arithmetic and copies ran while one was open for 0% of the time, Pallas kernels for 4%

profile of v1, /device:TPU:1, one launch (start us, length us, event | category | flops | bytes accessed | tf_op | source)
XLA Modules:
  0.0 24.4 jit_solution(1396827957479728494)
XLA Ops:
  0.0 0.7 %convert_bitcast_fusion = f32[16]{0:T(128)S(1)} fusion(s32[16,1]{0,1:T(1,128)} %param.11), kind=kLoop, calls=%fused_computation.1 | loop fusion | flops 16 | bytes 128 | tf_op jit(solution)/shard_map/broadcast_in_dim | solution.py:283
  0.7 0.1 broadcast_in_dim.8
  0.7 0.9 %pad_maximum_fusion.refs_0_ = f32[16,1152]{1,0:T(8,128)S(1)} fusion(f32[16,128]{1,0:T(8,128)S(1)} %broadcast_in_dim.8, f32[16,1024]{1,0:T(8,128)} %param.9), kind=kLoop, calls=%fused_computation | loop fusion | flops 18432 | bytes 147456 | tf_op jit(solution)/shard_map/concatenate | solution.py:284
  1.6 0.1 collective-permute-start
  1.7 2.7 %collective-permute-start.1 = (f32[16,1152]{1,0:T(8,128)S(1)}, f32[16,1152]{1,0:T(8,128)S(1)}, u32[]{:S(2)}, u32[]{:S(2)}) collective-permute-start(f32[16,1152]{1,0:T(8,128)S(1)} %pad_maximum_fusion.refs_0_), channel_id=1, source_target_pairs={{0,2},{1,3},{2,0},{3,1},{4,6},{5,7},{6,4},{7,5},{8,10},{9,11},{10,... | collective-permute-start | bytes 221192 | tf_op jit(solution)/shard_map/ppermute | solution.py:286
  4.4 0.0 collective-permute-start.2
  4.5 0.0 collective-permute-done.refs_1_
  4.5 2.5 %collective-permute-done.1.refs_2_ = f32[16,1152]{1,0:T(8,128)S(1)} collective-permute-done((f32[16,1152]{1,0:T(8,128)S(1)}, f32[16,1152]{1,0:T(8,128)S(1)}, u32[]{:S(2)}, u32[]{:S(2)}) %collective-permute-start.1) | collective-permute-done | bytes 73760 | tf_op jit(solution)/shard_map/ppermute | solution.py:286
  7.0 1.7 %collective-permute-done.2.refs_3_ = f32[16,1152]{1,0:T(8,128)S(1)} collective-permute-done((f32[16,1152]{1,0:T(8,128)S(1)}, f32[16,1152]{1,0:T(8,128)S(1)}, u32[]{:S(2)}, u32[]{:S(2)}) %collective-permute-start.2) | collective-permute-done | bytes 73760 | tf_op jit(solution)/shard_map/ppermute | solution.py:286
  8.7 0.0 copy-done.8
  8.7 0.6 %pick.1 = f32[8,1152]{1,0:T(8,128)S(1)} custom-call(s32[16]{0:T(128)S(1)} %copy-done.8, f32[16,1152]{1,0:T(8,128)S(1)} %pad_maximum_fusion.refs_0_, f32[16,1152]{1,0:T(8,128)S(1)} %collective-permute-done.refs_1_, f32[16,1152]{1,0:T(8,128)S(1)} %collective-permute-done.1.refs_2_, f32[16,1152]{1,0:T(8,128)S(1)} %collective-permute-done.2.refs_3_), custom_call_target="tpu_custom_call" | custom-call | tf_op jit(solution)/shard_map/pick/pallas_call | solution.py:291
  9.2 3.8 %collective-permute-start.3 = (f32[8,1152]{1,0:T(8,128)S(1)}, f32[8,1152]{1,0:T(8,128)S(1)}, u32[]{:S(2)}, u32[]{:S(2)}) collective-permute-start(f32[8,1152]{1,0:T(8,128)S(1)} %pick.1), channel_id=1, source_target_pairs={{2,0},{10,1},{18,2},{26,3},{6,4},{14,5},{22,6},{30,7},{3,8},{11,9}... | collective-permute-start | bytes 110600 | tf_op jit(solution)/shard_map/ppermute | solution.py:306
  13.1 2.0 %collective-permute-start.4 = (f32[8,1152]{1,0:T(8,128)S(1)}, f32[8,1152]{1,0:T(8,128)S(1)}, u32[]{:S(2)}, u32[]{:S(2)}) collective-permute-start(f32[8,1152]{1,0:T(8,128)S(1)} %pick.1), channel_id=1, source_target_pairs={{6,0},{14,1},{22,2},{30,3},{2,4},{10,5},{18,6},{26,7},{7,8},{15,9}... | collective-permute-start | bytes 110600 | tf_op jit(solution)/shard_map/ppermute | solution.py:306
  15.1 0.0 copy-done.6
  15.1 1.2 %copy-done = bf16[8,256,256]{2,1,0:T(8,128)(2,1)S(1)} copy-done((bf16[8,256,256]{2,1,0:T(8,128)(2,1)S(1)}, bf16[8,256,256]{2,1,0:T(8,128)(2,1)}, u32[]{:S(2)}) %copy-start) | copy-done | bytes 1048600
  16.3 1.2 %copy-done.2 = bf16[8,256,256]{2,1,0:T(8,128)(2,1)S(1)} copy-done((bf16[8,256,256]{2,1,0:T(8,128)(2,1)S(1)}, bf16[8,256,256]{2,1,0:T(8,128)(2,1)}, u32[]{:S(2)}) %copy-start.2) | copy-done | bytes 1048600
  17.5 1.1 %receivers.1 = (f32[8,64,256]{2,1,0:T(8,128)S(1)}, f32[64,128]{1,0:T(8,128)S(1)}) custom-call(f32[16,1152]{1,0:T(8,128)S(1)} %pad_maximum_fusion.refs_0_, f32[16,1152]{1,0:T(8,128)S(1)} %collective-permute-done.refs_1_, f32[16,1152]{1,0:T(8,128)S(1)} %collective-permute-done.1.refs_2_, f32[16,1152]{1,0:T(8,128)S(1)} %collective-permute-done.2.refs_3_, ...), custom_call_target="tpu_custom_call" | custom-call | tf_op jit(solution)/shard_map/receivers/pallas_call | solution.py:319
  18.6 0.0 collective-permute-done.3.refs_0_
  18.6 0.0 collective-permute-done.4.refs_1_
  18.6 0.1 copy-done.1
  18.7 0.3 %copy-done.3 = bf16[8,256,256]{2,1,0:T(8,128)(2,1)S(1)} copy-done((bf16[8,256,256]{2,1,0:T(8,128)(2,1)S(1)}, bf16[8,256,256]{2,1,0:T(8,128)(2,1)}, u32[]{:S(2)}) %copy-start.3) | copy-done | bytes 1048600
  19.1 1.2 %copy-done.4 = bf16[8,256,256]{2,1,0:T(8,128)(2,1)S(1)} copy-done((bf16[8,256,256]{2,1,0:T(8,128)(2,1)S(1)}, bf16[8,256,256]{2,1,0:T(8,128)(2,1)}, u32[]{:S(2)}) %copy-start.4) | copy-done | bytes 1048600
  20.3 1.2 %copy-done.5 = bf16[8,256,256]{2,1,0:T(8,128)(2,1)S(1)} copy-done((bf16[8,256,256]{2,1,0:T(8,128)(2,1)S(1)}, bf16[8,256,256]{2,1,0:T(8,128)(2,1)}, u32[]{:S(2)}) %copy-start.5) | copy-done | bytes 1048600
  21.5 2.8 %stacks.1 = f32[4,16,256]{2,1,0:T(8,128)} custom-call(f32[8,64,256]{2,1,0:T(8,128)S(1)} %get-tuple-element.7.spectrum, f32[64,128]{1,0:T(8,128)S(1)} %get-tuple-element.8.mask, f32[8,1152]{1,0:T(8,128)S(1)} %collective-permute-done.3.refs_0_, f32[8,1152]{1,0:T(8,128)S(1)} %collective-permute-done.4.refs_1_, f32[16,128]{1,0:T(8,128)S(1)} %copy-done.6, ...), custom_call_target="tpu_custom_call" | custom-call | tf_op jit(solution)/shard_map/stacks/pallas_call | solution.py:337
  (10 shorter events, 0.0 us)
Async XLA Ops:
  0.7 7.9 %copy-start.8 = (s32[16]{0:T(128)S(1)}, s32[16]{0:T(128)}, u32[]{:S(2)}) copy-start(s32[16]{0:T(128)} %src.1) | copy-start | bytes 196
  1.6 13.5 %copy-start.6 = (f32[16,128]{1,0:T(8,128)S(1)}, f32[16,128]{1,0:T(8,128)}, u32[]{:S(2)}) copy-start(f32[16,128]{1,0:T(8,128)} %constant.12.clone.refs_4_.refs_2_) | copy-start | bytes 24580
  1.6 13.5 %copy-start.7 = (f32[16,128]{1,0:T(8,128)S(1)}, f32[16,128]{1,0:T(8,128)}, u32[]{:S(2)}) copy-start(f32[16,128]{1,0:T(8,128)} %constant.13.clone.refs_5_.refs_3_) | copy-start | bytes 24580
  1.6 2.9 %collective-permute-start = (f32[16,1152]{1,0:T(8,128)S(1)}, f32[16,1152]{1,0:T(8,128)S(1)}, u32[]{:S(2)}, u32[]{:S(2)}) collective-permute-start(f32[16,1152]{1,0:T(8,128)S(1)} %pad_maximum_fusion.refs_0_), channel_id=1, source_target_pairs={{0,1},{1,0},{2,3},{3,2},{4,5},{5,4},{6,7},{7,6},{8,9},{9,8},{10,11... | collective-permute-start | bytes 221192 | tf_op jit(solution)/shard_map/ppermute | solution.py:286
  1.7 5.2 %collective-permute-start.1 = (f32[16,1152]{1,0:T(8,128)S(1)}, f32[16,1152]{1,0:T(8,128)S(1)}, u32[]{:S(2)}, u32[]{:S(2)}) collective-permute-start(f32[16,1152]{1,0:T(8,128)S(1)} %pad_maximum_fusion.refs_0_), channel_id=1, source_target_pairs={{0,2},{1,3},{2,0},{3,1},{4,6},{5,7},{6,4},{7,5},{8,10},{9,11},{10,... | collective-permute-start | bytes 221192 | tf_op jit(solution)/shard_map/ppermute | solution.py:286
  4.4 4.2 %collective-permute-start.2 = (f32[16,1152]{1,0:T(8,128)S(1)}, f32[16,1152]{1,0:T(8,128)S(1)}, u32[]{:S(2)}, u32[]{:S(2)}) collective-permute-start(f32[16,1152]{1,0:T(8,128)S(1)} %pad_maximum_fusion.refs_0_), channel_id=1, source_target_pairs={{0,3},{1,2},{2,1},{3,0},{4,7},{5,6},{6,5},{7,4},{8,11},{9,10},{10,... | collective-permute-start | bytes 221192 | tf_op jit(solution)/shard_map/ppermute | solution.py:286
  9.2 9.4 %collective-permute-start.3 = (f32[8,1152]{1,0:T(8,128)S(1)}, f32[8,1152]{1,0:T(8,128)S(1)}, u32[]{:S(2)}, u32[]{:S(2)}) collective-permute-start(f32[8,1152]{1,0:T(8,128)S(1)} %pick.1), channel_id=1, source_target_pairs={{2,0},{10,1},{18,2},{26,3},{6,4},{14,5},{22,6},{30,7},{3,8},{11,9}... | collective-permute-start | bytes 110600 | tf_op jit(solution)/shard_map/ppermute | solution.py:306
  13.1 5.5 %collective-permute-start.4 = (f32[8,1152]{1,0:T(8,128)S(1)}, f32[8,1152]{1,0:T(8,128)S(1)}, u32[]{:S(2)}, u32[]{:S(2)}) collective-permute-start(f32[8,1152]{1,0:T(8,128)S(1)} %pick.1), channel_id=1, source_target_pairs={{6,0},{14,1},{22,2},{30,3},{2,4},{10,5},{18,6},{26,7},{7,8},{15,9}... | collective-permute-start | bytes 110600 | tf_op jit(solution)/shard_map/ppermute | solution.py:306
  15.1 1.2 %copy-start = (bf16[8,256,256]{2,1,0:T(8,128)(2,1)S(1)}, bf16[8,256,256]{2,1,0:T(8,128)(2,1)}, u32[]{:S(2)}) copy-start(bf16[8,256,256]{2,1,0:T(8,128)(2,1)} %constant.14.clone.refs_6_.refs_4_) | copy-start | bytes 3145732
  16.3 1.2 %copy-start.2 = (bf16[8,256,256]{2,1,0:T(8,128)(2,1)S(1)}, bf16[8,256,256]{2,1,0:T(8,128)(2,1)}, u32[]{:S(2)}) copy-start(bf16[8,256,256]{2,1,0:T(8,128)(2,1)} %constant.15.clone.refs_7_.refs_5_) | copy-start | bytes 3145732
  17.5 1.2 %copy-start.1 = (bf16[8,256,256]{2,1,0:T(8,128)(2,1)S(1)}, bf16[8,256,256]{2,1,0:T(8,128)(2,1)}, u32[]{:S(2)}) copy-start(bf16[8,256,256]{2,1,0:T(8,128)(2,1)} %constant.14.clone.refs_6_.refs_4_) | copy-start | bytes 3145732
  17.5 1.5 %copy-start.3 = (bf16[8,256,256]{2,1,0:T(8,128)(2,1)S(1)}, bf16[8,256,256]{2,1,0:T(8,128)(2,1)}, u32[]{:S(2)}) copy-start(bf16[8,256,256]{2,1,0:T(8,128)(2,1)} %constant.15.clone.refs_7_.refs_5_) | copy-start | bytes 3145732
  19.1 1.2 %copy-start.4 = (bf16[8,256,256]{2,1,0:T(8,128)(2,1)S(1)}, bf16[8,256,256]{2,1,0:T(8,128)(2,1)}, u32[]{:S(2)}) copy-start(bf16[8,256,256]{2,1,0:T(8,128)(2,1)} %constant.16.clone.refs_6_) | copy-start | bytes 3145732
  20.3 1.2 %copy-start.5 = (bf16[8,256,256]{2,1,0:T(8,128)(2,1)S(1)}, bf16[8,256,256]{2,1,0:T(8,128)(2,1)}, u32[]{:S(2)}) copy-start(bf16[8,256,256]{2,1,0:T(8,128)(2,1)} %constant.17.clone.refs_7_) | copy-start | bytes 3145732

commit v2 on v1

--- a/solution.py
+++ b/solution.py
@@ -24,8 +24,7 @@
 
 def halves(table):
     high = table.astype(ml_dtypes.bfloat16)
-    low = (table - high.astype(np.float64)).astype(ml_dtypes.bfloat16)
-    return high, low
+    return np.stack([high, (table - high.astype(np.float64)).astype(ml_dtypes.bfloat16)])
 
 
 @functools.cache
@@ -64,8 +63,8 @@
     return (
         taper.astype(np.float32),
         inverse_counts.astype(np.float32),
-        *halves(forward),
-        *halves(lag),
+        halves(forward),
+        halves(lag),
     )
 
 
@@ -119,7 +118,7 @@
     return jnp.dot(a, b, preferred_element_type=F32)
 
 
-def spectra(xs, count, shift, taper, high_table, low_table, lhs, z):
+def spectra(xs, count, shift, taper, table, lhs, z, ready=None):
     seglen = RADIX * LANES
     step = 16
 
@@ -140,8 +139,10 @@
     for first in range(0, count, step):
         group(first)
     for p in range(PAIRS):
-        both = dot(lhs[p], high_table[p])
-        z[p] = both[:count] + both[count:] + dot(lhs[p, :count, :], low_table[p])
+        if ready is not None:
+            ready(p)
+        both = dot(lhs[p], table[0, p])
+        z[p] = both[:count] + both[count:] + dot(lhs[p, :count, :], table[1, p])
 
 
 def whiten(z, first, inverse_counts, put):
@@ -179,6 +180,23 @@
         put(q, block * scale)
 
 
+def join_kernel(record, valid, src, out, src_out, row, sems):
+    rows, hop = record.shape
+    copies = [
+        pltpu.make_async_copy(record, out.at[:, pl.ds(0, hop)], sems.at[0]),
+        pltpu.make_async_copy(valid, row, sems.at[1]),
+        pltpu.make_async_copy(src, src_out, sems.at[2]),
+    ]
+    for copy in copies:
+        copy.start()
+    copies[1].wait()
+    here = lax.broadcasted_iota(jnp.int32, (rows, rows), 0) == lax.broadcasted_iota(jnp.int32, (rows, rows), 1)
+    column = jnp.sum(jnp.where(here, row[...].astype(F32), 0.0), axis=1, keepdims=True)
+    out[:, hop:] = jnp.broadcast_to(column, (rows, LANES))
+    copies[2].wait()
+    copies[0].wait()
+
+
 def pick_kernel(per_group, src, *refs):
     blocks, out = refs[:-1], refs[-1]
     rows = blocks[0].shape[0]
@@ -192,7 +210,13 @@
 
 def receiver_kernel(segs, *refs):
     blocks = refs[:segs]
-    taper, inverse_counts, high_table, low_table, out, mask, xs, lhs, z = refs[segs:]
+    constants = refs[segs : segs + 4]
+    out, mask, taper, inverse_counts, table, lag, xs, lhs, z, sems = refs[segs + 4 :]
+    small = [pltpu.make_async_copy(constants[i], (taper, inverse_counts)[i], sems.at[i]) for i in range(2)]
+    steps = [pltpu.make_async_copy(constants[2].at[p // 4, pl.ds(2 * (p % 4), 2)], table.at[p // 4, pl.ds(2 * (p % 4), 2)], sems.at[2 + p]) for p in range(PAIRS)]
+    rest = [pltpu.make_async_copy(constants[3].at[p // 4, pl.ds(2 * (p % 4), 2)], lag.at[p // 4, pl.ds(2 * (p % 4), 2)], sems.at[2 + PAIRS + p]) for p in range(PAIRS)]
+    for copy in small + steps + rest:
+        copy.start()
     rows, width = blocks[0].shape
     hop = width - LANES
     me = lax.axis_index("tm")
@@ -202,19 +226,23 @@
         mask[pl.ds(start, rows), :] = block[:, hop:]
     xs[segs * rows :, :] = jnp.zeros((rows, hop), F32)
     count = segs * rows
-    spectra(xs, count, rows, taper, high_table, low_table, lhs, z)
+    for copy in small + steps:
+        copy.wait()
+    spectra(xs, count, rows, taper, table, lhs, z, None)
     for first in range(0, count, 8):
 
         def put(q, value):
             out[q // 2, pl.ds(first, 8), (q % 2) * LANES : (q % 2 + 1) * LANES] = value
 
         whiten(z, first, inverse_counts, put)
+    for copy in rest:
+        copy.wait()
 
 
 def stack_kernel(segs, parts, spectrum, mask, *refs):
     pay = refs[:parts]
-    taper, inverse_counts, high_table, low_table, high_lag, low_lag, out = refs[parts : parts + 7]
-    xs, lhs, z, straight, crossed, prod_high, prod_low = refs[parts + 7 :]
+    taper, inverse_counts, table, lag, out = refs[parts : parts + 5]
+    xs, lhs, z, straight, crossed, prod_high, prod_low = refs[parts + 5 :]
     hop = pay[0].shape[1] - LANES
     keep = LANES // 2
     per_part = pay[0].shape[0] // segs
@@ -229,7 +257,7 @@
                 xs[pl.ds(k * sources + slot * per_part + i, 1), :] = part[row : row + 1, :]
     xs[segs * sources :, :] = jnp.zeros((sources, hop + LANES), F32)
     count = segs * sources
-    spectra(xs, count, sources, taper, high_table, low_table, lhs, z)
+    spectra(xs, count, sources, taper, table, lhs, z)
     low_half = lax.broadcasted_iota(jnp.int32, (8, LANES), 1) < keep
     for first in range(0, count, 8):
 
@@ -251,7 +279,7 @@
                     i = k * sources + s
                     cross = straight[p, i : i + 1, cols] * recv + crossed[p, i : i + 1, cols] * turned
                     prod_high[p, i * rows : (i + 1) * rows, cols], prod_low[p, i * rows : (i + 1) * rows, cols] = split(cross)
-        part = dot(prod_high[p], high_lag[p]) + dot(prod_low[p], high_lag[p]) + dot(prod_high[p], low_lag[p])
+        part = dot(prod_high[p], lag[0, p]) + dot(prod_low[p], lag[0, p]) + dot(prod_high[p], lag[1, p])
         total = part if total is None else total + part
     scale = lax.rsqrt(jnp.mean(total * total, axis=1, keepdims=True) + 1e-6)
     normed = total * scale
@@ -273,17 +301,40 @@
 PARAMS = dict(compiler_params=pltpu.CompilerParams(vmem_limit_bytes=32 * 1024 * 1024))
 
 
+def others(value, segs):
+    held = {0: value}
+    bit = segs // 2
+    while bit:
+        for k in list(held):
+            held[k ^ bit] = lax.ppermute(held[k], "tm", [(i, i ^ bit) for i in range(segs)])
+        bit //= 2
+    return [held[k] for k in range(segs)]
+
+
 def local(record, source_channels, valid_mask):
     rows, hop = record.shape
     segs = lax.axis_size("tm")
     groups = lax.axis_size("recv")
     sources = source_channels.shape[0]
     mine = sources // segs
-    taper, inverse_counts, high_table, low_table, high_lag, low_lag = tables(2 * hop)
-    mask = jnp.broadcast_to(valid_mask.astype(F32), (rows, LANES))
-    payload = jnp.concatenate([record, mask], axis=1)
     width = hop + LANES
-    blocks = [payload] + [lax.ppermute(payload, "tm", [(i, i ^ k) for i in range(segs)]) for k in range(1, segs)]
+    constants = [pltpu.with_memory_space_constraint(c, pltpu.HBM) for c in tables(2 * hop)]
+    hbm = pl.BlockSpec(memory_space=pltpu.HBM)
+    smem = pl.BlockSpec(memory_space=pltpu.SMEM)
+    payload, channels = pl.pallas_call(
+        join_kernel,
+        out_shape=(jax.ShapeDtypeStruct((rows, width), F32), jax.ShapeDtypeStruct((sources,), jnp.int32)),
+        in_specs=[hbm] * 3,
+        out_specs=tuple(vmem(2)),
+        scratch_shapes=[pltpu.VMEM((1, rows), jnp.int32), pltpu.SemaphoreType.DMA((3,))],
+        name="join",
+        **PARAMS,
+    )(
+        pltpu.with_memory_space_constraint(record, pltpu.HBM),
+        pltpu.with_memory_space_constraint(valid_mask.reshape(1, rows), pltpu.HBM),
+        pltpu.with_memory_space_constraint(source_channels, pltpu.HBM),
+    )
+    blocks = others(payload, segs)
 
     if groups <= sources and groups % segs == 0:
         per_group = sources // groups
@@ -291,11 +342,11 @@
         picked = pl.pallas_call(
             functools.partial(pick_kernel, per_group),
             out_shape=jax.ShapeDtypeStruct((segs * per_group, width), F32),
-            in_specs=[pl.BlockSpec(memory_space=pltpu.SMEM)] + vmem(segs),
+            in_specs=[smem] + vmem(segs),
             out_specs=pl.BlockSpec(memory_space=pltpu.VMEM),
             name="pick",
             **PARAMS,
-        )(source_channels, *blocks)
+        )(channels, *blocks)
         pay = []
         for j in range(parts):
             route = [
@@ -316,28 +367,30 @@
         pay = [whole.reshape(segs * mine, width)]
 
     count = segs * rows
-    spectrum, weights = pl.pallas_call(
+    spectrum, weights, *loaded = pl.pallas_call(
         functools.partial(receiver_kernel, segs),
         out_shape=(
             jax.ShapeDtypeStruct((PAIRS, count, 2 * LANES), F32),
             jax.ShapeDtypeStruct((count, LANES), F32),
+            *[jax.ShapeDtypeStruct(c.shape, c.dtype) for c in constants],
         ),
-        in_specs=vmem(segs + 4),
-        out_specs=tuple(vmem(2)),
+        in_specs=vmem(segs) + [hbm] * len(constants),
+        out_specs=tuple(vmem(2 + len(constants))),
         scratch_shapes=[
             pltpu.VMEM((count + rows, hop), F32),
             pltpu.VMEM((PAIRS, 2 * count, 2 * LANES), BF),
             pltpu.VMEM((PAIRS, count, 2 * LANES), F32),
+            pltpu.SemaphoreType.DMA((2 + 2 * PAIRS,)),
         ],
         name="receivers",
         **PARAMS,
-    )(*blocks, taper, inverse_counts, high_table, low_table)
+    )(*blocks, *constants)
 
     src_count = segs * mine
     return pl.pallas_call(
         functools.partial(stack_kernel, segs, parts),
         out_shape=jax.ShapeDtypeStruct((mine, rows, LAGS), F32),
-        in_specs=vmem(2 + parts + 6),
+        in_specs=vmem(2 + parts + 4),
         out_specs=pl.BlockSpec(memory_space=pltpu.VMEM),
         scratch_shapes=[
             pltpu.VMEM((src_count + mine, width), F32),
@@ -350,7 +403,7 @@
         ],
         name="stacks",
         **PARAMS,
-    )(spectrum, weights, *pay, taper, inverse_counts, high_table, low_table, high_lag, low_lag)
+    )(spectrum, weights, *pay, *loaded)
 
 
 def solution(mesh):

time: 24.7 us -> 20.5 us (0.83)
  local copies, waits for them, and re-layouts: 5.43 us -> 0 us
  Pallas kernels: 4.49 us -> 7.02 us
  starting transfers between devices: 8.68 us -> 10.8 us
  waiting for transfers between devices: 4.18 us -> 2.38 us
  other arithmetic: 1.52 us -> 0 us
    unnamed x18 -> x0, local copies, waits for them, and re-layouts: 5.35 us -> none
    ppermute x3, waiting for transfers between devices: 4.18 us -> 1.7 us  [others(): lax.ppermute(held[k], 'tm', [(i, i ^ bit) for i in range(segs)])]
    ppermute x3, starting transfers between devices: 2.87 us -> 4.63 us  [others(): lax.ppermute(held[k], 'tm', [(i, i ^ bit) for i in range(segs)])]
    pallas_call x1, Pallas kernels: 1.07 us -> 2.75 us  [local(): pl.pallas_call(functools.partial(receiver_kernel, segs), out_shape=(jax.S...]
    pallas_call x0 -> x1, Pallas kernels: none -> 0.86 us  [local(): pl.pallas_call(join_kernel, out_shape=(jax.ShapeDtypeStruct((rows, width)...]
    concatenate x1 -> x0, other arithmetic: 0.86 us -> none  [local(): payload = jnp.concatenate([record, mask], axis=1)]
    ppermute x2, waiting for transfers between devices: 0.01 us -> 0.68 us  [local(): pay.append(lax.ppermute(picked, ('recv', 'tm'), route))]
    broadcast_in_dim x1 -> x0, other arithmetic: 0.66 us -> none  [local(): mask = jnp.broadcast_to(valid_mask.astype(F32), (rows, LANES))]
  transfers between devices with their start and end apart: 5 -> 5, of which waited for: 2 -> 3; matrix products, arithmetic and copies ran while one was open for 0% -> 0% of each run, Pallas kernels for 4% -> 14%
where the time goes in v2:
time: 20.5 us; the launch traced here: 20.3 us
  starting transfers between devices  10.8 us (53%)
  Pallas kernels  7.02 us (34%)
  waiting for transfers between devices  2.38 us (12%)
    ppermute x2, starting transfers between devices, local(): pay.append(lax.ppermute(picked, ('recv', 'tm'), route))  6.21 us
    ppermute x3, starting transfers between devices, others(): lax.ppermute(held[k], 'tm', [(i, i ^ bit) for i in range(segs)])  4.63 us
    pallas_call x1, Pallas kernels, local(): pl.pallas_call(functools.partial(stack_kernel, segs, parts), out_shape=ja...  2.83 us
    pallas_call x1, Pallas kernels, local(): pl.pallas_call(functools.partial(receiver_kernel, segs), out_shape=(jax.S...  2.75 us
    ppermute x3, waiting for transfers between devices, others(): lax.ppermute(held[k], 'tm', [(i, i ^ bit) for i in range(segs)])  1.7 us
    pallas_call x1, Pallas kernels, local(): pl.pallas_call(join_kernel, out_shape=(jax.ShapeDtypeStruct((rows, width)...  0.86 us
    ppermute x2, waiting for transfers between devices, local(): pay.append(lax.ppermute(picked, ('recv', 'tm'), route))  0.68 us
    pallas_call x1, Pallas kernels, local(): pl.pallas_call(functools.partial(pick_kernel, per_group), out_shape=jax.S...  0.57 us
  transfers between devices with their start and end apart: 5, of which 3 were waited for; matrix products, arithmetic and copies ran while one was open for 0% of the time, Pallas kernels for 14%

profile of v2, /device:TPU:1, one launch (start us, length us, event | category | flops | bytes accessed | tf_op | source)
XLA Modules:
  0.0 20.3 jit_solution(13453292192965958170)
XLA Ops:
  0.0 0.9 %join.1 = (f32[16,1152]{1,0:T(8,128)S(1)}, s32[16]{0:T(128)S(1)}) custom-call(f32[16,1024]{1,0:T(8,128)} %record.1, s32[1,16]{1,0:T(1,128)} %bitcast.1, s32[16]{0:T(128)} %src.1), custom_call_target="tpu_custom_call" | custom-call | tf_op jit(solution)/shard_map/join/pallas_call | solution.py:324
  0.9 2.1 %collective-permute-start.1 = (f32[16,1152]{1,0:T(8,128)S(1)}, f32[16,1152]{1,0:T(8,128)S(1)}, u32[]{:S(2)}, u32[]{:S(2)}) collective-permute-start(f32[16,1152]{1,0:T(8,128)S(1)} %get-tuple-element.13.refs_0_), channel_id=1, source_target_pairs={{0,2},{1,3},{2,0},{3,1},{4,6},{5,7},{6,4},{7,5},{8,10},{9,11},{10,... | collective-permute-start | bytes 221192 | tf_op jit(solution)/shard_map/ppermute | solution.py:309
  3.0 1.0 %collective-permute-start = (f32[16,1152]{1,0:T(8,128)S(1)}, f32[16,1152]{1,0:T(8,128)S(1)}, u32[]{:S(2)}, u32[]{:S(2)}) collective-permute-start(f32[16,1152]{1,0:T(8,128)S(1)} %get-tuple-element.13.refs_0_), channel_id=1, source_target_pairs={{0,1},{1,0},{2,3},{3,2},{4,5},{5,4},{6,7},{7,6},{8,9},{9,8},{10,11... | collective-permute-start | bytes 221192 | tf_op jit(solution)/shard_map/ppermute | solution.py:309
  4.0 0.8 %collective-permute-done.1.refs_2_ = f32[16,1152]{1,0:T(8,128)S(1)} collective-permute-done((f32[16,1152]{1,0:T(8,128)S(1)}, f32[16,1152]{1,0:T(8,128)S(1)}, u32[]{:S(2)}, u32[]{:S(2)}) %collective-permute-start.1) | collective-permute-done | bytes 73760 | tf_op jit(solution)/shard_map/ppermute | solution.py:309
  4.8 1.5 %collective-permute-start.2 = (f32[16,1152]{1,0:T(8,128)S(1)}, f32[16,1152]{1,0:T(8,128)S(1)}, u32[]{:S(2)}, u32[]{:S(2)}) collective-permute-start(f32[16,1152]{1,0:T(8,128)S(1)} %collective-permute-done.1.refs_2_), channel_id=1, source_target_pairs={{0,1},{1,0},{2,3},{3,2},{4,5},{5,4},{6,7},{7,6},{8,9},{9,8},{10,11... | collective-permute-start | bytes 221192 | tf_op jit(solution)/shard_map/ppermute | solution.py:309
  6.3 0.0 collective-permute-done.refs_1_
  6.3 0.9 %collective-permute-done.2.refs_3_ = f32[16,1152]{1,0:T(8,128)S(1)} collective-permute-done((f32[16,1152]{1,0:T(8,128)S(1)}, f32[16,1152]{1,0:T(8,128)S(1)}, u32[]{:S(2)}, u32[]{:S(2)}) %collective-permute-start.2) | collective-permute-done | bytes 73760 | tf_op jit(solution)/shard_map/ppermute | solution.py:309
  7.2 0.6 %pick.1 = f32[8,1152]{1,0:T(8,128)S(1)} custom-call(s32[16]{0:T(128)S(1)} %get-tuple-element.16.src, f32[16,1152]{1,0:T(8,128)S(1)} %get-tuple-element.13.refs_0_, f32[16,1152]{1,0:T(8,128)S(1)} %collective-permute-done.refs_1_, f32[16,1152]{1,0:T(8,128)S(1)} %collective-permute-done.1.refs_2_, f32[16,1152]{1,0:T(8,128)S(1)} %collective-permute-done.2.refs_3_), custom_call_target="tpu_custom_call" | custom-call | tf_op jit(solution)/shard_map/pick/pallas_call | solution.py:342
  7.8 4.1 %collective-permute-start.3 = (f32[8,1152]{1,0:T(8,128)S(1)}, f32[8,1152]{1,0:T(8,128)S(1)}, u32[]{:S(2)}, u32[]{:S(2)}) collective-permute-start(f32[8,1152]{1,0:T(8,128)S(1)} %pick.1), channel_id=1, source_target_pairs={{2,0},{10,1},{18,2},{26,3},{6,4},{14,5},{22,6},{30,7},{3,8},{11,9}... | collective-permute-start | bytes 110600 | tf_op jit(solution)/shard_map/ppermute | solution.py:357
  11.9 2.1 %collective-permute-start.4 = (f32[8,1152]{1,0:T(8,128)S(1)}, f32[8,1152]{1,0:T(8,128)S(1)}, u32[]{:S(2)}, u32[]{:S(2)}) collective-permute-start(f32[8,1152]{1,0:T(8,128)S(1)} %pick.1), channel_id=1, source_target_pairs={{6,0},{14,1},{22,2},{30,3},{2,4},{10,5},{18,6},{26,7},{7,8},{15,9}... | collective-permute-start | bytes 110600 | tf_op jit(solution)/shard_map/ppermute | solution.py:357
  14.0 2.7 %receivers.1 = (f32[8,64,256]{2,1,0:T(8,128)S(1)}, f32[64,128]{1,0:T(8,128)S(1)}, f32[16,128]{1,0:T(8,128)S(1)}, f32[16,128]{1,0:T(8,128)S(1)}, bf16[2,8,256,256...) custom-call(f32[16,1152]{1,0:T(8,128)S(1)} %get-tuple-element.13.refs_0_, ...), custom_call_target="tpu_custom_call" | custom-call | tf_op jit(solution)/shard_map/receivers/pallas_call | solution.py:370
  16.8 0.0 collective-permute-done.3.refs_0_
  16.8 0.7 %collective-permute-done.4.refs_1_ = f32[8,1152]{1,0:T(8,128)S(1)} collective-permute-done((f32[8,1152]{1,0:T(8,128)S(1)}, f32[8,1152]{1,0:T(8,128)S(1)}, u32[]{:S(2)}, u32[]{:S(2)}) %collective-permute-start.4) | collective-permute-done | bytes 36896 | tf_op jit(solution)/shard_map/ppermute | solution.py:357
  17.4 2.8 %stacks.1 = f32[4,16,256]{2,1,0:T(8,128)} custom-call(f32[8,64,256]{2,1,0:T(8,128)S(1)} %get-tuple-element.14.spectrum, f32[64,128]{1,0:T(8,128)S(1)} %get-tuple-element.15.mask, f32[8,1152]{1,0:T(8,128)S(1)} %collective-permute-done.3.refs_0_, f32[8,1152]{1,0:T(8,128)S(1)} %collective-permute-done.4.refs_1_, f32[16,128]{1,0:T(8,128)S(1)} %get-tuple-element.17.refs_2_, ...), custom_call_target="tpu_custom_call" | custom-call | tf_op jit(solution)/shard_map/stacks/pallas_call | solution.py:390
Async XLA Ops:
  0.9 3.9 %collective-permute-start.1 = (f32[16,1152]{1,0:T(8,128)S(1)}, f32[16,1152]{1,0:T(8,128)S(1)}, u32[]{:S(2)}, u32[]{:S(2)}) collective-permute-start(f32[16,1152]{1,0:T(8,128)S(1)} %get-tuple-element.13.refs_0_), channel_id=1, source_target_pairs={{0,2},{1,3},{2,0},{3,1},{4,6},{5,7},{6,4},{7,5},{8,10},{9,11},{10,... | collective-permute-start | bytes 221192 | tf_op jit(solution)/shard_map/ppermute | solution.py:309
  3.0 3.3 %collective-permute-start = (f32[16,1152]{1,0:T(8,128)S(1)}, f32[16,1152]{1,0:T(8,128)S(1)}, u32[]{:S(2)}, u32[]{:S(2)}) collective-permute-start(f32[16,1152]{1,0:T(8,128)S(1)} %get-tuple-element.13.refs_0_), channel_id=1, source_target_pairs={{0,1},{1,0},{2,3},{3,2},{4,5},{5,4},{6,7},{7,6},{8,9},{9,8},{10,11... | collective-permute-start | bytes 221192 | tf_op jit(solution)/shard_map/ppermute | solution.py:309
  4.8 2.5 %collective-permute-start.2 = (f32[16,1152]{1,0:T(8,128)S(1)}, f32[16,1152]{1,0:T(8,128)S(1)}, u32[]{:S(2)}, u32[]{:S(2)}) collective-permute-start(f32[16,1152]{1,0:T(8,128)S(1)} %collective-permute-done.1.refs_2_), channel_id=1, source_target_pairs={{0,1},{1,0},{2,3},{3,2},{4,5},{5,4},{6,7},{7,6},{8,9},{9,8},{10,11... | collective-permute-start | bytes 221192 | tf_op jit(solution)/shard_map/ppermute | solution.py:309
  7.8 9.0 %collective-permute-start.3 = (f32[8,1152]{1,0:T(8,128)S(1)}, f32[8,1152]{1,0:T(8,128)S(1)}, u32[]{:S(2)}, u32[]{:S(2)}) collective-permute-start(f32[8,1152]{1,0:T(8,128)S(1)} %pick.1), channel_id=1, source_target_pairs={{2,0},{10,1},{18,2},{26,3},{6,4},{14,5},{22,6},{30,7},{3,8},{11,9}... | collective-permute-start | bytes 110600 | tf_op jit(solution)/shard_map/ppermute | solution.py:357
  11.9 5.5 %collective-permute-start.4 = (f32[8,1152]{1,0:T(8,128)S(1)}, f32[8,1152]{1,0:T(8,128)S(1)}, u32[]{:S(2)}, u32[]{:S(2)}) collective-permute-start(f32[8,1152]{1,0:T(8,128)S(1)} %pick.1), channel_id=1, source_target_pairs={{6,0},{14,1},{22,2},{30,3},{2,4},{10,5},{18,6},{26,7},{7,8},{15,9}... | collective-permute-start | bytes 110600 | tf_op jit(solution)/shard_map/ppermute | solution.py:357

commit v3 on v2

--- a/solution.py
+++ b/solution.py
@@ -180,32 +180,27 @@
         put(q, block * scale)
 
 
-def join_kernel(record, valid, src, out, src_out, row, sems):
+def join_kernel(per_group, record, valid, src, out, *refs):
+    *picked, row, channels, sems = refs
     rows, hop = record.shape
     copies = [
-        pltpu.make_async_copy(record, out.at[:, pl.ds(0, hop)], sems.at[0]),
+        pltpu.make_async_copy(src, channels, sems.at[0]),
         pltpu.make_async_copy(valid, row, sems.at[1]),
-        pltpu.make_async_copy(src, src_out, sems.at[2]),
+        pltpu.make_async_copy(record, out.at[:, pl.ds(0, hop)], sems.at[2]),
     ]
     for copy in copies:
         copy.start()
     copies[1].wait()
-    here = lax.broadcasted_iota(jnp.int32, (rows, rows), 0) == lax.broadcasted_iota(jnp.int32, (rows, rows), 1)
+    square = (rows, rows)
+    here = lax.broadcasted_iota(jnp.int32, square, 0) == lax.broadcasted_iota(jnp.int32, square, 1)
     column = jnp.sum(jnp.where(here, row[...].astype(F32), 0.0), axis=1, keepdims=True)
     out[:, hop:] = jnp.broadcast_to(column, (rows, LANES))
+    copies[0].wait()
     copies[2].wait()
-    copies[0].wait()
-
-
-def pick_kernel(per_group, src, *refs):
-    blocks, out = refs[:-1], refs[-1]
-    rows = blocks[0].shape[0]
-    group = lax.axis_index("recv")
-    me = lax.axis_index("tm")
+    first = lax.axis_index("recv")
     for i in range(per_group):
-        row = src[group * per_group + i] - group * rows
-        for k, block in enumerate(blocks):
-            out[pl.ds((me ^ k) * per_group + i, 1), :] = block[pl.ds(row, 1), :]
+        place = channels[first * per_group + i] - first * rows
+        picked[0][i : i + 1, :] = out[pl.ds(place, 1), :]
 
 
 def receiver_kernel(segs, *refs):
@@ -239,22 +234,25 @@
         copy.wait()
 
 
-def stack_kernel(segs, parts, spectrum, mask, *refs):
-    pay = refs[:parts]
-    taper, inverse_counts, table, lag, out = refs[parts : parts + 5]
-    xs, lhs, z, straight, crossed, prod_high, prod_low = refs[parts + 5 :]
+def stack_kernel(segs, hops, spectrum, mask, *refs):
+    pay = refs[: len(hops)]
+    taper, inverse_counts, table, lag, out = refs[len(hops) : len(hops) + 5]
+    xs, lhs, z, straight, crossed, prod_high, prod_low = refs[len(hops) + 5 :]
     hop = pay[0].shape[1] - LANES
     keep = LANES // 2
-    per_part = pay[0].shape[0] // segs
-    sources = per_part * parts
     rows = mask.shape[0] // segs
     group = lax.axis_index("recv")
-    for j, part in enumerate(pay):
-        slot = (group + j) % parts
-        for k in range(segs):
+    me = lax.axis_index("tm")
+    parts = 1 + max(turn for turn, _ in hops)
+    sources = sum(p.shape[0] for p in pay) // segs
+    per_part = sources // parts
+    for (turn, pair), part in zip(hops, pay, strict=True):
+        slot = (group + turn) % parts
+        sender = 0 if pair is None else holder(turn, pair, group // parts, me, segs)
+        for k in range(part.shape[0] // per_part):
             for i in range(per_part):
                 row = k * per_part + i
-                xs[pl.ds(k * sources + slot * per_part + i, 1), :] = part[row : row + 1, :]
+                xs[pl.ds((sender ^ k) * sources + slot * per_part + i, 1), :] = part[row : row + 1, :]
     xs[segs * sources :, :] = jnp.zeros((sources, hop + LANES), F32)
     count = segs * sources
     spectra(xs, count, sources, taper, table, lhs, z)
@@ -282,18 +280,31 @@
         part = dot(prod_high[p], lag[0, p]) + dot(prod_low[p], lag[0, p]) + dot(prod_high[p], lag[1, p])
         total = part if total is None else total + part
     scale = lax.rsqrt(jnp.mean(total * total, axis=1, keepdims=True) + 1e-6)
-    normed = total * scale
     for s in range(sources):
         stack = None
         for k in range(segs):
             i = k * sources + s
-            weight = mask[k * rows : (k + 1) * rows, :] * xs[i : i + 1, hop:]
-            weight = jnp.concatenate([weight] * (LAGS // LANES), axis=1)
-            term = weight * normed[i * rows : (i + 1) * rows, :]
+            weight = mask[k * rows : (k + 1) * rows, 0:1] * xs[i : i + 1, hop : hop + 1]
+            term = total[i * rows : (i + 1) * rows, :] * (weight * scale[i * rows : (i + 1) * rows, :])
             stack = term if stack is None else stack + term
         out[s] = stack
 
 
+def chosen(values, index):
+    if isinstance(index, int):
+        return values[index]
+    return sum(jnp.where(index == i, value, 0) for i, value in enumerate(values))
+
+
+def holder(turn, pair, place, me, segs):
+    if segs != 4 or turn > 1:
+        return place ^ (2 * pair)
+    base = ((2, 3, 2, 1), (3, 1, 1, 0))[turn]
+    flip = ((3, 2, 3, 3), (2, 3, 2, 2))[turn]
+    start = (place % 2) * 2 + place // 2 if turn else place
+    return start ^ chosen(base, me) ^ (chosen(flip, me) if pair else 0)
+
+
 def vmem(count):
     return [pl.BlockSpec(memory_space=pltpu.VMEM)] * count
 
@@ -301,14 +312,8 @@
 PARAMS = dict(compiler_params=pltpu.CompilerParams(vmem_limit_bytes=32 * 1024 * 1024))
 
 
-def others(value, segs):
-    held = {0: value}
-    bit = segs // 2
-    while bit:
-        for k in list(held):
-            held[k ^ bit] = lax.ppermute(held[k], "tm", [(i, i ^ bit) for i in range(segs)])
-        bit //= 2
-    return [held[k] for k in range(segs)]
+def other(value, segs, k):
+    return lax.ppermute(value, "tm", [(i, i ^ k) for i in range(segs)])
 
 
 def local(record, source_channels, valid_mask):
@@ -320,50 +325,41 @@
     width = hop + LANES
     constants = [pltpu.with_memory_space_constraint(c, pltpu.HBM) for c in tables(2 * hop)]
     hbm = pl.BlockSpec(memory_space=pltpu.HBM)
-    smem = pl.BlockSpec(memory_space=pltpu.SMEM)
-    payload, channels = pl.pallas_call(
-        join_kernel,
-        out_shape=(jax.ShapeDtypeStruct((rows, width), F32), jax.ShapeDtypeStruct((sources,), jnp.int32)),
+    fast = groups <= sources and groups % segs == 0
+    per_group = sources // groups if fast else 0
+    payload, *piece = pl.pallas_call(
+        functools.partial(join_kernel, per_group),
+        out_shape=tuple(jax.ShapeDtypeStruct((n, width), F32) for n in (rows, per_group) if n),
         in_specs=[hbm] * 3,
-        out_specs=tuple(vmem(2)),
-        scratch_shapes=[pltpu.VMEM((1, rows), jnp.int32), pltpu.SemaphoreType.DMA((3,))],
+        out_specs=tuple(vmem(2 if fast else 1)),
+        scratch_shapes=[
+            pltpu.VMEM((1, rows), jnp.int32),
+            pltpu.SMEM((sources,), jnp.int32),
+            pltpu.SemaphoreType.DMA((3,)),
+        ],
         name="join",
         **PARAMS,
-    )(
-        pltpu.with_memory_space_constraint(record, pltpu.HBM),
-        pltpu.with_memory_space_constraint(valid_mask.reshape(1, rows), pltpu.HBM),
-        pltpu.with_memory_space_constraint(source_channels, pltpu.HBM),
-    )
-    blocks = others(payload, segs)
-
-    if groups <= sources and groups % segs == 0:
-        per_group = sources // groups
+    )(*[pltpu.with_memory_space_constraint(a, pltpu.HBM) for a in (record, valid_mask.reshape(1, rows), source_channels)])
+    blocks = [payload] + [other(payload, segs, k) for k in range(1, segs)]
+    if fast:
         parts = groups // segs
-        picked = pl.pallas_call(
-            functools.partial(pick_kernel, per_group),
-            out_shape=jax.ShapeDtypeStruct((segs * per_group, width), F32),
-            in_specs=[smem] + vmem(segs),
-            out_specs=pl.BlockSpec(memory_space=pltpu.VMEM),
-            name="pick",
-            **PARAMS,
-        )(channels, *blocks)
+        picked = jnp.concatenate([piece[0], other(piece[0], segs, 1)], axis=0)
+        hops = [(turn, pair) for turn in reversed(range(parts)) for pair in range(segs // 2)]
         pay = []
-        for j in range(parts):
+        for turn, pair in hops:
             route = [
-                ((t * parts + (r + j) % parts) * segs + (r // parts + segs // 2) % segs, r * segs + t)
+                ((t * parts + (r + turn) % parts) * segs + holder(turn, pair, r // parts, t, segs), r * segs + t)
                 for r in range(groups)
                 for t in range(segs)
             ]
             pay.append(lax.ppermute(picked, ("recv", "tm"), route))
     else:
-        parts = 1
+        hops = [(0, None)]
         row = source_channels - lax.axis_index("recv") * rows
         here = (row >= 0) & (row < rows)
-        places = lax.axis_index("tm") ^ jnp.arange(segs)
-        held = jnp.stack(blocks)[places]
-        picked = jnp.where(here[None, :, None], held[:, jnp.clip(row, 0, rows - 1), :], 0.0)
-        whole = lax.psum(picked, "recv")
-        whole = lax.dynamic_slice_in_dim(whole, lax.axis_index("tm") * mine, mine, 1)
+        mine_now = jnp.where(here[:, None], payload[jnp.clip(row, 0, rows - 1)], 0.0)
+        whole = lax.psum(mine_now, "recv").reshape(segs, mine, width)
+        whole = lax.all_to_all(whole, "tm", 0, 0)
         pay = [whole.reshape(segs * mine, width)]
 
     count = segs * rows
@@ -388,9 +384,9 @@
 
     src_count = segs * mine
     return pl.pallas_call(
-        functools.partial(stack_kernel, segs, parts),
+        functools.partial(stack_kernel, segs, hops),
         out_shape=jax.ShapeDtypeStruct((mine, rows, LAGS), F32),
-        in_specs=vmem(2 + parts + 4),
+        in_specs=vmem(2 + len(pay) + 4),
         out_specs=pl.BlockSpec(memory_space=pltpu.VMEM),
         scratch_shapes=[
             pltpu.VMEM((src_count + mine, width), F32),

time: 20.5 us -> 17.3 us (0.84)
  the two profiles are of different devices: /device:TPU:1 before, /device:TPU:0 now
where the time goes in v3:
time: 17.3 us; the launch traced here: 17.1 us
  starting transfers between devices  10.4 us (60%)
  Pallas kernels  6.57 us (38%)
    ppermute x4, starting transfers between devices, local(): pay.append(lax.ppermute(picked, ('recv', 'tm'), route))  6.87 us
    ppermute x4, starting transfers between devices, other(): return lax.ppermute(value, 'tm', [(i, i ^ k) for i in range(segs)])  3.54 us
    pallas_call x1, Pallas kernels, local(): pl.pallas_call(functools.partial(stack_kernel, segs, hops), out_shape=jax...  2.94 us
    pallas_call x1, Pallas kernels, local(): pl.pallas_call(functools.partial(receiver_kernel, segs), out_shape=(jax.S...  2.75 us
    pallas_call x1, Pallas kernels, local(): pl.pallas_call(functools.partial(join_kernel, per_group), out_shape=tuple...  0.89 us
  transfers between devices with their start and end apart: 8, of which 0 were waited for; matrix products, arithmetic and copies ran while one was open for 0% of the time, Pallas kernels for 16%

profile of v3, /device:TPU:0, one launch (start us, length us, event | category | flops | bytes accessed | tf_op | source)
XLA Modules:
  0.0 17.1 jit_solution(17841115764063343853)
XLA Ops:
  0.0 0.9 %join.1 = (f32[16,1152]{1,0:T(8,128)S(1)}, f32[2,1152]{1,0:T(2,128)S(1)}) custom-call(f32[16,1024]{1,0:T(8,128)} %record.1, s32[1,16]{1,0:T(1,128)} %bitcast.1, s32[16]{0:T(128)} %src.1), custom_call_target="tpu_custom_call" | custom-call | tf_op jit(solution)/shard_map/join/pallas_call | solution.py:330
  0.9 0.5 %collective-permute-start.3 = (f32[2,1152]{1,0:T(2,128)S(1)}, f32[2,1152]{1,0:T(2,128)S(1)}, u32[]{:S(2)}, u32[]{:S(2)}) collective-permute-start(f32[2,1152]{1,0:T(2,128)S(1)} %get-tuple-element.16), channel_id=1, source_target_pairs={{0,1},{1,0},{2,3},{3,2},{4,5},{5,4},{6,7},{7,6},{8,9},{9,8},{10,11... | collective-permute-start | bytes 27656 | tf_op jit(solution)/shard_map/ppermute | solution.py:316
  1.4 0.1 collective-permute-start
  1.5 2.9 %collective-permute-start.1 = (f32[16,1152]{1,0:T(8,128)S(1)}, f32[16,1152]{1,0:T(8,128)S(1)}, u32[]{:S(2)}, u32[]{:S(2)}) collective-permute-start(f32[16,1152]{1,0:T(8,128)S(1)} %get-tuple-element.13.refs_0_), channel_id=1, source_target_pairs={{0,2},{1,3},{2,0},{3,1},{4,6},{5,7},{6,4},{7,5},{8,10},{9,11},{10,... | collective-permute-start | bytes 221192 | tf_op jit(solution)/shard_map/ppermute | solution.py:316
  4.4 0.0 collective-permute-start.2
  4.4 0.0 collective-permute-done.3
  4.5 4.6 %collective-permute-start.4 = (f32[4,1152]{1,0:T(4,128)S(1)}, f32[4,1152]{1,0:T(4,128)S(1)}, u32[]{:S(2)}, u32[]{:S(2)}) collective-permute-start(f32[4,1152]{1,0:T(4,128)S(1)} %pad_maximum_fusion), channel_id=1, source_target_pairs={{7,0},{13,1},{21,2},{28,3},{3,4},{9,5},{17,6},{24,7},{5,8},{15,9},... | collective-permute-start | bytes 55304 | tf_op jit(solution)/shard_map/ppermute | solution.py:355
  9.0 0.4 %collective-permute-start.5 = (f32[4,1152]{1,0:T(4,128)S(1)}, f32[4,1152]{1,0:T(4,128)S(1)}, u32[]{:S(2)}, u32[]{:S(2)}) collective-permute-start(f32[4,1152]{1,0:T(4,128)S(1)} %pad_maximum_fusion), channel_id=1, source_target_pairs={{5,0},{14,1},{23,2},{30,3},{1,4},{10,5},{19,6},{26,7},{7,8},{12,9}... | collective-permute-start | bytes 55304 | tf_op jit(solution)/shard_map/ppermute | solution.py:355
  9.4 0.0 collective-permute-done.refs_1_
  9.4 1.7 %collective-permute-start.6 = (f32[4,1152]{1,0:T(4,128)S(1)}, f32[4,1152]{1,0:T(4,128)S(1)}, u32[]{:S(2)}, u32[]{:S(2)}) collective-permute-start(f32[4,1152]{1,0:T(4,128)S(1)} %pad_maximum_fusion), channel_id=1, source_target_pairs={{2,0},{11,1},{18,2},{25,3},{6,4},{15,5},{22,6},{29,7},{3,8},{10,9}... | collective-permute-start | bytes 55304 | tf_op jit(solution)/shard_map/ppermute | solution.py:355
  11.1 0.0 collective-permute-done.1.refs_2_
  11.1 0.2 %collective-permute-start.7 = (f32[4,1152]{1,0:T(4,128)S(1)}, f32[4,1152]{1,0:T(4,128)S(1)}, u32[]{:S(2)}, u32[]{:S(2)}) collective-permute-start(f32[4,1152]{1,0:T(4,128)S(1)} %pad_maximum_fusion), channel_id=1, source_target_pairs={{1,0},{9,1},{17,2},{26,3},{5,4},{13,5},{21,6},{30,7},{0,8},{8,9},{... | collective-permute-start | bytes 55304 | tf_op jit(solution)/shard_map/ppermute | solution.py:355
  11.3 0.0 collective-permute-done.2.refs_3_
  11.3 2.7 %receivers.1 = (f32[8,64,256]{2,1,0:T(8,128)S(1)}, f32[64,128]{1,0:T(8,128)S(1)}, f32[16,128]{1,0:T(8,128)S(1)}, f32[16,128]{1,0:T(8,128)S(1)}, bf16[2,8,256,256...) custom-call(f32[16,1152]{1,0:T(8,128)S(1)} %get-tuple-element.13.refs_0_, ...), custom_call_target="tpu_custom_call" | custom-call | tf_op jit(solution)/shard_map/receivers/pallas_call | solution.py:366
  14.1 0.0 collective-permute-done.4.refs_0_
  14.1 0.0 collective-permute-done.5.refs_1_
  14.1 0.0 collective-permute-done.6.refs_2_
  14.1 0.0 collective-permute-done.7.refs_3_
  14.1 2.9 %stacks.1 = f32[4,16,256]{2,1,0:T(8,128)} custom-call(f32[8,64,256]{2,1,0:T(8,128)S(1)} %get-tuple-element.14.spectrum, f32[64,128]{1,0:T(8,128)S(1)} %get-tuple-element.15.mask, f32[4,1152]{1,0:T(4,128)S(1)} %collective-permute-done.4.refs_0_, f32[4,1152]{1,0:T(4,128)S(1)} %collective-permute-done.5.refs_1_, f32[4,1152]{1,0:T(4,128)S(1)} %collective-permute-done.6.refs_2_, ...), custom_call_target="tpu_custom_call" | custom-call | tf_op jit(solution)/shard_map/stacks/pallas_call | solution.py:386
  (1 shorter events, 0.0 us)
Async XLA Ops:
  0.9 3.5 %collective-permute-start.3 = (f32[2,1152]{1,0:T(2,128)S(1)}, f32[2,1152]{1,0:T(2,128)S(1)}, u32[]{:S(2)}, u32[]{:S(2)}) collective-permute-start(f32[2,1152]{1,0:T(2,128)S(1)} %get-tuple-element.16), channel_id=1, source_target_pairs={{0,1},{1,0},{2,3},{3,2},{4,5},{5,4},{6,7},{7,6},{8,9},{9,8},{10,11... | collective-permute-start | bytes 27656 | tf_op jit(solution)/shard_map/ppermute | solution.py:316
  1.4 8.0 %collective-permute-start = (f32[16,1152]{1,0:T(8,128)S(1)}, f32[16,1152]{1,0:T(8,128)S(1)}, u32[]{:S(2)}, u32[]{:S(2)}) collective-permute-start(f32[16,1152]{1,0:T(8,128)S(1)} %get-tuple-element.13.refs_0_), channel_id=1, source_target_pairs={{0,1},{1,0},{2,3},{3,2},{4,5},{5,4},{6,7},{7,6},{8,9},{9,8},{10,11... | collective-permute-start | bytes 221192 | tf_op jit(solution)/shard_map/ppermute | solution.py:316
  1.5 9.6 %collective-permute-start.1 = (f32[16,1152]{1,0:T(8,128)S(1)}, f32[16,1152]{1,0:T(8,128)S(1)}, u32[]{:S(2)}, u32[]{:S(2)}) collective-permute-start(f32[16,1152]{1,0:T(8,128)S(1)} %get-tuple-element.13.refs_0_), channel_id=1, source_target_pairs={{0,2},{1,3},{2,0},{3,1},{4,6},{5,7},{6,4},{7,5},{8,10},{9,11},{10,... | collective-permute-start | bytes 221192 | tf_op jit(solution)/shard_map/ppermute | solution.py:316
  4.4 6.9 %collective-permute-start.2 = (f32[16,1152]{1,0:T(8,128)S(1)}, f32[16,1152]{1,0:T(8,128)S(1)}, u32[]{:S(2)}, u32[]{:S(2)}) collective-permute-start(f32[16,1152]{1,0:T(8,128)S(1)} %get-tuple-element.13.refs_0_), channel_id=1, source_target_pairs={{0,3},{1,2},{2,1},{3,0},{4,7},{5,6},{6,5},{7,4},{8,11},{9,10},{10,... | collective-permute-start | bytes 221192 | tf_op jit(solution)/shard_map/ppermute | solution.py:316
  4.5 9.6 %collective-permute-start.4 = (f32[4,1152]{1,0:T(4,128)S(1)}, f32[4,1152]{1,0:T(4,128)S(1)}, u32[]{:S(2)}, u32[]{:S(2)}) collective-permute-start(f32[4,1152]{1,0:T(4,128)S(1)} %pad_maximum_fusion), channel_id=1, source_target_pairs={{7,0},{13,1},{21,2},{28,3},{3,4},{9,5},{17,6},{24,7},{5,8},{15,9},... | collective-permute-start | bytes 55304 | tf_op jit(solution)/shard_map/ppermute | solution.py:355
  9.0 5.1 %collective-permute-start.5 = (f32[4,1152]{1,0:T(4,128)S(1)}, f32[4,1152]{1,0:T(4,128)S(1)}, u32[]{:S(2)}, u32[]{:S(2)}) collective-permute-start(f32[4,1152]{1,0:T(4,128)S(1)} %pad_maximum_fusion), channel_id=1, source_target_pairs={{5,0},{14,1},{23,2},{30,3},{1,4},{10,5},{19,6},{26,7},{7,8},{12,9}... | collective-permute-start | bytes 55304 | tf_op jit(solution)/shard_map/ppermute | solution.py:355
  9.4 4.7 %collective-permute-start.6 = (f32[4,1152]{1,0:T(4,128)S(1)}, f32[4,1152]{1,0:T(4,128)S(1)}, u32[]{:S(2)}, u32[]{:S(2)}) collective-permute-start(f32[4,1152]{1,0:T(4,128)S(1)} %pad_maximum_fusion), channel_id=1, source_target_pairs={{2,0},{11,1},{18,2},{25,3},{6,4},{15,5},{22,6},{29,7},{3,8},{10,9}... | collective-permute-start | bytes 55304 | tf_op jit(solution)/shard_map/ppermute | solution.py:355
  11.1 3.0 %collective-permute-start.7 = (f32[4,1152]{1,0:T(4,128)S(1)}, f32[4,1152]{1,0:T(4,128)S(1)}, u32[]{:S(2)}, u32[]{:S(2)}) collective-permute-start(f32[4,1152]{1,0:T(4,128)S(1)} %pad_maximum_fusion), channel_id=1, source_target_pairs={{1,0},{9,1},{17,2},{26,3},{5,4},{13,5},{21,6},{30,7},{0,8},{8,9},{... | collective-permute-start | bytes 55304 | tf_op jit(solution)/shard_map/ppermute | solution.py:355

commit v4 on v3

v4 whole, which is shorter than its diff:
```python
import functools

import jax
import jax.numpy as jnp
import ml_dtypes
import numpy as np
from jax import lax
from jax.experimental import pallas as pl
from jax.experimental.pallas import tpu as pltpu
from jax.sharding import PartitionSpec as P

LANES = 128
LAGS = 256
SMOOTH = 64
RADIX = 16
PAIRS = RADIX // 2
ROUTES = ((16418906, 3916122, 644028, 12946108), (2217278, 9243262, 12455114, 7848848))
BF = jnp.bfloat16
F32 = jnp.float32


def order():
    return np.arange(PAIRS)[:, None] + PAIRS * np.arange(2)


def halves(table):
    high = table.astype(ml_dtypes.bfloat16)
    return np.stack([high, (table - high.astype(np.float64)).astype(ml_dtypes.bfloat16)])


@functools.cache
def tables(seglen):
    bins = seglen // 2
    keep = bins // RADIX
    samples = np.arange(seglen)
    taper = (0.5 - 0.5 * np.cos(2 * np.pi * samples / seglen)).reshape(RADIX, LANES)
    n2 = np.arange(LANES)[:, None]
    angle = 2 * np.pi * ((n2 * np.arange(keep)[None, :]) % LANES) / LANES
    cos, sin = np.cos(angle), np.sin(angle)
    step = np.concatenate(list(halves(np.block([[cos, -sin], [-sin, -cos]]))), axis=1)
    angle = 2 * np.pi * (np.arange(RADIX)[:, None] * n2.T) / seglen
    f = order()[:, :, None] + RADIX * np.arange(keep)
    counts = np.minimum(f + SMOOTH, bins - 1) - np.maximum(f - SMOOTH, 0) + 1
    inverse_counts = (1.0 / counts).reshape(PAIRS, LANES)
    f2 = np.arange(keep)[:, None]
    angle_low = 2 * np.pi * ((f2 * np.arange(LANES)) % LANES) / LANES
    lags = np.arange(LAGS) - LAGS // 2
    angle_high = 2 * np.pi * np.arange(RADIX)[:, None] * lags / seglen
    factor = 2.0 / seglen
    small = [
        taper,
        np.cos(angle),
        np.sin(angle),
        inverse_counts,
        np.cos(angle_low),
        np.sin(angle_low),
        factor * np.cos(angle_high).reshape(-1, LANES),
        factor * np.sin(angle_high).reshape(-1, LANES),
    ]
    return np.concatenate(small).astype(np.float32), step


def radix_step(x):
    r = float(np.sqrt(0.5))
    c1 = float(np.cos(np.pi / 8))
    c3 = float(np.cos(3 * np.pi / 8))
    c = [None] + [x[n] + x[16 - n] for n in range(1, 8)]
    s = [None] + [x[n] - x[16 - n] for n in range(1, 8)]
    e = [x[0] + x[8]] + [c[n] + c[8 - n] for n in range(1, 4)] + [c[4]]
    o = [x[0] - x[8]] + [c[n] - c[8 - n] for n in range(1, 4)]
    g = [None] + [s[n] - s[8 - n] for n in range(1, 4)]
    h = [None] + [s[n] + s[8 - n] for n in range(1, 4)] + [s[4]]
    e04 = e[0] + e[4]
    e04m = e[0] - e[4]
    e13 = e[1] + e[3]
    e13m = r * (e[1] - e[3])
    e042 = e04 + e[2]
    g13 = r * (g[1] + g[3])
    o2 = r * o[2]
    h2 = r * h[2]
    re = {
        0: e042 + e13,
        8: e042 - e13,
        4: e04 - e[2],
        2: e04m + e13m,
        6: e04m - e13m,
        1: (o[0] + o2) + (c1 * o[1] + c3 * o[3]),
        7: (o[0] + o2) - (c1 * o[1] + c3 * o[3]),
        3: (o[0] - o2) + (c3 * o[1] - c1 * o[3]),
        5: (o[0] - o2) - (c3 * o[1] - c1 * o[3]),
    }
    im = {
        2: g13 + g[2],
        4: g[1] - g[3],
        6: g13 - g[2],
        1: (h2 + h[4]) + (c3 * h[1] + c1 * h[3]),
        7: (c3 * h[1] + c1 * h[3]) - (h2 + h[4]),
        3: (h2 - h[4]) + (c1 * h[1] - c3 * h[3]),
        5: (c1 * h[1] - c3 * h[3]) - (h2 - h[4]),
    }
    return re, im


def split(value):
    high = value.astype(BF)
    return high, (value - high.astype(F32)).astype(BF)


def dot(a, b):
    return jnp.dot(a, b, preferred_element_type=F32)


def spectra(xs, count, shift, small, step_table, lhs, z):
    seglen = RADIX * LANES
    step = 16
    every = RADIX * count

    def group(first):
        x = [xs[first : first + step, n * LANES : (n + 1) * LANES] for n in range(PAIRS)]
        x += [xs[first + shift : first + shift + step, n * LANES : (n + 1) * LANES] for n in range(PAIRS)]
        total = x[0]
        for part in x[1:]:
            total = total + part
        mean = jnp.sum(total, axis=1, keepdims=True) * (1.0 / seglen)
        x = [(x[n] - mean) * small[n : n + 1, :] for n in range(RADIX)]
        re, im = radix_step(x)
        for p in range(PAIRS):
            for half in range(2):
                f1 = p + PAIRS * half
                cos, sin = small[RADIX + f1 : RADIX + f1 + 1, :], small[2 * RADIX + f1 : 2 * RADIX + f1 + 1, :]
                if f1 == 0:
                    parts = (re[0], jnp.zeros_like(re[0]))
                elif f1 == PAIRS:
                    parts = (re[f1] * cos, re[f1] * sin)
                elif f1 < PAIRS:
                    parts = (re[f1] * cos - im[f1] * sin, re[f1] * sin + im[f1] * cos)
                else:
                    a, b = re[RADIX - f1], im[RADIX - f1]
                    parts = (a * cos + b * sin, a * sin - b * cos)
                for i, part in enumerate(parts):
                    high, low = split(part)
                    cols = slice(i * LANES, (i + 1) * LANES)
                    at = f1 * count + first
                    lhs[at : at + step, cols] = high
                    lhs[every + at : every + at + step, cols] = low

    for first in range(0, count, step):
        group(first)
    both = dot(lhs[...], step_table[...])
    both = both[:, :LANES] + both[:, LANES:]
    z[...] = both[:every] + both[every:]


def whiten(z, count, first, small, put):
    keep = LANES // 2
    lane = lax.broadcasted_iota(jnp.int32, (8, LANES), 1)
    place = lane % keep
    upper = lane >= keep
    blocks = []
    for p in range(PAIRS):
        a = z[p * count + first : p * count + first + 8, :]
        b = z[(p + PAIRS) * count + first : (p + PAIRS) * count + first + 8, :]
        blocks.append((jnp.where(upper, pltpu.roll(b, keep, 1), a), jnp.where(upper, b, pltpu.roll(a, keep, 1))))
    power = [x * x + y * y for x, y in blocks]
    upto = [power[0]]
    for p in range(1, PAIRS):
        upto.append(upto[-1] + power[p])
    since = [power[PAIRS - 1]]
    for p in range(PAIRS - 2, -1, -1):
        since.append(since[-1] + power[p])
    since = since[::-1]
    turned = pltpu.roll(upto[-1], keep, 1)
    total = upto[-1] + turned
    below = jnp.where(upper, turned, 0.0)
    above = jnp.where(upper, 0.0, turned)

    def later(value, by):
        return jnp.where(place < keep - by, pltpu.roll(value, LANES - by, 1), 0.0)

    def earlier(value, by):
        return jnp.where(place >= by, pltpu.roll(value, by, 1), 0.0)

    reach = SMOOTH // RADIX
    inner = total
    for by in range(1, reach):
        inner = inner + (later(total, by) + earlier(total, by))
    for p, (x, y) in enumerate(blocks):
        window = inner + (earlier(since[p] + above, reach) + later(upto[p] + below, reach))
        scale = lax.rsqrt(window * small[3 * RADIX + p : 3 * RADIX + p + 1, :] + 1e-6)
        put(p, x * scale, y * scale)


def join_kernel(per_group, record, valid, src, constant, step_constant, out, small, step_table, *refs):
    *picked, row, channels, sems = refs
    rows, hop = record.shape
    copies = [
        pltpu.make_async_copy(src, channels, sems.at[0]),
        pltpu.make_async_copy(valid, row, sems.at[1]),
        pltpu.make_async_copy(record, out.at[:, pl.ds(0, hop)], sems.at[2]),
        pltpu.make_async_copy(constant, small, sems.at[3]),
        pltpu.make_async_copy(step_constant, step_table, sems.at[4]),
    ]
    for copy in copies:
        copy.start()
    copies[1].wait()
    square = (rows, rows)
    here = lax.broadcasted_iota(jnp.int32, square, 0) == lax.broadcasted_iota(jnp.int32, square, 1)
    column = jnp.sum(jnp.where(here, row[...].astype(F32), 0.0), axis=1, keepdims=True)
    out[:, hop:] = jnp.broadcast_to(column, (rows, LANES))
    copies[0].wait()
    copies[2].wait()
    first = lax.axis_index("recv")
    for i in range(per_group):
        place = channels[first * per_group + i] - first * rows
        picked[0][i : i + 1, :] = out[pl.ds(place, 1), :]
    copies[3].wait()
    copies[4].wait()


def lag_kernel(small, lag):
    keep = LANES // 2
    step = 16
    low = 3 * RADIX + PAIRS
    high = low + 2 * keep
    wide = LAGS // LANES
    first = lax.broadcasted_iota(jnp.int32, (step, LANES), 0) == 0
    for f1 in range(RADIX):
        for h in range(wide):
            at = high + f1 * wide + h
            cos_high = small[at : at + 1, :]
            sin_high = small[at + RADIX * wide : at + RADIX * wide + 1, :]
            for f2 in range(0, keep, step):
                cos_low = small[low + f2 : low + f2 + step, :]
                sin_low = small[low + keep + f2 : low + keep + f2 + step, :]
                cos = cos_high * cos_low - sin_high * sin_low
                sin = sin_high * cos_low + cos_high * sin_low
                if f1 == 0 and f2 == 0:
                    cos = jnp.where(first, 0.5 * cos, cos)
                    sin = jnp.where(first, 0.5 * sin, sin)
                for c, value in enumerate((cos, -sin)):
                    row = (2 * (f1 % PAIRS) + c) * LANES + (f1 // PAIRS) * keep + f2
                    for i, part in enumerate(split(value)):
                        lag[i, row : row + step, h * LANES : (h + 1) * LANES] = part


def receiver_kernel(segs, *refs):
    blocks = refs[:segs]
    small, step_table, out, mask, xs, lhs, z = refs[segs:]
    rows, width = blocks[0].shape
    hop = width - LANES
    me = lax.axis_index("tm")
    for k, block in enumerate(blocks):
        start = pl.multiple_of((me ^ k) * rows, rows)
        xs[pl.ds(start, rows), :] = block[:, :hop]
        mask[pl.ds(start, rows), :] = block[:, hop:]
    xs[segs * rows :, :] = jnp.zeros((rows, hop), F32)
    count = segs * rows

    spectra(xs, count, rows, small, step_table, lhs, z)
    for at in range(0, count, 8):

        def put(p, x, y):
            out[p, at : at + 8, :LANES] = x
            out[p, at : at + 8, LANES:] = y

        whiten(z, count, at, small, put)


def stack_kernel(segs, hops, spectrum, mask, *refs):
    count = max(hops, 1)
    pay = refs[:count]
    small, step_table, lag, out = refs[count : count + 4]
    xs, lhs, z, near, prod = refs[count + 4 :]
    hop = pay[0].shape[1] - LANES
    rows = mask.shape[0] // segs
    group = lax.axis_index("recv")
    me = lax.axis_index("tm")
    sources = sum(p.shape[0] for p in pay) // segs
    if hops:
        per_part = sources // 2
        for hop_no, part in enumerate(pay):
            side, sender = holder(hop_no, group // 2, group % 2, me, segs)
            for half in range(2):
                for k in range(2):
                    for i in range(per_part):
                        row = (2 * half + k) * per_part + i
                        at = (sender ^ k) * sources + (side ^ half) * per_part + i
                        xs[pl.ds(at, 1), :] = part[row : row + 1, :]
    else:
        xs[: segs * sources, :] = pay[0][...]
    xs[segs * sources :, :] = jnp.zeros((sources, hop + LANES), F32)
    count = segs * sources
    spectra(xs, count, sources, small, step_table, lhs, z)
    for first in range(0, count, 8):

        def put(p, x, y):
            near[p, first : first + 8, :LANES] = x
            near[p, first : first + 8, LANES:] = y

        whiten(z, count, first, small, put)
    size = count * rows
    for p in range(PAIRS):
        for k in range(segs):
            rx, ry = (spectrum[p, k * rows : (k + 1) * rows, c * LANES : (c + 1) * LANES] for c in range(2))
            for s in range(sources):
                i = k * sources + s
                sx, sy = (near[p, i : i + 1, c * LANES : (c + 1) * LANES] for c in range(2))
                for c, cross in enumerate((sx * rx + sy * ry, sx * ry - sy * rx)):
                    cols = slice((2 * p + c) * LANES, (2 * p + c + 1) * LANES)
                    high, low = split(cross)
                    prod[i * rows : (i + 1) * rows, cols] = high
                    prod[size + i * rows : size + (i + 1) * rows, cols] = low
    both = dot(prod[...], lag[0])
    total = both[:size] + both[size:] + dot(prod[:size, :], lag[1])
    scale = lax.rsqrt(jnp.mean(total * total, axis=1, keepdims=True) + 1e-6)
    for s in range(sources):
        stack = None
        for k in range(segs):
            i = k * sources + s
            weight = mask[k * rows : (k + 1) * rows, 0:1] * xs[i : i + 1, hop : hop + 1]
            term = total[i * rows : (i + 1) * rows, :] * (weight * scale[i * rows : (i + 1) * rows, :])
            stack = term if stack is None else stack + term
        out[s] = stack


def chosen(values, index):
    if isinstance(index, int):
        return values[index]
    return sum(jnp.where(index == i, value, 0) for i, value in enumerate(values))


def holder(hop, place, side, me, segs):
    packed = chosen(ROUTES[hop], me) >> (3 * (2 * place + side))
    return packed & 1, 2 * ((packed >> 2) & 1) + ((packed >> 1) & 1)


def vmem(count):
    return [pl.BlockSpec(memory_space=pltpu.VMEM)] * count


PARAMS = dict(compiler_params=pltpu.CompilerParams(vmem_limit_bytes=32 * 1024 * 1024))


def other(value, segs, k):
    return lax.ppermute(value, "tm", [(i, i ^ k) for i in range(segs)])


def local(record, source_channels, valid_mask):
    rows, hop = record.shape
    segs = lax.axis_size("tm")
    groups = lax.axis_size("recv")
    sources = source_channels.shape[0]
    mine = sources // segs
    width = hop + LANES
    constant, step_constant = [pltpu.with_memory_space_constraint(c, pltpu.HBM) for c in tables(2 * hop)]
    hbm = pl.BlockSpec(memory_space=pltpu.HBM)
    fast = segs == 4 and groups == 2 * segs and sources % groups == 0
    per_group = sources // groups if fast else 0
    payload, small, step_table, *piece = pl.pallas_call(
        functools.partial(join_kernel, per_group),
        out_shape=(
            jax.ShapeDtypeStruct((rows, width), F32),
            jax.ShapeDtypeStruct(constant.shape, F32),
            jax.ShapeDtypeStruct(step_constant.shape, BF),
            *[jax.ShapeDtypeStruct((per_group, width), F32)] * fast,
        ),
        in_specs=[hbm] * 5,
        out_specs=tuple(vmem(3 + fast)),
        scratch_shapes=[
            pltpu.VMEM((1, rows), jnp.int32),
            pltpu.SMEM((sources,), jnp.int32),
            pltpu.SemaphoreType.DMA((5,)),
        ],
        name="join",
        **PARAMS,
    )(*[pltpu.with_memory_space_constraint(a, pltpu.HBM) for a in (record, valid_mask.reshape(1, rows), source_channels)], constant, step_constant)
    lag = pl.pallas_call(
        lag_kernel,
        out_shape=jax.ShapeDtypeStruct((2, RADIX * LANES, LAGS), BF),
        in_specs=vmem(1),
        out_specs=pl.BlockSpec(memory_space=pltpu.VMEM),
        name="waves",
        **PARAMS,
    )(small)
    blocks = [payload] + [other(payload, segs, k) for k in range(1, segs)]
    if fast:
        hops = segs // 2
        neighbour, lag = lax.optimization_barrier((other(piece[0], segs, 1), lag))
        pair = jnp.concatenate([piece[0], neighbour], axis=0)
        beside = lax.ppermute(pair, "recv", [(r, r ^ 1) for r in range(groups)])
        picked = jnp.concatenate([pair, beside], axis=0)
        pay = []
        for hop_no in range(hops):
            route = []
            for r in range(groups):
                for t in range(segs):
                    side, sender = holder(hop_no, r // 2, r % 2, t, segs)
                    route.append(((2 * t + side) * segs + sender, r * segs + t))
            pay.append(lax.ppermute(picked, ("recv", "tm"), route))
    else:
        hops = 0
        row = source_channels - lax.axis_index("recv") * rows
        here = (row >= 0) & (row < rows)
        mine_now = jnp.where(here[:, None], payload[jnp.clip(row, 0, rows - 1)], 0.0)
        whole = lax.psum(mine_now, "recv").reshape(segs, mine, width)
        whole = lax.all_to_all(whole, "tm", 0, 0)
        pay = [whole.reshape(segs * mine, width)]

    count = segs * rows
    spectrum, weights = pl.pallas_call(
        functools.partial(receiver_kernel, segs),
        out_shape=(
            jax.ShapeDtypeStruct((PAIRS, count, 2 * LANES), F32),
            jax.ShapeDtypeStruct((count, LANES), F32),
        ),
        in_specs=vmem(segs + 2),
        out_specs=tuple(vmem(2)),
        scratch_shapes=[
            pltpu.VMEM((count + rows, hop), F32),
            pltpu.VMEM((2 * RADIX * count, 2 * LANES), BF),
            pltpu.VMEM((RADIX * count, LANES), F32),
        ],
        name="receivers",
        **PARAMS,
    )(*blocks, small, step_table)

    src_count = segs * mine
    return pl.pallas_call(
        functools.partial(stack_kernel, segs, hops),
        out_shape=jax.ShapeDtypeStruct((mine, rows, LAGS), F32),
        in_specs=vmem(5 + len(pay)),
        out_specs=pl.BlockSpec(memory_space=pltpu.VMEM),
        scratch_shapes=[
            pltpu.VMEM((src_count + mine, width), F32),
            pltpu.VMEM((2 * RADIX * src_count, 2 * LANES), BF),
            pltpu.VMEM((RADIX * src_count, LANES), F32),
            pltpu.VMEM((PAIRS, src_count, 2 * LANES), F32),
            pltpu.VMEM((2 * src_count * rows, RADIX * LANES), BF),
        ],
        name="stacks",
        **PARAMS,
    )(spectrum, weights, *pay, small, step_table, lag)


def solution(mesh):
    placed = (P("recv", "tm"), P(), P("recv", "tm"))
    return jax.shard_map(
        local, mesh=mesh, in_specs=placed, out_specs=P("tm", "recv", None), check_vma=False
    )
```

time: 17.3 us -> 16.4 us (0.948)
  Pallas kernels: 6.57 us -> 5.56 us
  waiting for transfers between devices: 0.02 us -> 0.71 us
  starting transfers between devices: 10.4 us -> 9.85 us
    ppermute x0 -> x1, starting transfers between devices: none -> 2.9 us  [local(): beside = lax.ppermute(pair, 'recv', [(r, r ^ 1) for r in range(groups)])]
    ppermute x4 -> x2, starting transfers between devices: 6.87 us -> 4.57 us  [local(): pay.append(lax.ppermute(picked, ('recv', 'tm'), route))]
    pallas_call x1, Pallas kernels: 2.75 us -> 1.16 us  [local(): pl.pallas_call(functools.partial(receiver_kernel, segs), out_shape=(jax.S...]
    ppermute x4, starting transfers between devices: 3.54 us -> 2.38 us  [other(): return lax.ppermute(value, 'tm', [(i, i ^ k) for i in range(segs)])]
    pallas_call x1 -> x2, Pallas kernels: 0.89 us -> 1.64 us  [the longest x1 1.06 us: local(): pl.pallas_call(functools.partial(join_kernel, per_group), out_shape=(jax....]
    ppermute x4, waiting for transfers between devices: 0.01 us -> 0.4 us  [other(): return lax.ppermute(value, 'tm', [(i, i ^ k) for i in range(segs)])]
    ppermute x4 -> x2, waiting for transfers between devices: 0.01 us -> 0.31 us  [local(): pay.append(lax.ppermute(picked, ('recv', 'tm'), route))]
    pallas_call x1, Pallas kernels: 2.94 us -> 2.76 us  [local(): pl.pallas_call(functools.partial(stack_kernel, segs, hops), out_shape=jax...]
  transfers between devices with their start and end apart: 8 -> 7, of which waited for: 0 -> 3; matrix products, arithmetic and copies ran while one was open for 0% -> 0% of each run, Pallas kernels for 16% -> 11%
where the time goes in v4:
time: 16.4 us; the launch traced here: 16.2 us
  starting transfers between devices  9.85 us (60%)
  Pallas kernels  5.56 us (34%)
  waiting for transfers between devices  0.71 us (4%)
    ppermute x2, starting transfers between devices, local(): pay.append(lax.ppermute(picked, ('recv', 'tm'), route))  4.57 us
    ppermute x1, starting transfers between devices, local(): beside = lax.ppermute(pair, 'recv', [(r, r ^ 1) for r in range(groups)])  2.9 us
    pallas_call x1, Pallas kernels, local(): pl.pallas_call(functools.partial(stack_kernel, segs, hops), out_shape=jax...  2.76 us
    ppermute x4, starting transfers between devices, other(): return lax.ppermute(value, 'tm', [(i, i ^ k) for i in range(segs)])  2.38 us
    pallas_call x1, Pallas kernels, local(): pl.pallas_call(functools.partial(receiver_kernel, segs), out_shape=(jax.S...  1.16 us
    pallas_call x1, Pallas kernels, local(): pl.pallas_call(functools.partial(join_kernel, per_group), out_shape=(jax....  1.06 us
    pallas_call x1, Pallas kernels, local(): pl.pallas_call(lag_kernel, out_shape=jax.ShapeDtypeStruct((2, RADIX * LAN...  0.58 us
    ppermute x4, waiting for transfers between devices, other(): return lax.ppermute(value, 'tm', [(i, i ^ k) for i in range(segs)])  0.4 us
  transfers between devices with their start and end apart: 7, of which 3 were waited for; matrix products, arithmetic and copies ran while one was open for 0% of the time, Pallas kernels for 11%

profile of v4, /device:TPU:0, one launch (start us, length us, event | category | flops | bytes accessed | tf_op | source)
XLA Modules:
  0.0 16.2 jit_solution(3256427406748179517)
XLA Ops:
  0.0 1.1 %join.1 = (f32[16,1152]{1,0:T(8,128)S(1)}, f32[248,128]{1,0:T(8,128)S(1)}, bf16[256,256]{1,0:T(8,128)(2,1)S(1)}, f32[2,1152]{1,0:T(2,128)S(1)}) custom-call(f32[16,1024]{1,0:T(8,128)} %record.1, s32[1,16]{1,0:T(1,128)} %bitcast.1, s32[16]{0:T(128)} %src.1, f32[248,128]{1,0:T(8,128)} %constant.5.clone, bf16[256,256]{1,0:T(8,128)(2,1)} %constant.6.clone.step_constant), custom_call_target="tpu_custom_call" | custom-call | tf_op jit(solution)/shard_map/join/pallas_call | solution.py:359
  1.1 0.5 %collective-permute-start.3 = (f32[2,1152]{1,0:T(2,128)S(1)}, f32[2,1152]{1,0:T(2,128)S(1)}, u32[]{:S(2)}, u32[]{:S(2)}) collective-permute-start(f32[2,1152]{1,0:T(2,128)S(1)} %get-tuple-element.18), channel_id=1, source_target_pairs={{0,1},{1,0},{2,3},{3,2},{4,5},{5,4},{6,7},{7,6},{8,9},{9,8},{10,11... | collective-permute-start | bytes 27656 | tf_op jit(solution)/shard_map/ppermute | solution.py:345
  1.6 0.6 %waves.1.refs_4_ = bf16[2,2048,256]{2,1,0:T(8,128)(2,1)S(1)} custom-call(f32[248,128]{1,0:T(8,128)S(1)} %get-tuple-element.14.refs_4_.small.refs_2_), custom_call_target="tpu_custom_call" | custom-call | tf_op jit(solution)/shard_map/waves/pallas_call | solution.py:377
  2.2 0.2 %collective-permute-done.3 = f32[2,1152]{1,0:T(2,128)S(1)} collective-permute-done((f32[2,1152]{1,0:T(2,128)S(1)}, f32[2,1152]{1,0:T(2,128)S(1)}, u32[]{:S(2)}, u32[]{:S(2)}) %collective-permute-start.3) | collective-permute-done | bytes 9248 | tf_op jit(solution)/shard_map/ppermute | solution.py:345
  2.4 2.9 %collective-permute-start.4 = (f32[4,1152]{1,0:T(4,128)S(1)}, f32[4,1152]{1,0:T(4,128)S(1)}, u32[]{:S(2)}, u32[]{:S(2)}) collective-permute-start(f32[4,1152]{1,0:T(4,128)S(1)} %pad_maximum_fusion.1), channel_id=1, source_target_pairs={{0,4},{4,0},{8,12},{12,8},{16,20},{20,16},{24,28},{28,24},{1,5},{5... | collective-permute-start | bytes 55304 | tf_op jit(solution)/shard_map/ppermute | solution.py:390
  5.3 1.0 %collective-permute-start.2 = (f32[16,1152]{1,0:T(8,128)S(1)}, f32[16,1152]{1,0:T(8,128)S(1)}, u32[]{:S(2)}, u32[]{:S(2)}) collective-permute-start(f32[16,1152]{1,0:T(8,128)S(1)} %get-tuple-element.13.refs_0_), channel_id=1, source_target_pairs={{0,3},{1,2},{2,1},{3,0},{4,7},{5,6},{6,5},{7,4},{8,11},{9,10},{10,... | collective-permute-start | bytes 221192 | tf_op jit(solution)/shard_map/ppermute | solution.py:345
  6.3 0.5 %collective-permute-start.1 = (f32[16,1152]{1,0:T(8,128)S(1)}, f32[16,1152]{1,0:T(8,128)S(1)}, u32[]{:S(2)}, u32[]{:S(2)}) collective-permute-start(f32[16,1152]{1,0:T(8,128)S(1)} %get-tuple-element.13.refs_0_), channel_id=1, source_target_pairs={{0,2},{1,3},{2,0},{3,1},{4,6},{5,7},{6,4},{7,5},{8,10},{9,11},{10,... | collective-permute-start | bytes 221192 | tf_op jit(solution)/shard_map/ppermute | solution.py:345
  6.9 0.3 %collective-permute-start = (f32[16,1152]{1,0:T(8,128)S(1)}, f32[16,1152]{1,0:T(8,128)S(1)}, u32[]{:S(2)}, u32[]{:S(2)}) collective-permute-start(f32[16,1152]{1,0:T(8,128)S(1)} %get-tuple-element.13.refs_0_), channel_id=1, source_target_pairs={{0,1},{1,0},{2,3},{3,2},{4,5},{5,4},{6,7},{7,6},{8,9},{9,8},{10,11... | collective-permute-start | bytes 221192 | tf_op jit(solution)/shard_map/ppermute | solution.py:345
  7.2 0.0 collective-permute-done.4
  7.2 4.1 %collective-permute-start.6 = (f32[8,1152]{1,0:T(8,128)S(1)}, f32[8,1152]{1,0:T(8,128)S(1)}, u32[]{:S(2)}, u32[]{:S(2)}) collective-permute-start(f32[8,1152]{1,0:T(8,128)S(1)} %pad_maximum_fusion), channel_id=1, source_target_pairs={{3,0},{11,1},{17,2},{24,3},{7,4},{15,5},{20,6},{25,7},{2,8},{12,9}... | collective-permute-start | bytes 110600 | tf_op jit(solution)/shard_map/ppermute | solution.py:399
  11.3 0.5 %collective-permute-start.5 = (f32[8,1152]{1,0:T(8,128)S(1)}, f32[8,1152]{1,0:T(8,128)S(1)}, u32[]{:S(2)}, u32[]{:S(2)}) collective-permute-start(f32[8,1152]{1,0:T(8,128)S(1)} %pad_maximum_fusion), channel_id=1, source_target_pairs={{1,0},{9,1},{18,2},{26,3},{5,4},{13,5},{23,6},{31,7},{4,8},{14,9},... | collective-permute-start | bytes 110600 | tf_op jit(solution)/shard_map/ppermute | solution.py:399
  11.8 0.0 collective-permute-done.2.refs_3_
  11.8 0.1 collective-permute-done.1.refs_2_
  11.9 0.0 collective-permute-done.refs_1_
  11.9 1.2 %receivers.1 = (f32[8,64,256]{2,1,0:T(8,128)S(1)}, f32[64,128]{1,0:T(8,128)S(1)}) custom-call(f32[16,1152]{1,0:T(8,128)S(1)} %get-tuple-element.13.refs_0_, f32[16,1152]{1,0:T(8,128)S(1)} %collective-permute-done.refs_1_, f32[16,1152]{1,0:T(8,128)S(1)} %collective-permute-done.1.refs_2_, f32[16,1152]{1,0:T(8,128)S(1)} %collective-permute-done.2.refs_3_, ...), custom_call_target="tpu_custom_call" | custom-call | tf_op jit(solution)/shard_map/receivers/pallas_call | solution.py:410
  13.1 0.0 collective-permute-done.6.refs_1_
  13.1 0.3 %collective-permute-done.5.refs_0_ = f32[8,1152]{1,0:T(8,128)S(1)} collective-permute-done((f32[8,1152]{1,0:T(8,128)S(1)}, f32[8,1152]{1,0:T(8,128)S(1)}, u32[]{:S(2)}, u32[]{:S(2)}) %collective-permute-start.5) | collective-permute-done | bytes 36896 | tf_op jit(solution)/shard_map/ppermute | solution.py:399
  13.4 2.8 %stacks.1 = f32[4,16,256]{2,1,0:T(8,128)} custom-call(f32[8,64,256]{2,1,0:T(8,128)S(1)} %get-tuple-element.16.spectrum, f32[64,128]{1,0:T(8,128)S(1)} %get-tuple-element.17.mask, f32[8,1152]{1,0:T(8,128)S(1)} %collective-permute-done.5.refs_0_, f32[8,1152]{1,0:T(8,128)S(1)} %collective-permute-done.6.refs_1_, ...), custom_call_target="tpu_custom_call" | custom-call | tf_op jit(solution)/shard_map/stacks/pallas_call | solution.py:428
  (2 shorter events, 0.0 us)
Async XLA Ops:
  1.1 1.3 %collective-permute-start.3 = (f32[2,1152]{1,0:T(2,128)S(1)}, f32[2,1152]{1,0:T(2,128)S(1)}, u32[]{:S(2)}, u32[]{:S(2)}) collective-permute-start(f32[2,1152]{1,0:T(2,128)S(1)} %get-tuple-element.18), channel_id=1, source_target_pairs={{0,1},{1,0},{2,3},{3,2},{4,5},{5,4},{6,7},{7,6},{8,9},{9,8},{10,11... | collective-permute-start | bytes 27656 | tf_op jit(solution)/shard_map/ppermute | solution.py:345
  2.4 4.8 %collective-permute-start.4 = (f32[4,1152]{1,0:T(4,128)S(1)}, f32[4,1152]{1,0:T(4,128)S(1)}, u32[]{:S(2)}, u32[]{:S(2)}) collective-permute-start(f32[4,1152]{1,0:T(4,128)S(1)} %pad_maximum_fusion.1), channel_id=1, source_target_pairs={{0,4},{4,0},{8,12},{12,8},{16,20},{20,16},{24,28},{28,24},{1,5},{5... | collective-permute-start | bytes 55304 | tf_op jit(solution)/shard_map/ppermute | solution.py:390
  5.3 6.5 %collective-permute-start.2 = (f32[16,1152]{1,0:T(8,128)S(1)}, f32[16,1152]{1,0:T(8,128)S(1)}, u32[]{:S(2)}, u32[]{:S(2)}) collective-permute-start(f32[16,1152]{1,0:T(8,128)S(1)} %get-tuple-element.13.refs_0_), channel_id=1, source_target_pairs={{0,3},{1,2},{2,1},{3,0},{4,7},{5,6},{6,5},{7,4},{8,11},{9,10},{10,... | collective-permute-start | bytes 221192 | tf_op jit(solution)/shard_map/ppermute | solution.py:345
  6.3 5.6 %collective-permute-start.1 = (f32[16,1152]{1,0:T(8,128)S(1)}, f32[16,1152]{1,0:T(8,128)S(1)}, u32[]{:S(2)}, u32[]{:S(2)}) collective-permute-start(f32[16,1152]{1,0:T(8,128)S(1)} %get-tuple-element.13.refs_0_), channel_id=1, source_target_pairs={{0,2},{1,3},{2,0},{3,1},{4,6},{5,7},{6,4},{7,5},{8,10},{9,11},{10,... | collective-permute-start | bytes 221192 | tf_op jit(solution)/shard_map/ppermute | solution.py:345
  6.9 5.1 %collective-permute-start = (f32[16,1152]{1,0:T(8,128)S(1)}, f32[16,1152]{1,0:T(8,128)S(1)}, u32[]{:S(2)}, u32[]{:S(2)}) collective-permute-start(f32[16,1152]{1,0:T(8,128)S(1)} %get-tuple-element.13.refs_0_), channel_id=1, source_target_pairs={{0,1},{1,0},{2,3},{3,2},{4,5},{5,4},{6,7},{7,6},{8,9},{9,8},{10,11... | collective-permute-start | bytes 221192 | tf_op jit(solution)/shard_map/ppermute | solution.py:345
  7.2 5.9 %collective-permute-start.6 = (f32[8,1152]{1,0:T(8,128)S(1)}, f32[8,1152]{1,0:T(8,128)S(1)}, u32[]{:S(2)}, u32[]{:S(2)}) collective-permute-start(f32[8,1152]{1,0:T(8,128)S(1)} %pad_maximum_fusion), channel_id=1, source_target_pairs={{3,0},{11,1},{17,2},{24,3},{7,4},{15,5},{20,6},{25,7},{2,8},{12,9}... | collective-permute-start | bytes 110600 | tf_op jit(solution)/shard_map/ppermute | solution.py:399
  11.3 2.1 %collective-permute-start.5 = (f32[8,1152]{1,0:T(8,128)S(1)}, f32[8,1152]{1,0:T(8,128)S(1)}, u32[]{:S(2)}, u32[]{:S(2)}) collective-permute-start(f32[8,1152]{1,0:T(8,128)S(1)} %pad_maximum_fusion), channel_id=1, source_target_pairs={{1,0},{9,1},{18,2},{26,3},{5,4},{13,5},{23,6},{31,7},{4,8},{14,9},... | collective-permute-start | bytes 110600 | tf_op jit(solution)/shard_map/ppermute | solution.py:399

commit v5 on v4

--- a/solution.py
+++ b/solution.py
@@ -14,7 +14,7 @@
 SMOOTH = 64
 RADIX = 16
 PAIRS = RADIX // 2
-ROUTES = ((16418906, 3916122, 644028, 12946108), (2217278, 9243262, 12455114, 7848848))
+ROUTES = ((16288538, 6472634, 2894654, 14524972), (2279102, 11640342, 15946392, 7032648))
 BF = jnp.bfloat16
 F32 = jnp.float32
 
@@ -151,15 +151,15 @@
     z[...] = both[:every] + both[every:]
 
 
-def whiten(z, count, first, small, put):
+def whiten(z, count, first, height, small, put):
     keep = LANES // 2
-    lane = lax.broadcasted_iota(jnp.int32, (8, LANES), 1)
+    lane = lax.broadcasted_iota(jnp.int32, (height, LANES), 1)
     place = lane % keep
     upper = lane >= keep
     blocks = []
     for p in range(PAIRS):
-        a = z[p * count + first : p * count + first + 8, :]
-        b = z[(p + PAIRS) * count + first : (p + PAIRS) * count + first + 8, :]
+        a = z[p * count + first : p * count + first + height, :]
+        b = z[(p + PAIRS) * count + first : (p + PAIRS) * count + first + height, :]
         blocks.append((jnp.where(upper, pltpu.roll(b, keep, 1), a), jnp.where(upper, b, pltpu.roll(a, keep, 1))))
     power = [x * x + y * y for x, y in blocks]
     upto = [power[0]]
@@ -169,23 +169,25 @@
     for p in range(PAIRS - 2, -1, -1):
         since.append(since[-1] + power[p])
     since = since[::-1]
-    turned = pltpu.roll(upto[-1], keep, 1)
-    total = upto[-1] + turned
-    below = jnp.where(upper, turned, 0.0)
-    above = jnp.where(upper, 0.0, turned)
-
-    def later(value, by):
-        return jnp.where(place < keep - by, pltpu.roll(value, LANES - by, 1), 0.0)
-
-    def earlier(value, by):
-        return jnp.where(place >= by, pltpu.roll(value, by, 1), 0.0)
-
+    half = upto[-1]
     reach = SMOOTH // RADIX
-    inner = total
+
+    def moved(value, by):
+        inside = (place < keep - by) if by > 0 else (place >= -by)
+        return jnp.where(inside, pltpu.roll(value, -by % LANES, 1), 0.0)
+
+    def across(by):
+        if by == 0:
+            return pltpu.roll(half, keep, 1)
+        inside = (place < keep - by) if by > 0 else (place >= -by)
+        return jnp.where(inside, pltpu.roll(half, (keep - by) % LANES, 1), 0.0)
+
+    inner = half + across(0)
     for by in range(1, reach):
-        inner = inner + (later(total, by) + earlier(total, by))
+        inner = inner + ((moved(half, by) + moved(half, -by)) + (across(by) + across(-by)))
+    inner = inner + (jnp.where(upper, across(reach), 0.0) + jnp.where(upper, 0.0, across(-reach)))
     for p, (x, y) in enumerate(blocks):
-        window = inner + (earlier(since[p] + above, reach) + later(upto[p] + below, reach))
+        window = inner + (moved(since[p], -reach) + moved(upto[p], reach))
         scale = lax.rsqrt(window * small[3 * RADIX + p : 3 * RADIX + p + 1, :] + 1e-6)
         put(p, x * scale, y * scale)
 
@@ -263,14 +265,14 @@
             out[p, at : at + 8, :LANES] = x
             out[p, at : at + 8, LANES:] = y
 
-        whiten(z, count, at, small, put)
+        whiten(z, count, at, 8, small, put)
 
 
 def stack_kernel(segs, hops, spectrum, mask, *refs):
     count = max(hops, 1)
     pay = refs[:count]
     small, step_table, lag, out = refs[count : count + 4]
-    xs, lhs, z, near, prod = refs[count + 4 :]
+    xs, lhs, z, near, *prod = refs[count + 4 :]
     hop = pay[0].shape[1] - LANES
     rows = mask.shape[0] // segs
     group = lax.axis_index("recv")
@@ -291,14 +293,14 @@
     xs[segs * sources :, :] = jnp.zeros((sources, hop + LANES), F32)
     count = segs * sources
     spectra(xs, count, sources, small, step_table, lhs, z)
-    for first in range(0, count, 8):
-
-        def put(p, x, y):
-            near[p, first : first + 8, :LANES] = x
-            near[p, first : first + 8, LANES:] = y
-
-        whiten(z, count, first, small, put)
+
+    def put(p, x, y):
+        near[p, :, :LANES] = x
+        near[p, :, LANES:] = y
+
+    whiten(z, count, 0, count, small, put)
     size = count * rows
+    total = None
     for p in range(PAIRS):
         for k in range(segs):
             rx, ry = (spectrum[p, k * rows : (k + 1) * rows, c * LANES : (c + 1) * LANES] for c in range(2))
@@ -306,12 +308,14 @@
                 i = k * sources + s
                 sx, sy = (near[p, i : i + 1, c * LANES : (c + 1) * LANES] for c in range(2))
                 for c, cross in enumerate((sx * rx + sy * ry, sx * ry - sy * rx)):
-                    cols = slice((2 * p + c) * LANES, (2 * p + c + 1) * LANES)
+                    cols = slice(c * LANES, (c + 1) * LANES)
                     high, low = split(cross)
-                    prod[i * rows : (i + 1) * rows, cols] = high
-                    prod[size + i * rows : size + (i + 1) * rows, cols] = low
-    both = dot(prod[...], lag[0])
-    total = both[:size] + both[size:] + dot(prod[:size, :], lag[1])
+                    prod[p][i * rows : (i + 1) * rows, cols] = high
+                    prod[p][size + i * rows : size + (i + 1) * rows, cols] = low
+        depth = slice(2 * p * LANES, (2 * p + 2) * LANES)
+        both = dot(prod[p][...], lag[0, depth, :])
+        part = both[:size] + both[size:] + dot(prod[p][:size, :], lag[1, depth, :])
+        total = part if total is None else total + part
     scale = lax.rsqrt(jnp.mean(total * total, axis=1, keepdims=True) + 1e-6)
     for s in range(sources):
         stack = None
@@ -385,10 +389,12 @@
     blocks = [payload] + [other(payload, segs, k) for k in range(1, segs)]
     if fast:
         hops = segs // 2
-        neighbour, lag = lax.optimization_barrier((other(piece[0], segs, 1), lag))
-        pair = jnp.concatenate([piece[0], neighbour], axis=0)
-        beside = lax.ppermute(pair, "recv", [(r, r ^ 1) for r in range(groups)])
-        picked = jnp.concatenate([pair, beside], axis=0)
+        pieces = [piece[0]]
+        for side, bit in ((0, 1), (1, 0), (1, 1)):
+            route = [(r * segs + t, (r ^ side) * segs + (t ^ bit)) for r in range(groups) for t in range(segs)]
+            pieces.append(lax.ppermute(piece[0], ("recv", "tm"), route))
+        pieces, lag = lax.optimization_barrier((pieces, lag))
+        picked = jnp.concatenate(pieces, axis=0)
         pay = []
         for hop_no in range(hops):
             route = []
@@ -435,7 +441,7 @@
             pltpu.VMEM((2 * RADIX * src_count, 2 * LANES), BF),
             pltpu.VMEM((RADIX * src_count, LANES), F32),
             pltpu.VMEM((PAIRS, src_count, 2 * LANES), F32),
-            pltpu.VMEM((2 * src_count * rows, RADIX * LANES), BF),
+            *[pltpu.VMEM((2 * src_count * rows, 2 * LANES), BF)] * PAIRS,
         ],
         name="stacks",
         **PARAMS,

time: 16.4 us -> 15.7 us (0.957)
  starting transfers between devices: 9.85 us -> 9.23 us
  Pallas kernels: 5.56 us -> 5.37 us
    ppermute x2, starting transfers between devices: 4.57 us -> 3.94 us  [local(): pay.append(lax.ppermute(picked, ('recv', 'tm'), route))]
    ppermute x4 -> x3, waiting for transfers between devices: 0.4 us -> 0.01 us  [other(): return lax.ppermute(value, 'tm', [(i, i ^ k) for i in range(segs)])]
    ppermute x2, waiting for transfers between devices: 0.31 us -> 0.56 us  [local(): pay.append(lax.ppermute(picked, ('recv', 'tm'), route))]
    ppermute x1 -> x3, starting transfers between devices: 2.9 us -> 3.12 us  [local(): pieces.append(lax.ppermute(piece[0], ('recv', 'tm'), route))]
    ppermute x1 -> x3, waiting for transfers between devices: 0.01 us -> 0.21 us  [local(): pieces.append(lax.ppermute(piece[0], ('recv', 'tm'), route))]
    ppermute x4 -> x3, starting transfers between devices: 2.38 us -> 2.17 us  [other(): return lax.ppermute(value, 'tm', [(i, i ^ k) for i in range(segs)])]
  transfers between devices with their start and end apart: 7 -> 8, of which waited for: 3 -> 3; matrix products, arithmetic and copies ran while one was open for 0% -> 0% of each run, Pallas kernels for 11% -> 11%
where the time goes in v5:
time: 15.7 us; the launch traced here: 15.5 us
  starting transfers between devices  9.23 us (59%)
  Pallas kernels  5.37 us (34%)
  waiting for transfers between devices  0.78 us (5%)
    ppermute x2, starting transfers between devices, local(): pay.append(lax.ppermute(picked, ('recv', 'tm'), route))  3.94 us
    ppermute x3, starting transfers between devices, local(): pieces.append(lax.ppermute(piece[0], ('recv', 'tm'), route))  3.12 us
    pallas_call x1, Pallas kernels, local(): pl.pallas_call(functools.partial(stack_kernel, segs, hops), out_shape=jax...  2.6 us
    ppermute x3, starting transfers between devices, other(): return lax.ppermute(value, 'tm', [(i, i ^ k) for i in range(segs)])  2.17 us
    pallas_call x1, Pallas kernels, local(): pl.pallas_call(functools.partial(receiver_kernel, segs), out_shape=(jax.S...  1.12 us
    pallas_call x1, Pallas kernels, local(): pl.pallas_call(functools.partial(join_kernel, per_group), out_shape=(jax....  1.06 us
    pallas_call x1, Pallas kernels, local(): pl.pallas_call(lag_kernel, out_shape=jax.ShapeDtypeStruct((2, RADIX * LAN...  0.58 us
    ppermute x2, waiting for transfers between devices, local(): pay.append(lax.ppermute(picked, ('recv', 'tm'), route))  0.56 us
  transfers between devices with their start and end apart: 8, of which 3 were waited for; matrix products, arithmetic and copies ran while one was open for 0% of the time, Pallas kernels for 11%

profile of v5, /device:TPU:0, one launch (start us, length us, event | category | flops | bytes accessed | tf_op | source)
XLA Modules:
  0.0 15.5 jit_solution(12165201274065347765)
XLA Ops:
  0.0 1.1 %join.1 = (f32[16,1152]{1,0:T(8,128)S(1)}, f32[248,128]{1,0:T(8,128)S(1)}, bf16[256,256]{1,0:T(8,128)(2,1)S(1)}, f32[2,1152]{1,0:T(2,128)S(1)}) custom-call(f32[16,1024]{1,0:T(8,128)} %record.1, s32[1,16]{1,0:T(1,128)} %bitcast.1, s32[16]{0:T(128)} %src.1, f32[248,128]{1,0:T(8,128)} %constant.5.clone, bf16[256,256]{1,0:T(8,128)(2,1)} %constant.6.clone.step_constant), custom_call_target="tpu_custom_call" | custom-call | tf_op jit(solution)/shard_map/join/pallas_call | solution.py:363
  1.1 2.4 %collective-permute-start.5 = (f32[2,1152]{1,0:T(2,128)S(1)}, f32[2,1152]{1,0:T(2,128)S(1)}, u32[]{:S(2)}, u32[]{:S(2)}) collective-permute-start(f32[2,1152]{1,0:T(2,128)S(1)} %get-tuple-element.22), channel_id=1, source_target_pairs={{0,5},{1,4},{2,7},{3,6},{4,1},{5,0},{6,3},{7,2},{8,13},{9,12},{10,... | collective-permute-start | bytes 27656 | tf_op jit(solution)/shard_map/ppermute | solution.py:395
  3.5 0.6 %collective-permute-start.4 = (f32[2,1152]{1,0:T(2,128)S(1)}, f32[2,1152]{1,0:T(2,128)S(1)}, u32[]{:S(2)}, u32[]{:S(2)}) collective-permute-start(f32[2,1152]{1,0:T(2,128)S(1)} %get-tuple-element.22), channel_id=1, source_target_pairs={{0,4},{1,5},{2,6},{3,7},{4,0},{5,1},{6,2},{7,3},{8,12},{9,13},{10,... | collective-permute-start | bytes 27656 | tf_op jit(solution)/shard_map/ppermute | solution.py:395
  4.2 0.0 collective-permute-start.3
  4.2 1.6 %collective-permute-start.2 = (f32[16,1152]{1,0:T(8,128)S(1)}, f32[16,1152]{1,0:T(8,128)S(1)}, u32[]{:S(2)}, u32[]{:S(2)}) collective-permute-start(f32[16,1152]{1,0:T(8,128)S(1)} %get-tuple-element.16.refs_0_), channel_id=1, source_target_pairs={{0,3},{1,2},{2,1},{3,0},{4,7},{5,6},{6,5},{7,4},{8,11},{9,10},{10,... | collective-permute-start | bytes 221192 | tf_op jit(solution)/shard_map/ppermute | solution.py:349
  5.8 0.5 %collective-permute-start.1 = (f32[16,1152]{1,0:T(8,128)S(1)}, f32[16,1152]{1,0:T(8,128)S(1)}, u32[]{:S(2)}, u32[]{:S(2)}) collective-permute-start(f32[16,1152]{1,0:T(8,128)S(1)} %get-tuple-element.16.refs_0_), channel_id=1, source_target_pairs={{0,2},{1,3},{2,0},{3,1},{4,6},{5,7},{6,4},{7,5},{8,10},{9,11},{10,... | collective-permute-start | bytes 221192 | tf_op jit(solution)/shard_map/ppermute | solution.py:349
  6.3 0.6 %waves.1.refs_4_ = bf16[2,2048,256]{2,1,0:T(8,128)(2,1)S(1)} custom-call(f32[248,128]{1,0:T(8,128)S(1)} %get-tuple-element.17.refs_4_.small.refs_2_), custom_call_target="tpu_custom_call" | custom-call | tf_op jit(solution)/shard_map/waves/pallas_call | solution.py:381
  6.9 0.0 collective-permute-done.5
  6.9 0.1 collective-permute-start
  7.0 0.2 %collective-permute-done.4 = f32[2,1152]{1,0:T(2,128)S(1)} collective-permute-done((f32[2,1152]{1,0:T(2,128)S(1)}, f32[2,1152]{1,0:T(2,128)S(1)}, u32[]{:S(2)}, u32[]{:S(2)}) %collective-permute-start.4) | collective-permute-done | bytes 9248 | tf_op jit(solution)/shard_map/ppermute | solution.py:395
  7.2 0.0 collective-permute-done.3
  7.2 3.7 %collective-permute-start.7 = (f32[8,1152]{1,0:T(8,128)S(1)}, f32[8,1152]{1,0:T(8,128)S(1)}, u32[]{:S(2)}, u32[]{:S(2)}) collective-permute-start(f32[8,1152]{1,0:T(8,128)S(1)} %pad_maximum_fusion), channel_id=1, source_target_pairs={{3,0},{11,1},{16,2},{24,3},{7,4},{9,5},{21,6},{28,7},{1,8},{8,9},{... | collective-permute-start | bytes 110600 | tf_op jit(solution)/shard_map/ppermute | solution.py:405
  10.9 0.3 %collective-permute-start.6 = (f32[8,1152]{1,0:T(8,128)S(1)}, f32[8,1152]{1,0:T(8,128)S(1)}, u32[]{:S(2)}, u32[]{:S(2)}) collective-permute-start(f32[8,1152]{1,0:T(8,128)S(1)} %pad_maximum_fusion), channel_id=1, source_target_pairs={{1,0},{9,1},{19,2},{26,3},{5,4},{15,5},{23,6},{30,7},{2,8},{11,9},... | collective-permute-start | bytes 110600 | tf_op jit(solution)/shard_map/ppermute | solution.py:405
  11.1 0.0 collective-permute-done.2.refs_3_
  11.2 0.0 collective-permute-done.1.refs_2_
  11.2 0.0 collective-permute-done.refs_1_
  11.2 1.1 %receivers.1 = (f32[8,64,256]{2,1,0:T(8,128)S(1)}, f32[64,128]{1,0:T(8,128)S(1)}) custom-call(f32[16,1152]{1,0:T(8,128)S(1)} %get-tuple-element.16.refs_0_, f32[16,1152]{1,0:T(8,128)S(1)} %collective-permute-done.refs_1_, f32[16,1152]{1,0:T(8,128)S(1)} %collective-permute-done.1.refs_2_, f32[16,1152]{1,0:T(8,128)S(1)} %collective-permute-done.2.refs_3_, ...), custom_call_target="tpu_custom_call" | custom-call | tf_op jit(solution)/shard_map/receivers/pallas_call | solution.py:416
  12.3 0.2 %collective-permute-done.7.refs_1_ = f32[8,1152]{1,0:T(8,128)S(1)} collective-permute-done((f32[8,1152]{1,0:T(8,128)S(1)}, f32[8,1152]{1,0:T(8,128)S(1)}, u32[]{:S(2)}, u32[]{:S(2)}) %collective-permute-start.7) | collective-permute-done | bytes 36896 | tf_op jit(solution)/shard_map/ppermute | solution.py:405
  12.5 0.3 %collective-permute-done.6.refs_0_ = f32[8,1152]{1,0:T(8,128)S(1)} collective-permute-done((f32[8,1152]{1,0:T(8,128)S(1)}, f32[8,1152]{1,0:T(8,128)S(1)}, u32[]{:S(2)}, u32[]{:S(2)}) %collective-permute-start.6) | collective-permute-done | bytes 36896 | tf_op jit(solution)/shard_map/ppermute | solution.py:405
  12.8 2.6 %stacks.1 = f32[4,16,256]{2,1,0:T(8,128)} custom-call(f32[8,64,256]{2,1,0:T(8,128)S(1)} %get-tuple-element.19.spectrum, f32[64,128]{1,0:T(8,128)S(1)} %get-tuple-element.20.mask, f32[8,1152]{1,0:T(8,128)S(1)} %collective-permute-done.6.refs_0_, f32[8,1152]{1,0:T(8,128)S(1)} %collective-permute-done.7.refs_1_, ...), custom_call_target="tpu_custom_call" | custom-call | tf_op jit(solution)/shard_map/stacks/pallas_call | solution.py:434
  (1 shorter events, 0.0 us)
Async XLA Ops:
  1.1 5.8 %collective-permute-start.5 = (f32[2,1152]{1,0:T(2,128)S(1)}, f32[2,1152]{1,0:T(2,128)S(1)}, u32[]{:S(2)}, u32[]{:S(2)}) collective-permute-start(f32[2,1152]{1,0:T(2,128)S(1)} %get-tuple-element.22), channel_id=1, source_target_pairs={{0,5},{1,4},{2,7},{3,6},{4,1},{5,0},{6,3},{7,2},{8,13},{9,12},{10,... | collective-permute-start | bytes 27656 | tf_op jit(solution)/shard_map/ppermute | solution.py:395
  3.5 3.7 %collective-permute-start.4 = (f32[2,1152]{1,0:T(2,128)S(1)}, f32[2,1152]{1,0:T(2,128)S(1)}, u32[]{:S(2)}, u32[]{:S(2)}) collective-permute-start(f32[2,1152]{1,0:T(2,128)S(1)} %get-tuple-element.22), channel_id=1, source_target_pairs={{0,4},{1,5},{2,6},{3,7},{4,0},{5,1},{6,2},{7,3},{8,12},{9,13},{10,... | collective-permute-start | bytes 27656 | tf_op jit(solution)/shard_map/ppermute | solution.py:395
  4.2 3.0 %collective-permute-start.3 = (f32[2,1152]{1,0:T(2,128)S(1)}, f32[2,1152]{1,0:T(2,128)S(1)}, u32[]{:S(2)}, u32[]{:S(2)}) collective-permute-start(f32[2,1152]{1,0:T(2,128)S(1)} %get-tuple-element.22), channel_id=1, source_target_pairs={{0,1},{1,0},{2,3},{3,2},{4,5},{5,4},{6,7},{7,6},{8,9},{9,8},{10,11... | collective-permute-start | bytes 27656 | tf_op jit(solution)/shard_map/ppermute | solution.py:395
  4.2 7.0 %collective-permute-start.2 = (f32[16,1152]{1,0:T(8,128)S(1)}, f32[16,1152]{1,0:T(8,128)S(1)}, u32[]{:S(2)}, u32[]{:S(2)}) collective-permute-start(f32[16,1152]{1,0:T(8,128)S(1)} %get-tuple-element.16.refs_0_), channel_id=1, source_target_pairs={{0,3},{1,2},{2,1},{3,0},{4,7},{5,6},{6,5},{7,4},{8,11},{9,10},{10,... | collective-permute-start | bytes 221192 | tf_op jit(solution)/shard_map/ppermute | solution.py:349
  5.8 5.4 %collective-permute-start.1 = (f32[16,1152]{1,0:T(8,128)S(1)}, f32[16,1152]{1,0:T(8,128)S(1)}, u32[]{:S(2)}, u32[]{:S(2)}) collective-permute-start(f32[16,1152]{1,0:T(8,128)S(1)} %get-tuple-element.16.refs_0_), channel_id=1, source_target_pairs={{0,2},{1,3},{2,0},{3,1},{4,6},{5,7},{6,4},{7,5},{8,10},{9,11},{10,... | collective-permute-start | bytes 221192 | tf_op jit(solution)/shard_map/ppermute | solution.py:349
  6.9 4.3 %collective-permute-start = (f32[16,1152]{1,0:T(8,128)S(1)}, f32[16,1152]{1,0:T(8,128)S(1)}, u32[]{:S(2)}, u32[]{:S(2)}) collective-permute-start(f32[16,1152]{1,0:T(8,128)S(1)} %get-tuple-element.16.refs_0_), channel_id=1, source_target_pairs={{0,1},{1,0},{2,3},{3,2},{4,5},{5,4},{6,7},{7,6},{8,9},{9,8},{10,11... | collective-permute-start | bytes 221192 | tf_op jit(solution)/shard_map/ppermute | solution.py:349
  7.2 5.3 %collective-permute-start.7 = (f32[8,1152]{1,0:T(8,128)S(1)}, f32[8,1152]{1,0:T(8,128)S(1)}, u32[]{:S(2)}, u32[]{:S(2)}) collective-permute-start(f32[8,1152]{1,0:T(8,128)S(1)} %pad_maximum_fusion), channel_id=1, source_target_pairs={{3,0},{11,1},{16,2},{24,3},{7,4},{9,5},{21,6},{28,7},{1,8},{8,9},{... | collective-permute-start | bytes 110600 | tf_op jit(solution)/shard_map/ppermute | solution.py:405
  10.9 2.0 %collective-permute-start.6 = (f32[8,1152]{1,0:T(8,128)S(1)}, f32[8,1152]{1,0:T(8,128)S(1)}, u32[]{:S(2)}, u32[]{:S(2)}) collective-permute-start(f32[8,1152]{1,0:T(8,128)S(1)} %pad_maximum_fusion), channel_id=1, source_target_pairs={{1,0},{9,1},{19,2},{26,3},{5,4},{15,5},{23,6},{30,7},{2,8},{11,9},... | collective-permute-start | bytes 110600 | tf_op jit(solution)/shard_map/ppermute | solution.py:405

commit v6 on v5

--- a/solution.py
+++ b/solution.py
@@ -14,7 +14,7 @@
 SMOOTH = 64
 RADIX = 16
 PAIRS = RADIX // 2
-ROUTES = ((16288538, 6472634, 2894654, 14524972), (2279102, 11640342, 15946392, 7032648))
+ROUTES = ((16288538, 2345882, 350014, 8161454), (2279102, 11637822, 11779208, 11256728))
 BF = jnp.bfloat16
 F32 = jnp.float32
 
@@ -47,17 +47,14 @@
     lags = np.arange(LAGS) - LAGS // 2
     angle_high = 2 * np.pi * np.arange(RADIX)[:, None] * lags / seglen
     factor = 2.0 / seglen
-    small = [
-        taper,
-        np.cos(angle),
-        np.sin(angle),
-        inverse_counts,
+    small = [taper, np.cos(angle), np.sin(angle), inverse_counts]
+    waves = [
         np.cos(angle_low),
         np.sin(angle_low),
         factor * np.cos(angle_high).reshape(-1, LANES),
         factor * np.sin(angle_high).reshape(-1, LANES),
     ]
-    return np.concatenate(small).astype(np.float32), step
+    return np.concatenate(small).astype(np.float32), step, np.concatenate(waves).astype(np.float32)
 
 
 def radix_step(x):
@@ -192,15 +189,14 @@
         put(p, x * scale, y * scale)
 
 
-def join_kernel(per_group, record, valid, src, constant, step_constant, out, small, step_table, *refs):
+def join_kernel(per_group, record, valid, src, constant, out, waves, *refs):
     *picked, row, channels, sems = refs
     rows, hop = record.shape
     copies = [
         pltpu.make_async_copy(src, channels, sems.at[0]),
         pltpu.make_async_copy(valid, row, sems.at[1]),
         pltpu.make_async_copy(record, out.at[:, pl.ds(0, hop)], sems.at[2]),
-        pltpu.make_async_copy(constant, small, sems.at[3]),
-        pltpu.make_async_copy(step_constant, step_table, sems.at[4]),
+        pltpu.make_async_copy(constant, waves, sems.at[3]),
     ]
     for copy in copies:
         copy.start()
@@ -216,24 +212,23 @@
         place = channels[first * per_group + i] - first * rows
         picked[0][i : i + 1, :] = out[pl.ds(place, 1), :]
     copies[3].wait()
-    copies[4].wait()
-
-
-def lag_kernel(small, lag):
+
+
+def lag_kernel(waves, lag):
     keep = LANES // 2
     step = 16
-    low = 3 * RADIX + PAIRS
-    high = low + 2 * keep
+    low = 0
+    high = 2 * keep
     wide = LAGS // LANES
     first = lax.broadcasted_iota(jnp.int32, (step, LANES), 0) == 0
     for f1 in range(RADIX):
         for h in range(wide):
             at = high + f1 * wide + h
-            cos_high = small[at : at + 1, :]
-            sin_high = small[at + RADIX * wide : at + RADIX * wide + 1, :]
+            cos_high = waves[at : at + 1, :]
+            sin_high = waves[at + RADIX * wide : at + RADIX * wide + 1, :]
             for f2 in range(0, keep, step):
-                cos_low = small[low + f2 : low + f2 + step, :]
-                sin_low = small[low + keep + f2 : low + keep + f2 + step, :]
+                cos_low = waves[low + f2 : low + f2 + step, :]
+                sin_low = waves[low + keep + f2 : low + keep + f2 + step, :]
                 cos = cos_high * cos_low - sin_high * sin_low
                 sin = sin_high * cos_low + cos_high * sin_low
                 if f1 == 0 and f2 == 0:
@@ -259,13 +254,13 @@
     count = segs * rows
 
     spectra(xs, count, rows, small, step_table, lhs, z)
-    for at in range(0, count, 8):
+    for at in range(0, count, 16):
 
         def put(p, x, y):
-            out[p, at : at + 8, :LANES] = x
-            out[p, at : at + 8, LANES:] = y
-
-        whiten(z, count, at, 8, small, put)
+            out[p, at : at + 16, :LANES] = x
+            out[p, at : at + 16, LANES:] = y
+
+        whiten(z, count, at, 16, small, put)
 
 
 def stack_kernel(segs, hops, spectrum, mask, *refs):
@@ -356,28 +351,28 @@
     sources = source_channels.shape[0]
     mine = sources // segs
     width = hop + LANES
-    constant, step_constant = [pltpu.with_memory_space_constraint(c, pltpu.HBM) for c in tables(2 * hop)]
+    small, step_table, constant = tables(2 * hop)
+    constant = pltpu.with_memory_space_constraint(constant, pltpu.HBM)
     hbm = pl.BlockSpec(memory_space=pltpu.HBM)
     fast = segs == 4 and groups == 2 * segs and sources % groups == 0
     per_group = sources // groups if fast else 0
-    payload, small, step_table, *piece = pl.pallas_call(
+    payload, waves, *piece = pl.pallas_call(
         functools.partial(join_kernel, per_group),
         out_shape=(
             jax.ShapeDtypeStruct((rows, width), F32),
             jax.ShapeDtypeStruct(constant.shape, F32),
-            jax.ShapeDtypeStruct(step_constant.shape, BF),
             *[jax.ShapeDtypeStruct((per_group, width), F32)] * fast,
         ),
-        in_specs=[hbm] * 5,
-        out_specs=tuple(vmem(3 + fast)),
+        in_specs=[hbm] * 4,
+        out_specs=tuple(vmem(2 + fast)),
         scratch_shapes=[
             pltpu.VMEM((1, rows), jnp.int32),
             pltpu.SMEM((sources,), jnp.int32),
-            pltpu.SemaphoreType.DMA((5,)),
+            pltpu.SemaphoreType.DMA((4,)),
         ],
         name="join",
         **PARAMS,
-    )(*[pltpu.with_memory_space_constraint(a, pltpu.HBM) for a in (record, valid_mask.reshape(1, rows), source_channels)], constant, step_constant)
+    )(*[pltpu.with_memory_space_constraint(a, pltpu.HBM) for a in (record, valid_mask.reshape(1, rows), source_channels)], constant)
     lag = pl.pallas_call(
         lag_kernel,
         out_shape=jax.ShapeDtypeStruct((2, RADIX * LANES, LAGS), BF),
@@ -385,7 +380,7 @@
         out_specs=pl.BlockSpec(memory_space=pltpu.VMEM),
         name="waves",
         **PARAMS,
-    )(small)
+    )(waves)
     blocks = [payload] + [other(payload, segs, k) for k in range(1, segs)]
     if fast:
         hops = segs // 2

time: 15.7 us -> 15.7 us (level)
  no operation moved by 1% of the time
where the time goes in v6:
time: 15.7 us; the launch traced here: 15.4 us
  starting transfers between devices  9.23 us (59%)
  Pallas kernels  5.31 us (34%)
  waiting for transfers between devices  0.77 us (5%)
    ppermute x2, starting transfers between devices, local(): pay.append(lax.ppermute(picked, ('recv', 'tm'), route))  3.94 us
    ppermute x3, starting transfers between devices, local(): pieces.append(lax.ppermute(piece[0], ('recv', 'tm'), route))  3.12 us
    pallas_call x1, Pallas kernels, local(): pl.pallas_call(functools.partial(stack_kernel, segs, hops), out_shape=jax...  2.6 us
    ppermute x3, starting transfers between devices, other(): return lax.ppermute(value, 'tm', [(i, i ^ k) for i in range(segs)])  2.17 us
    pallas_call x1, Pallas kernels, local(): pl.pallas_call(functools.partial(receiver_kernel, segs), out_shape=(jax.S...  1.11 us
    pallas_call x1, Pallas kernels, local(): pl.pallas_call(functools.partial(join_kernel, per_group), out_shape=(jax....  1.01 us
    pallas_call x1, Pallas kernels, local(): pl.pallas_call(lag_kernel, out_shape=jax.ShapeDtypeStruct((2, RADIX * LAN...  0.58 us
    ppermute x2, waiting for transfers between devices, local(): pay.append(lax.ppermute(picked, ('recv', 'tm'), route))  0.55 us
  transfers between devices with their start and end apart: 8, of which 3 were waited for; matrix products, arithmetic and copies ran while one was open for 0% of the time, Pallas kernels for 11%

profile of v6, /device:TPU:0, one launch (start us, length us, event | category | flops | bytes accessed | tf_op | source)
XLA Modules:
  0.0 15.4 jit_solution(17959317382400283518)
XLA Ops:
  0.0 0.0 copy-start
  0.0 0.0 copy-start.1
  0.0 1.0 %join.1 = (f32[16,1152]{1,0:T(8,128)S(1)}, f32[192,128]{1,0:T(8,128)S(1)}, f32[2,1152]{1,0:T(2,128)S(1)}) custom-call(f32[16,1024]{1,0:T(8,128)} %record.1, s32[1,16]{1,0:T(1,128)} %bitcast.1, s32[16]{0:T(128)} %src.1, f32[192,128]{1,0:T(8,128)} %constant.7.clone), custom_call_target="tpu_custom_call" | custom-call | tf_op jit(solution)/shard_map/join/pallas_call | solution.py:359
  1.0 2.4 %collective-permute-start.5 = (f32[2,1152]{1,0:T(2,128)S(1)}, f32[2,1152]{1,0:T(2,128)S(1)}, u32[]{:S(2)}, u32[]{:S(2)}) collective-permute-start(f32[2,1152]{1,0:T(2,128)S(1)} %get-tuple-element.20), channel_id=1, source_target_pairs={{0,5},{1,4},{2,7},{3,6},{4,1},{5,0},{6,3},{7,2},{8,13},{9,12},{10,... | collective-permute-start | bytes 27656 | tf_op jit(solution)/shard_map/ppermute | solution.py:390
  3.5 0.6 %collective-permute-start.4 = (f32[2,1152]{1,0:T(2,128)S(1)}, f32[2,1152]{1,0:T(2,128)S(1)}, u32[]{:S(2)}, u32[]{:S(2)}) collective-permute-start(f32[2,1152]{1,0:T(2,128)S(1)} %get-tuple-element.20), channel_id=1, source_target_pairs={{0,4},{1,5},{2,6},{3,7},{4,0},{5,1},{6,2},{7,3},{8,12},{9,13},{10,... | collective-permute-start | bytes 27656 | tf_op jit(solution)/shard_map/ppermute | solution.py:390
  4.1 0.0 collective-permute-start.3
  4.1 1.6 %collective-permute-start.2 = (f32[16,1152]{1,0:T(8,128)S(1)}, f32[16,1152]{1,0:T(8,128)S(1)}, u32[]{:S(2)}, u32[]{:S(2)}) collective-permute-start(f32[16,1152]{1,0:T(8,128)S(1)} %get-tuple-element.15.refs_0_), channel_id=1, source_target_pairs={{0,3},{1,2},{2,1},{3,0},{4,7},{5,6},{6,5},{7,4},{8,11},{9,10},{10,... | collective-permute-start | bytes 221192 | tf_op jit(solution)/shard_map/ppermute | solution.py:344
  5.7 0.5 %collective-permute-start.1 = (f32[16,1152]{1,0:T(8,128)S(1)}, f32[16,1152]{1,0:T(8,128)S(1)}, u32[]{:S(2)}, u32[]{:S(2)}) collective-permute-start(f32[16,1152]{1,0:T(8,128)S(1)} %get-tuple-element.15.refs_0_), channel_id=1, source_target_pairs={{0,2},{1,3},{2,0},{3,1},{4,6},{5,7},{6,4},{7,5},{8,10},{9,11},{10,... | collective-permute-start | bytes 221192 | tf_op jit(solution)/shard_map/ppermute | solution.py:344
  6.2 0.6 %waves.1.refs_4_ = bf16[2,2048,256]{2,1,0:T(8,128)(2,1)S(1)} custom-call(f32[192,128]{1,0:T(8,128)S(1)} %get-tuple-element.19.waves), custom_call_target="tpu_custom_call" | custom-call | tf_op jit(solution)/shard_map/waves/pallas_call | solution.py:376
  6.8 0.0 collective-permute-done.5
  6.8 0.1 collective-permute-start
  6.9 0.2 %collective-permute-done.4 = f32[2,1152]{1,0:T(2,128)S(1)} collective-permute-done((f32[2,1152]{1,0:T(2,128)S(1)}, f32[2,1152]{1,0:T(2,128)S(1)}, u32[]{:S(2)}, u32[]{:S(2)}) %collective-permute-start.4) | collective-permute-done | bytes 9248 | tf_op jit(solution)/shard_map/ppermute | solution.py:390
  7.1 0.0 collective-permute-done.3
  7.2 3.7 %collective-permute-start.7 = (f32[8,1152]{1,0:T(8,128)S(1)}, f32[8,1152]{1,0:T(8,128)S(1)}, u32[]{:S(2)}, u32[]{:S(2)}) collective-permute-start(f32[8,1152]{1,0:T(8,128)S(1)} %pad_maximum_fusion), channel_id=1, source_target_pairs={{3,0},{11,1},{16,2},{24,3},{7,4},{15,5},{20,6},{29,7},{1,8},{8,9},... | collective-permute-start | bytes 110600 | tf_op jit(solution)/shard_map/ppermute | solution.py:400
  10.8 0.3 %collective-permute-start.6 = (f32[8,1152]{1,0:T(8,128)S(1)}, f32[8,1152]{1,0:T(8,128)S(1)}, u32[]{:S(2)}, u32[]{:S(2)}) collective-permute-start(f32[8,1152]{1,0:T(8,128)S(1)} %pad_maximum_fusion), channel_id=1, source_target_pairs={{1,0},{9,1},{19,2},{27,3},{5,4},{13,5},{23,6},{30,7},{2,8},{11,9},... | collective-permute-start | bytes 110600 | tf_op jit(solution)/shard_map/ppermute | solution.py:400
  11.1 0.0 collective-permute-done.2.refs_3_
  11.1 0.0 collective-permute-done.1.refs_2_
  11.1 0.0 collective-permute-done.refs_1_
  11.1 0.0 copy-done
  11.1 0.0 copy-done.1
  11.1 1.1 %receivers.1 = (f32[8,64,256]{2,1,0:T(8,128)S(1)}, f32[64,128]{1,0:T(8,128)S(1)}) custom-call(f32[16,1152]{1,0:T(8,128)S(1)} %get-tuple-element.15.refs_0_, f32[16,1152]{1,0:T(8,128)S(1)} %collective-permute-done.refs_1_, f32[16,1152]{1,0:T(8,128)S(1)} %collective-permute-done.1.refs_2_, f32[16,1152]{1,0:T(8,128)S(1)} %collective-permute-done.2.refs_3_, ...), custom_call_target="tpu_custom_call" | custom-call | tf_op jit(solution)/shard_map/receivers/pallas_call | solution.py:411
  12.3 0.2 %collective-permute-done.7.refs_1_ = f32[8,1152]{1,0:T(8,128)S(1)} collective-permute-done((f32[8,1152]{1,0:T(8,128)S(1)}, f32[8,1152]{1,0:T(8,128)S(1)}, u32[]{:S(2)}, u32[]{:S(2)}) %collective-permute-start.7) | collective-permute-done | bytes 36896 | tf_op jit(solution)/shard_map/ppermute | solution.py:400
  12.5 0.3 %collective-permute-done.6.refs_0_ = f32[8,1152]{1,0:T(8,128)S(1)} collective-permute-done((f32[8,1152]{1,0:T(8,128)S(1)}, f32[8,1152]{1,0:T(8,128)S(1)}, u32[]{:S(2)}, u32[]{:S(2)}) %collective-permute-start.6) | collective-permute-done | bytes 36896 | tf_op jit(solution)/shard_map/ppermute | solution.py:400
  12.8 2.6 %stacks.1 = f32[4,16,256]{2,1,0:T(8,128)} custom-call(f32[8,64,256]{2,1,0:T(8,128)S(1)} %get-tuple-element.16.spectrum, f32[64,128]{1,0:T(8,128)S(1)} %get-tuple-element.17.mask, f32[8,1152]{1,0:T(8,128)S(1)} %collective-permute-done.6.refs_0_, f32[8,1152]{1,0:T(8,128)S(1)} %collective-permute-done.7.refs_1_, f32[56,128]{1,0:T(8,128)S(1)} %copy-done.1, ...), custom_call_target="tpu_custom_call" | custom-call | tf_op jit(solution)/shard_map/stacks/pallas_call | solution.py:429
  (1 shorter events, 0.0 us)
Async XLA Ops:
  0.0 11.1 %copy-start = (bf16[256,256]{1,0:T(8,128)(2,1)S(1)}, bf16[256,256]{1,0:T(8,128)(2,1)}, u32[]{:S(2)}) copy-start(bf16[256,256]{1,0:T(8,128)(2,1)} %constant.9.clone.refs_5_.refs_3_) | copy-start | bytes 393220
  0.0 11.1 %copy-start.1 = (f32[56,128]{1,0:T(8,128)S(1)}, f32[56,128]{1,0:T(8,128)}, u32[]{:S(2)}) copy-start(f32[56,128]{1,0:T(8,128)} %constant.8.clone.refs_4_.refs_2_) | copy-start | bytes 86020
  1.0 5.8 %collective-permute-start.5 = (f32[2,1152]{1,0:T(2,128)S(1)}, f32[2,1152]{1,0:T(2,128)S(1)}, u32[]{:S(2)}, u32[]{:S(2)}) collective-permute-start(f32[2,1152]{1,0:T(2,128)S(1)} %get-tuple-element.20), channel_id=1, source_target_pairs={{0,5},{1,4},{2,7},{3,6},{4,1},{5,0},{6,3},{7,2},{8,13},{9,12},{10,... | collective-permute-start | bytes 27656 | tf_op jit(solution)/shard_map/ppermute | solution.py:390
  3.5 3.7 %collective-permute-start.4 = (f32[2,1152]{1,0:T(2,128)S(1)}, f32[2,1152]{1,0:T(2,128)S(1)}, u32[]{:S(2)}, u32[]{:S(2)}) collective-permute-start(f32[2,1152]{1,0:T(2,128)S(1)} %get-tuple-element.20), channel_id=1, source_target_pairs={{0,4},{1,5},{2,6},{3,7},{4,0},{5,1},{6,2},{7,3},{8,12},{9,13},{10,... | collective-permute-start | bytes 27656 | tf_op jit(solution)/shard_map/ppermute | solution.py:390
  4.1 3.0 %collective-permute-start.3 = (f32[2,1152]{1,0:T(2,128)S(1)}, f32[2,1152]{1,0:T(2,128)S(1)}, u32[]{:S(2)}, u32[]{:S(2)}) collective-permute-start(f32[2,1152]{1,0:T(2,128)S(1)} %get-tuple-element.20), channel_id=1, source_target_pairs={{0,1},{1,0},{2,3},{3,2},{4,5},{5,4},{6,7},{7,6},{8,9},{9,8},{10,11... | collective-permute-start | bytes 27656 | tf_op jit(solution)/shard_map/ppermute | solution.py:390
  4.1 7.0 %collective-permute-start.2 = (f32[16,1152]{1,0:T(8,128)S(1)}, f32[16,1152]{1,0:T(8,128)S(1)}, u32[]{:S(2)}, u32[]{:S(2)}) collective-permute-start(f32[16,1152]{1,0:T(8,128)S(1)} %get-tuple-element.15.refs_0_), channel_id=1, source_target_pairs={{0,3},{1,2},{2,1},{3,0},{4,7},{5,6},{6,5},{7,4},{8,11},{9,10},{10,... | collective-permute-start | bytes 221192 | tf_op jit(solution)/shard_map/ppermute | solution.py:344
  5.7 5.4 %collective-permute-start.1 = (f32[16,1152]{1,0:T(8,128)S(1)}, f32[16,1152]{1,0:T(8,128)S(1)}, u32[]{:S(2)}, u32[]{:S(2)}) collective-permute-start(f32[16,1152]{1,0:T(8,128)S(1)} %get-tuple-element.15.refs_0_), channel_id=1, source_target_pairs={{0,2},{1,3},{2,0},{3,1},{4,6},{5,7},{6,4},{7,5},{8,10},{9,11},{10,... | collective-permute-start | bytes 221192 | tf_op jit(solution)/shard_map/ppermute | solution.py:344
  6.8 4.3 %collective-permute-start = (f32[16,1152]{1,0:T(8,128)S(1)}, f32[16,1152]{1,0:T(8,128)S(1)}, u32[]{:S(2)}, u32[]{:S(2)}) collective-permute-start(f32[16,1152]{1,0:T(8,128)S(1)} %get-tuple-element.15.refs_0_), channel_id=1, source_target_pairs={{0,1},{1,0},{2,3},{3,2},{4,5},{5,4},{6,7},{7,6},{8,9},{9,8},{10,11... | collective-permute-start | bytes 221192 | tf_op jit(solution)/shard_map/ppermute | solution.py:344
  7.2 5.3 %collective-permute-start.7 = (f32[8,1152]{1,0:T(8,128)S(1)}, f32[8,1152]{1,0:T(8,128)S(1)}, u32[]{:S(2)}, u32[]{:S(2)}) collective-permute-start(f32[8,1152]{1,0:T(8,128)S(1)} %pad_maximum_fusion), channel_id=1, source_target_pairs={{3,0},{11,1},{16,2},{24,3},{7,4},{15,5},{20,6},{29,7},{1,8},{8,9},... | collective-permute-start | bytes 110600 | tf_op jit(solution)/shard_map/ppermute | solution.py:400
  10.8 2.0 %collective-permute-start.6 = (f32[8,1152]{1,0:T(8,128)S(1)}, f32[8,1152]{1,0:T(8,128)S(1)}, u32[]{:S(2)}, u32[]{:S(2)}) collective-permute-start(f32[8,1152]{1,0:T(8,128)S(1)} %pad_maximum_fusion), channel_id=1, source_target_pairs={{1,0},{9,1},{19,2},{27,3},{5,4},{13,5},{23,6},{30,7},{2,8},{11,9},... | collective-permute-start | bytes 110600 | tf_op jit(solution)/shard_map/ppermute | solution.py:400

commit v7 on v5

--- a/solution.py
+++ b/solution.py
@@ -214,7 +214,8 @@
     first = lax.axis_index("recv")
     for i in range(per_group):
         place = channels[first * per_group + i] - first * rows
-        picked[0][i : i + 1, :] = out[pl.ds(place, 1), :]
+        wanted = lax.broadcasted_iota(jnp.int32, out.shape, 0) == place
+        picked[0][i : i + 1, :] = jnp.sum(jnp.where(wanted, out[...], 0.0), axis=0, keepdims=True)
     copies[3].wait()
     copies[4].wait()
 
@@ -290,7 +291,7 @@
                         xs[pl.ds(at, 1), :] = part[row : row + 1, :]
     else:
         xs[: segs * sources, :] = pay[0][...]
-    xs[segs * sources :, :] = jnp.zeros((sources, hop + LANES), F32)
+    xs[segs * sources :, :] = jnp.zeros((xs.shape[0] - segs * sources, hop + LANES), F32)
     count = segs * sources
     spectra(xs, count, sources, small, step_table, lhs, z)
 
@@ -437,7 +438,7 @@
         in_specs=vmem(5 + len(pay)),
         out_specs=pl.BlockSpec(memory_space=pltpu.VMEM),
         scratch_shapes=[
-            pltpu.VMEM((src_count + mine, width), F32),
+            pltpu.VMEM((8 * pl.cdiv(src_count + mine, 8) + 8, width), F32),
             pltpu.VMEM((2 * RADIX * src_count, 2 * LANES), BF),
             pltpu.VMEM((RADIX * src_count, LANES), F32),
             pltpu.VMEM((PAIRS, src_count, 2 * LANES), F32),

time: 15.7 us -> 15.7 us (level)
  no operation moved by 1% of the time
where the time goes in v7:
time: 15.7 us; the launch traced here: 15.5 us
  starting transfers between devices  9.23 us (59%)
  Pallas kernels  5.38 us (34%)
  waiting for transfers between devices  0.78 us (5%)
    ppermute x2, starting transfers between devices, local(): pay.append(lax.ppermute(picked, ('recv', 'tm'), route))  3.94 us
    ppermute x3, starting transfers between devices, local(): pieces.append(lax.ppermute(piece[0], ('recv', 'tm'), route))  3.12 us
    pallas_call x1, Pallas kernels, local(): pl.pallas_call(functools.partial(stack_kernel, segs, hops), out_shape=jax...  2.62 us
    ppermute x3, starting transfers between devices, other(): return lax.ppermute(value, 'tm', [(i, i ^ k) for i in range(segs)])  2.17 us
    pallas_call x1, Pallas kernels, local(): pl.pallas_call(functools.partial(receiver_kernel, segs), out_shape=(jax.S...  1.12 us
    pallas_call x1, Pallas kernels, local(): pl.pallas_call(functools.partial(join_kernel, per_group), out_shape=(jax....  1.06 us
    pallas_call x1, Pallas kernels, local(): pl.pallas_call(lag_kernel, out_shape=jax.ShapeDtypeStruct((2, RADIX * LAN...  0.58 us
    ppermute x2, waiting for transfers between devices, local(): pay.append(lax.ppermute(picked, ('recv', 'tm'), route))  0.56 us
  transfers between devices with their start and end apart: 8, of which 3 were waited for; matrix products, arithmetic and copies ran while one was open for 0% of the time, Pallas kernels for 11%

profile of v7, /device:TPU:0, one launch (start us, length us, event | category | flops | bytes accessed | tf_op | source)
XLA Modules:
  0.0 15.5 jit_solution(17033282901721276751)
XLA Ops:
  0.0 1.1 %join.1 = (f32[16,1152]{1,0:T(8,128)S(1)}, f32[248,128]{1,0:T(8,128)S(1)}, bf16[256,256]{1,0:T(8,128)(2,1)S(1)}, f32[2,1152]{1,0:T(2,128)S(1)}) custom-call(f32[16,1024]{1,0:T(8,128)} %record.1, s32[1,16]{1,0:T(1,128)} %bitcast.1, s32[16]{0:T(128)} %src.1, f32[248,128]{1,0:T(8,128)} %constant.5.clone, bf16[256,256]{1,0:T(8,128)(2,1)} %constant.6.clone.step_constant), custom_call_target="tpu_custom_call" | custom-call | tf_op jit(solution)/shard_map/join/pallas_call | solution.py:364
  1.1 2.4 %collective-permute-start.5 = (f32[2,1152]{1,0:T(2,128)S(1)}, f32[2,1152]{1,0:T(2,128)S(1)}, u32[]{:S(2)}, u32[]{:S(2)}) collective-permute-start(f32[2,1152]{1,0:T(2,128)S(1)} %get-tuple-element.22), channel_id=1, source_target_pairs={{0,5},{1,4},{2,7},{3,6},{4,1},{5,0},{6,3},{7,2},{8,13},{9,12},{10,... | collective-permute-start | bytes 27656 | tf_op jit(solution)/shard_map/ppermute | solution.py:396
  3.5 0.6 %collective-permute-start.4 = (f32[2,1152]{1,0:T(2,128)S(1)}, f32[2,1152]{1,0:T(2,128)S(1)}, u32[]{:S(2)}, u32[]{:S(2)}) collective-permute-start(f32[2,1152]{1,0:T(2,128)S(1)} %get-tuple-element.22), channel_id=1, source_target_pairs={{0,4},{1,5},{2,6},{3,7},{4,0},{5,1},{6,2},{7,3},{8,12},{9,13},{10,... | collective-permute-start | bytes 27656 | tf_op jit(solution)/shard_map/ppermute | solution.py:396
  4.2 0.0 collective-permute-start.3
  4.2 1.6 %collective-permute-start.2 = (f32[16,1152]{1,0:T(8,128)S(1)}, f32[16,1152]{1,0:T(8,128)S(1)}, u32[]{:S(2)}, u32[]{:S(2)}) collective-permute-start(f32[16,1152]{1,0:T(8,128)S(1)} %get-tuple-element.16.refs_0_), channel_id=1, source_target_pairs={{0,3},{1,2},{2,1},{3,0},{4,7},{5,6},{6,5},{7,4},{8,11},{9,10},{10,... | collective-permute-start | bytes 221192 | tf_op jit(solution)/shard_map/ppermute | solution.py:350
  5.8 0.5 %collective-permute-start.1 = (f32[16,1152]{1,0:T(8,128)S(1)}, f32[16,1152]{1,0:T(8,128)S(1)}, u32[]{:S(2)}, u32[]{:S(2)}) collective-permute-start(f32[16,1152]{1,0:T(8,128)S(1)} %get-tuple-element.16.refs_0_), channel_id=1, source_target_pairs={{0,2},{1,3},{2,0},{3,1},{4,6},{5,7},{6,4},{7,5},{8,10},{9,11},{10,... | collective-permute-start | bytes 221192 | tf_op jit(solution)/shard_map/ppermute | solution.py:350
  6.3 0.6 %waves.1.refs_4_ = bf16[2,2048,256]{2,1,0:T(8,128)(2,1)S(1)} custom-call(f32[248,128]{1,0:T(8,128)S(1)} %get-tuple-element.17.refs_4_.small.refs_2_), custom_call_target="tpu_custom_call" | custom-call | tf_op jit(solution)/shard_map/waves/pallas_call | solution.py:382
  6.9 0.0 collective-permute-done.5
  6.9 0.1 collective-permute-start
  7.0 0.2 %collective-permute-done.4 = f32[2,1152]{1,0:T(2,128)S(1)} collective-permute-done((f32[2,1152]{1,0:T(2,128)S(1)}, f32[2,1152]{1,0:T(2,128)S(1)}, u32[]{:S(2)}, u32[]{:S(2)}) %collective-permute-start.4) | collective-permute-done | bytes 9248 | tf_op jit(solution)/shard_map/ppermute | solution.py:396
  7.2 0.0 collective-permute-done.3
  7.2 3.7 %collective-permute-start.7 = (f32[8,1152]{1,0:T(8,128)S(1)}, f32[8,1152]{1,0:T(8,128)S(1)}, u32[]{:S(2)}, u32[]{:S(2)}) collective-permute-start(f32[8,1152]{1,0:T(8,128)S(1)} %pad_maximum_fusion), channel_id=1, source_target_pairs={{3,0},{11,1},{16,2},{24,3},{7,4},{9,5},{21,6},{28,7},{1,8},{8,9},{... | collective-permute-start | bytes 110600 | tf_op jit(solution)/shard_map/ppermute | solution.py:406
  10.9 0.3 %collective-permute-start.6 = (f32[8,1152]{1,0:T(8,128)S(1)}, f32[8,1152]{1,0:T(8,128)S(1)}, u32[]{:S(2)}, u32[]{:S(2)}) collective-permute-start(f32[8,1152]{1,0:T(8,128)S(1)} %pad_maximum_fusion), channel_id=1, source_target_pairs={{1,0},{9,1},{19,2},{26,3},{5,4},{15,5},{23,6},{30,7},{2,8},{11,9},... | collective-permute-start | bytes 110600 | tf_op jit(solution)/shard_map/ppermute | solution.py:406
  11.1 0.0 collective-permute-done.2.refs_3_
  11.2 0.0 collective-permute-done.1.refs_2_
  11.2 0.0 collective-permute-done.refs_1_
  11.2 1.1 %receivers.1 = (f32[8,64,256]{2,1,0:T(8,128)S(1)}, f32[64,128]{1,0:T(8,128)S(1)}) custom-call(f32[16,1152]{1,0:T(8,128)S(1)} %get-tuple-element.16.refs_0_, f32[16,1152]{1,0:T(8,128)S(1)} %collective-permute-done.refs_1_, f32[16,1152]{1,0:T(8,128)S(1)} %collective-permute-done.1.refs_2_, f32[16,1152]{1,0:T(8,128)S(1)} %collective-permute-done.2.refs_3_, ...), custom_call_target="tpu_custom_call" | custom-call | tf_op jit(solution)/shard_map/receivers/pallas_call | solution.py:417
  12.3 0.2 %collective-permute-done.7.refs_1_ = f32[8,1152]{1,0:T(8,128)S(1)} collective-permute-done((f32[8,1152]{1,0:T(8,128)S(1)}, f32[8,1152]{1,0:T(8,128)S(1)}, u32[]{:S(2)}, u32[]{:S(2)}) %collective-permute-start.7) | collective-permute-done | bytes 36896 | tf_op jit(solution)/shard_map/ppermute | solution.py:406
  12.5 0.3 %collective-permute-done.6.refs_0_ = f32[8,1152]{1,0:T(8,128)S(1)} collective-permute-done((f32[8,1152]{1,0:T(8,128)S(1)}, f32[8,1152]{1,0:T(8,128)S(1)}, u32[]{:S(2)}, u32[]{:S(2)}) %collective-permute-start.6) | collective-permute-done | bytes 36896 | tf_op jit(solution)/shard_map/ppermute | solution.py:406
  12.8 2.6 %stacks.1 = f32[4,16,256]{2,1,0:T(8,128)} custom-call(f32[8,64,256]{2,1,0:T(8,128)S(1)} %get-tuple-element.19.spectrum, f32[64,128]{1,0:T(8,128)S(1)} %get-tuple-element.20.mask, f32[8,1152]{1,0:T(8,128)S(1)} %collective-permute-done.6.refs_0_, f32[8,1152]{1,0:T(8,128)S(1)} %collective-permute-done.7.refs_1_, ...), custom_call_target="tpu_custom_call" | custom-call | tf_op jit(solution)/shard_map/stacks/pallas_call | solution.py:435
  (1 shorter events, 0.0 us)
Async XLA Ops:
  1.1 5.8 %collective-permute-start.5 = (f32[2,1152]{1,0:T(2,128)S(1)}, f32[2,1152]{1,0:T(2,128)S(1)}, u32[]{:S(2)}, u32[]{:S(2)}) collective-permute-start(f32[2,1152]{1,0:T(2,128)S(1)} %get-tuple-element.22), channel_id=1, source_target_pairs={{0,5},{1,4},{2,7},{3,6},{4,1},{5,0},{6,3},{7,2},{8,13},{9,12},{10,... | collective-permute-start | bytes 27656 | tf_op jit(solution)/shard_map/ppermute | solution.py:396
  3.5 3.7 %collective-permute-start.4 = (f32[2,1152]{1,0:T(2,128)S(1)}, f32[2,1152]{1,0:T(2,128)S(1)}, u32[]{:S(2)}, u32[]{:S(2)}) collective-permute-start(f32[2,1152]{1,0:T(2,128)S(1)} %get-tuple-element.22), channel_id=1, source_target_pairs={{0,4},{1,5},{2,6},{3,7},{4,0},{5,1},{6,2},{7,3},{8,12},{9,13},{10,... | collective-permute-start | bytes 27656 | tf_op jit(solution)/shard_map/ppermute | solution.py:396
  4.2 3.0 %collective-permute-start.3 = (f32[2,1152]{1,0:T(2,128)S(1)}, f32[2,1152]{1,0:T(2,128)S(1)}, u32[]{:S(2)}, u32[]{:S(2)}) collective-permute-start(f32[2,1152]{1,0:T(2,128)S(1)} %get-tuple-element.22), channel_id=1, source_target_pairs={{0,1},{1,0},{2,3},{3,2},{4,5},{5,4},{6,7},{7,6},{8,9},{9,8},{10,11... | collective-permute-start | bytes 27656 | tf_op jit(solution)/shard_map/ppermute | solution.py:396
  4.2 7.0 %collective-permute-start.2 = (f32[16,1152]{1,0:T(8,128)S(1)}, f32[16,1152]{1,0:T(8,128)S(1)}, u32[]{:S(2)}, u32[]{:S(2)}) collective-permute-start(f32[16,1152]{1,0:T(8,128)S(1)} %get-tuple-element.16.refs_0_), channel_id=1, source_target_pairs={{0,3},{1,2},{2,1},{3,0},{4,7},{5,6},{6,5},{7,4},{8,11},{9,10},{10,... | collective-permute-start | bytes 221192 | tf_op jit(solution)/shard_map/ppermute | solution.py:350
  5.8 5.4 %collective-permute-start.1 = (f32[16,1152]{1,0:T(8,128)S(1)}, f32[16,1152]{1,0:T(8,128)S(1)}, u32[]{:S(2)}, u32[]{:S(2)}) collective-permute-start(f32[16,1152]{1,0:T(8,128)S(1)} %get-tuple-element.16.refs_0_), channel_id=1, source_target_pairs={{0,2},{1,3},{2,0},{3,1},{4,6},{5,7},{6,4},{7,5},{8,10},{9,11},{10,... | collective-permute-start | bytes 221192 | tf_op jit(solution)/shard_map/ppermute | solution.py:350
  6.9 4.3 %collective-permute-start = (f32[16,1152]{1,0:T(8,128)S(1)}, f32[16,1152]{1,0:T(8,128)S(1)}, u32[]{:S(2)}, u32[]{:S(2)}) collective-permute-start(f32[16,1152]{1,0:T(8,128)S(1)} %get-tuple-element.16.refs_0_), channel_id=1, source_target_pairs={{0,1},{1,0},{2,3},{3,2},{4,5},{5,4},{6,7},{7,6},{8,9},{9,8},{10,11... | collective-permute-start | bytes 221192 | tf_op jit(solution)/shard_map/ppermute | solution.py:350
  7.2 5.3 %collective-permute-start.7 = (f32[8,1152]{1,0:T(8,128)S(1)}, f32[8,1152]{1,0:T(8,128)S(1)}, u32[]{:S(2)}, u32[]{:S(2)}) collective-permute-start(f32[8,1152]{1,0:T(8,128)S(1)} %pad_maximum_fusion), channel_id=1, source_target_pairs={{3,0},{11,1},{16,2},{24,3},{7,4},{9,5},{21,6},{28,7},{1,8},{8,9},{... | collective-permute-start | bytes 110600 | tf_op jit(solution)/shard_map/ppermute | solution.py:406
  10.9 2.0 %collective-permute-start.6 = (f32[8,1152]{1,0:T(8,128)S(1)}, f32[8,1152]{1,0:T(8,128)S(1)}, u32[]{:S(2)}, u32[]{:S(2)}) collective-permute-start(f32[8,1152]{1,0:T(8,128)S(1)} %pad_maximum_fusion), channel_id=1, source_target_pairs={{1,0},{9,1},{19,2},{26,3},{5,4},{15,5},{23,6},{30,7},{2,8},{11,9},... | collective-permute-start | bytes 110600 | tf_op jit(solution)/shard_map/ppermute | solution.py:406

commit v8 on v5

--- a/solution.py
+++ b/solution.py
@@ -202,8 +202,8 @@
         pltpu.make_async_copy(constant, small, sems.at[3]),
         pltpu.make_async_copy(step_constant, step_table, sems.at[4]),
     ]
-    for copy in copies:
-        copy.start()
+    for i in (2, 0, 1, 3, 4):
+        copies[i].start()
     copies[1].wait()
     square = (rows, rows)
     here = lax.broadcasted_iota(jnp.int32, square, 0) == lax.broadcasted_iota(jnp.int32, square, 1)
@@ -259,13 +259,13 @@
     count = segs * rows
 
     spectra(xs, count, rows, small, step_table, lhs, z)
-    for at in range(0, count, 8):
+    for at in range(0, count, 16):
 
         def put(p, x, y):
-            out[p, at : at + 8, :LANES] = x
-            out[p, at : at + 8, LANES:] = y
-
-        whiten(z, count, at, 8, small, put)
+            out[p, at : at + 16, :LANES] = x
+            out[p, at : at + 16, LANES:] = y
+
+        whiten(z, count, at, 16, small, put)
 
 
 def stack_kernel(segs, hops, spectrum, mask, *refs):

time: 15.7 us -> 15.7 us (level)
  no operation moved by 1% of the time
where the time goes in v8:
time: 15.7 us; the launch traced here: 15.5 us
  starting transfers between devices  9.23 us (59%)
  Pallas kernels  5.36 us (34%)
  waiting for transfers between devices  0.79 us (5%)
    ppermute x2, starting transfers between devices, local(): pay.append(lax.ppermute(picked, ('recv', 'tm'), route))  3.94 us
    ppermute x3, starting transfers between devices, local(): pieces.append(lax.ppermute(piece[0], ('recv', 'tm'), route))  3.12 us
    pallas_call x1, Pallas kernels, local(): pl.pallas_call(functools.partial(stack_kernel, segs, hops), out_shape=jax...  2.6 us
    ppermute x3, starting transfers between devices, other(): return lax.ppermute(value, 'tm', [(i, i ^ k) for i in range(segs)])  2.17 us
    pallas_call x1, Pallas kernels, local(): pl.pallas_call(functools.partial(receiver_kernel, segs), out_shape=(jax.S...  1.11 us
    pallas_call x1, Pallas kernels, local(): pl.pallas_call(functools.partial(join_kernel, per_group), out_shape=(jax....  1.06 us
    pallas_call x1, Pallas kernels, local(): pl.pallas_call(lag_kernel, out_shape=jax.ShapeDtypeStruct((2, RADIX * LAN...  0.58 us
    ppermute x2, waiting for transfers between devices, local(): pay.append(lax.ppermute(picked, ('recv', 'tm'), route))  0.57 us
  transfers between devices with their start and end apart: 8, of which 3 were waited for; matrix products, arithmetic and copies ran while one was open for 0% of the time, Pallas kernels for 11%

profile of v8, /device:TPU:0, one launch (start us, length us, event | category | flops | bytes accessed | tf_op | source)
XLA Modules:
  0.0 15.5 jit_solution(10260755073557193670)
XLA Ops:
  0.0 1.1 %join.1 = (f32[16,1152]{1,0:T(8,128)S(1)}, f32[248,128]{1,0:T(8,128)S(1)}, bf16[256,256]{1,0:T(8,128)(2,1)S(1)}, f32[2,1152]{1,0:T(2,128)S(1)}) custom-call(f32[16,1024]{1,0:T(8,128)} %record.1, s32[1,16]{1,0:T(1,128)} %bitcast.1, s32[16]{0:T(128)} %src.1, f32[248,128]{1,0:T(8,128)} %constant.5.clone, bf16[256,256]{1,0:T(8,128)(2,1)} %constant.6.clone.step_constant), custom_call_target="tpu_custom_call" | custom-call | tf_op jit(solution)/shard_map/join/pallas_call | solution.py:363
  1.1 2.4 %collective-permute-start.5 = (f32[2,1152]{1,0:T(2,128)S(1)}, f32[2,1152]{1,0:T(2,128)S(1)}, u32[]{:S(2)}, u32[]{:S(2)}) collective-permute-start(f32[2,1152]{1,0:T(2,128)S(1)} %get-tuple-element.22), channel_id=1, source_target_pairs={{0,5},{1,4},{2,7},{3,6},{4,1},{5,0},{6,3},{7,2},{8,13},{9,12},{10,... | collective-permute-start | bytes 27656 | tf_op jit(solution)/shard_map/ppermute | solution.py:395
  3.5 0.6 %collective-permute-start.4 = (f32[2,1152]{1,0:T(2,128)S(1)}, f32[2,1152]{1,0:T(2,128)S(1)}, u32[]{:S(2)}, u32[]{:S(2)}) collective-permute-start(f32[2,1152]{1,0:T(2,128)S(1)} %get-tuple-element.22), channel_id=1, source_target_pairs={{0,4},{1,5},{2,6},{3,7},{4,0},{5,1},{6,2},{7,3},{8,12},{9,13},{10,... | collective-permute-start | bytes 27656 | tf_op jit(solution)/shard_map/ppermute | solution.py:395
  4.2 0.0 collective-permute-start.3
  4.2 1.6 %collective-permute-start.2 = (f32[16,1152]{1,0:T(8,128)S(1)}, f32[16,1152]{1,0:T(8,128)S(1)}, u32[]{:S(2)}, u32[]{:S(2)}) collective-permute-start(f32[16,1152]{1,0:T(8,128)S(1)} %get-tuple-element.16.refs_0_), channel_id=1, source_target_pairs={{0,3},{1,2},{2,1},{3,0},{4,7},{5,6},{6,5},{7,4},{8,11},{9,10},{10,... | collective-permute-start | bytes 221192 | tf_op jit(solution)/shard_map/ppermute | solution.py:349
  5.8 0.5 %collective-permute-start.1 = (f32[16,1152]{1,0:T(8,128)S(1)}, f32[16,1152]{1,0:T(8,128)S(1)}, u32[]{:S(2)}, u32[]{:S(2)}) collective-permute-start(f32[16,1152]{1,0:T(8,128)S(1)} %get-tuple-element.16.refs_0_), channel_id=1, source_target_pairs={{0,2},{1,3},{2,0},{3,1},{4,6},{5,7},{6,4},{7,5},{8,10},{9,11},{10,... | collective-permute-start | bytes 221192 | tf_op jit(solution)/shard_map/ppermute | solution.py:349
  6.3 0.6 %waves.1.refs_4_ = bf16[2,2048,256]{2,1,0:T(8,128)(2,1)S(1)} custom-call(f32[248,128]{1,0:T(8,128)S(1)} %get-tuple-element.17.refs_4_.small.refs_2_), custom_call_target="tpu_custom_call" | custom-call | tf_op jit(solution)/shard_map/waves/pallas_call | solution.py:381
  6.9 0.0 collective-permute-done.5
  6.9 0.1 collective-permute-start
  7.0 0.2 %collective-permute-done.4 = f32[2,1152]{1,0:T(2,128)S(1)} collective-permute-done((f32[2,1152]{1,0:T(2,128)S(1)}, f32[2,1152]{1,0:T(2,128)S(1)}, u32[]{:S(2)}, u32[]{:S(2)}) %collective-permute-start.4) | collective-permute-done | bytes 9248 | tf_op jit(solution)/shard_map/ppermute | solution.py:395
  7.2 0.0 collective-permute-done.3
  7.2 3.7 %collective-permute-start.7 = (f32[8,1152]{1,0:T(8,128)S(1)}, f32[8,1152]{1,0:T(8,128)S(1)}, u32[]{:S(2)}, u32[]{:S(2)}) collective-permute-start(f32[8,1152]{1,0:T(8,128)S(1)} %pad_maximum_fusion), channel_id=1, source_target_pairs={{3,0},{11,1},{16,2},{24,3},{7,4},{9,5},{21,6},{28,7},{1,8},{8,9},{... | collective-permute-start | bytes 110600 | tf_op jit(solution)/shard_map/ppermute | solution.py:405
  10.9 0.3 %collective-permute-start.6 = (f32[8,1152]{1,0:T(8,128)S(1)}, f32[8,1152]{1,0:T(8,128)S(1)}, u32[]{:S(2)}, u32[]{:S(2)}) collective-permute-start(f32[8,1152]{1,0:T(8,128)S(1)} %pad_maximum_fusion), channel_id=1, source_target_pairs={{1,0},{9,1},{19,2},{26,3},{5,4},{15,5},{23,6},{30,7},{2,8},{11,9},... | collective-permute-start | bytes 110600 | tf_op jit(solution)/shard_map/ppermute | solution.py:405
  11.1 0.0 collective-permute-done.2.refs_3_
  11.2 0.0 collective-permute-done.1.refs_2_
  11.2 0.0 collective-permute-done.refs_1_
  11.2 1.1 %receivers.1 = (f32[8,64,256]{2,1,0:T(8,128)S(1)}, f32[64,128]{1,0:T(8,128)S(1)}) custom-call(f32[16,1152]{1,0:T(8,128)S(1)} %get-tuple-element.16.refs_0_, f32[16,1152]{1,0:T(8,128)S(1)} %collective-permute-done.refs_1_, f32[16,1152]{1,0:T(8,128)S(1)} %collective-permute-done.1.refs_2_, f32[16,1152]{1,0:T(8,128)S(1)} %collective-permute-done.2.refs_3_, ...), custom_call_target="tpu_custom_call" | custom-call | tf_op jit(solution)/shard_map/receivers/pallas_call | solution.py:416
  12.3 0.2 %collective-permute-done.7.refs_1_ = f32[8,1152]{1,0:T(8,128)S(1)} collective-permute-done((f32[8,1152]{1,0:T(8,128)S(1)}, f32[8,1152]{1,0:T(8,128)S(1)}, u32[]{:S(2)}, u32[]{:S(2)}) %collective-permute-start.7) | collective-permute-done | bytes 36896 | tf_op jit(solution)/shard_map/ppermute | solution.py:405
  12.5 0.3 %collective-permute-done.6.refs_0_ = f32[8,1152]{1,0:T(8,128)S(1)} collective-permute-done((f32[8,1152]{1,0:T(8,128)S(1)}, f32[8,1152]{1,0:T(8,128)S(1)}, u32[]{:S(2)}, u32[]{:S(2)}) %collective-permute-start.6) | collective-permute-done | bytes 36896 | tf_op jit(solution)/shard_map/ppermute | solution.py:405
  12.9 2.6 %stacks.1 = f32[4,16,256]{2,1,0:T(8,128)} custom-call(f32[8,64,256]{2,1,0:T(8,128)S(1)} %get-tuple-element.19.spectrum, f32[64,128]{1,0:T(8,128)S(1)} %get-tuple-element.20.mask, f32[8,1152]{1,0:T(8,128)S(1)} %collective-permute-done.6.refs_0_, f32[8,1152]{1,0:T(8,128)S(1)} %collective-permute-done.7.refs_1_, ...), custom_call_target="tpu_custom_call" | custom-call | tf_op jit(solution)/shard_map/stacks/pallas_call | solution.py:434
  (1 shorter events, 0.0 us)
Async XLA Ops:
  1.1 5.8 %collective-permute-start.5 = (f32[2,1152]{1,0:T(2,128)S(1)}, f32[2,1152]{1,0:T(2,128)S(1)}, u32[]{:S(2)}, u32[]{:S(2)}) collective-permute-start(f32[2,1152]{1,0:T(2,128)S(1)} %get-tuple-element.22), channel_id=1, source_target_pairs={{0,5},{1,4},{2,7},{3,6},{4,1},{5,0},{6,3},{7,2},{8,13},{9,12},{10,... | collective-permute-start | bytes 27656 | tf_op jit(solution)/shard_map/ppermute | solution.py:395
  3.5 3.7 %collective-permute-start.4 = (f32[2,1152]{1,0:T(2,128)S(1)}, f32[2,1152]{1,0:T(2,128)S(1)}, u32[]{:S(2)}, u32[]{:S(2)}) collective-permute-start(f32[2,1152]{1,0:T(2,128)S(1)} %get-tuple-element.22), channel_id=1, source_target_pairs={{0,4},{1,5},{2,6},{3,7},{4,0},{5,1},{6,2},{7,3},{8,12},{9,13},{10,... | collective-permute-start | bytes 27656 | tf_op jit(solution)/shard_map/ppermute | solution.py:395
  4.2 3.0 %collective-permute-start.3 = (f32[2,1152]{1,0:T(2,128)S(1)}, f32[2,1152]{1,0:T(2,128)S(1)}, u32[]{:S(2)}, u32[]{:S(2)}) collective-permute-start(f32[2,1152]{1,0:T(2,128)S(1)} %get-tuple-element.22), channel_id=1, source_target_pairs={{0,1},{1,0},{2,3},{3,2},{4,5},{5,4},{6,7},{7,6},{8,9},{9,8},{10,11... | collective-permute-start | bytes 27656 | tf_op jit(solution)/shard_map/ppermute | solution.py:395
  4.2 7.0 %collective-permute-start.2 = (f32[16,1152]{1,0:T(8,128)S(1)}, f32[16,1152]{1,0:T(8,128)S(1)}, u32[]{:S(2)}, u32[]{:S(2)}) collective-permute-start(f32[16,1152]{1,0:T(8,128)S(1)} %get-tuple-element.16.refs_0_), channel_id=1, source_target_pairs={{0,3},{1,2},{2,1},{3,0},{4,7},{5,6},{6,5},{7,4},{8,11},{9,10},{10,... | collective-permute-start | bytes 221192 | tf_op jit(solution)/shard_map/ppermute | solution.py:349
  5.8 5.4 %collective-permute-start.1 = (f32[16,1152]{1,0:T(8,128)S(1)}, f32[16,1152]{1,0:T(8,128)S(1)}, u32[]{:S(2)}, u32[]{:S(2)}) collective-permute-start(f32[16,1152]{1,0:T(8,128)S(1)} %get-tuple-element.16.refs_0_), channel_id=1, source_target_pairs={{0,2},{1,3},{2,0},{3,1},{4,6},{5,7},{6,4},{7,5},{8,10},{9,11},{10,... | collective-permute-start | bytes 221192 | tf_op jit(solution)/shard_map/ppermute | solution.py:349
  6.9 4.3 %collective-permute-start = (f32[16,1152]{1,0:T(8,128)S(1)}, f32[16,1152]{1,0:T(8,128)S(1)}, u32[]{:S(2)}, u32[]{:S(2)}) collective-permute-start(f32[16,1152]{1,0:T(8,128)S(1)} %get-tuple-element.16.refs_0_), channel_id=1, source_target_pairs={{0,1},{1,0},{2,3},{3,2},{4,5},{5,4},{6,7},{7,6},{8,9},{9,8},{10,11... | collective-permute-start | bytes 221192 | tf_op jit(solution)/shard_map/ppermute | solution.py:349
  7.2 5.3 %collective-permute-start.7 = (f32[8,1152]{1,0:T(8,128)S(1)}, f32[8,1152]{1,0:T(8,128)S(1)}, u32[]{:S(2)}, u32[]{:S(2)}) collective-permute-start(f32[8,1152]{1,0:T(8,128)S(1)} %pad_maximum_fusion), channel_id=1, source_target_pairs={{3,0},{11,1},{16,2},{24,3},{7,4},{9,5},{21,6},{28,7},{1,8},{8,9},{... | collective-permute-start | bytes 110600 | tf_op jit(solution)/shard_map/ppermute | solution.py:405
  10.9 2.0 %collective-permute-start.6 = (f32[8,1152]{1,0:T(8,128)S(1)}, f32[8,1152]{1,0:T(8,128)S(1)}, u32[]{:S(2)}, u32[]{:S(2)}) collective-permute-start(f32[8,1152]{1,0:T(8,128)S(1)} %pad_maximum_fusion), channel_id=1, source_target_pairs={{1,0},{9,1},{19,2},{26,3},{5,4},{15,5},{23,6},{30,7},{2,8},{11,9},... | collective-permute-start | bytes 110600 | tf_op jit(solution)/shard_map/ppermute | solution.py:405
